TPU v7x, 128 devices: a whole 4x4x4 slice. The times are simulated.
128 devices in a mesh: seq: 8 (over z, y_hi), fsdp: 16 (over y_lo, x, core).
Axes of the slice: x: 4, y: 4 (y_hi: 2, y_lo: 2; y = y_hi * 2 + y_lo), z: 4, core: 2. Of those that a mesh axis runs over, the one named last changes fastest.
Arguments:
- inputs: bfloat16 [16, 1024, 1024], P('fsdp', 'seq'), may hold values from -6 to 6
- doc_starts: int32 [16, 2], P('fsdp'), may hold values from 1 to 1023, as said below
- route: int32 [16, 8, 128], P('fsdp', 'seq'), may hold values from 0 to 127, each once within a row
- norm_gain: bfloat16 [2, 1024], P(None, 'fsdp'), may hold values from 0.5 to 1.5
- norm_bias: bfloat16 [2, 1024], P(None, 'fsdp'), may hold values from -1 to 1
- w_qkv: bfloat16 [1024, 3072], P('fsdp'), may hold values from -0.1875 to 0.1875
- w_out: bfloat16 [1024, 1024], P('fsdp'), may hold values from -0.75 to 0.75
- w_up: bfloat16 [1024, 4096], P('fsdp'), may hold values from -0.1875 to 0.1875
- w_down: bfloat16 [4096, 1024], P('fsdp'), may hold values from -0.09375 to 0.09375
- exp_gain: bfloat16 [16, 2, 1024], P('fsdp'), may hold values from 0.5 to 1.5
- exp_bias: bfloat16 [16, 2, 1024], P('fsdp'), may hold values from -1 to 1
- exp_in: bfloat16 [16, 2, 1024, 4096], P('fsdp', None, None, 'seq'), may hold values from -0.1875 to 0.1875
- exp_out: bfloat16 [16, 2, 4096, 1024], P('fsdp', None, 'seq'), may hold values from -0.09375 to 0.09375
- centroid: bfloat16 [16, 1024], P('fsdp'), may hold values from -0.1875 to 0.1875
- cotangent: bfloat16 [16, 1024, 1024], P('fsdp', 'seq'), may hold values from -6 to 6
Outputs:
- result: bfloat16 [16, 1024, 1024], P('fsdp', 'seq')
- grad_input: float32 [16, 1024, 1024], P('fsdp', 'seq')
- grad_norm_gain: float32 [2, 1024], P(None, 'fsdp')
- grad_norm_bias: float32 [2, 1024], P(None, 'fsdp')
- grad_qkv: float32 [1024, 3072], P('fsdp')
- grad_out: float32 [1024, 1024], P('fsdp')
- grad_up: float32 [1024, 4096], P('fsdp')
- grad_down: float32 [4096, 1024], P('fsdp')
- grad_exp_gain: float32 [16, 2, 1024], P('fsdp')
- grad_exp_bias: float32 [16, 2, 1024], P('fsdp')
- grad_exp_in: float32 [16, 2, 1024, 4096], P('fsdp', None, None, 'seq')
- grad_exp_out: float32 [16, 2, 4096, 1024], P('fsdp', None, 'seq')
- grad_centroid: float32 [16, 1024], P('fsdp')
Inputs may be any that keep to these rules, and one draw needn't show every extreme that they name: `doc_starts`: in each sequence column 0 lies within the first 128 positions and column 1 within the last 128 positions, so the second document runs from the first device of seq to the last. `route`: each device's row is a permutation of its 128 tokens' slots; slot p belongs to expert p // 8, so every device sends each expert exactly 8 tokens.
All inputs are finite; a program needn't handle non-finite values.
Results may differ from a plain program's by a relative error of at most 0.024.
Values may be sent and summed in bfloat16 or wider, within the bound.
A program may use at most 192 MiB of HBM per device.

v0:
```python
import jax
import jax.numpy as jnp
from jax import lax
from jax.sharding import PartitionSpec as P

HEADS = 16


epsilon = 1e-05
masked_score = -1e30


def norm_rows(values, gain, offset):
    average = jnp.mean(values, axis=-1, keepdims=True)
    centered = values - average
    spread = jnp.mean(centered * centered, axis=-1, keepdims=True)
    return centered * lax.rsqrt(spread + epsilon) * gain + offset


def labels_of(position, starts):
    return (position[None, :] >= starts[:, 0:1]).astype(jnp.int32) + (
        position[None, :] >= starts[:, 1:2]
    ).astype(jnp.int32)


def row_product(left, right, pattern):
    return jnp.einsum(pattern, left, right, preferred_element_type=jnp.float32)


def gelu_back(pre_act, grad_acted):
    unused, slope_pull = jax.vjp(jax.nn.gelu, pre_act)
    return slope_pull(grad_acted)[0]


def on_device(
    inputs,
    doc_starts,
    route,
    norm_gain,
    norm_bias,
    w_qkv,
    w_out,
    w_up,
    w_down,
    exp_gain,
    exp_bias,
    exp_in,
    exp_out,
    centroid,
    cotangent,
):
    seq_count, local_len, model_width = inputs.shape
    tok_rows = seq_count * local_len
    head_count = HEADS
    head_width = model_width // head_count
    score_scale = head_width ** (-0.5)
    gains, offsets, qkv_weight, out_weight, up_weight, down_weight = (
        lax.all_gather(norm_gain, "fsdp", axis=1, tiled=True),
        lax.all_gather(norm_bias, "fsdp", axis=1, tiled=True),
        lax.all_gather(w_qkv, "fsdp", axis=0, tiled=True),
        lax.all_gather(w_out, "fsdp", axis=0, tiled=True),
        lax.all_gather(w_up, "fsdp", axis=0, tiled=True),
        lax.all_gather(w_down, "fsdp", axis=0, tiled=True),
    )
    rows_in = inputs.reshape(tok_rows, model_width).astype(jnp.float32)
    normed_one = norm_rows(
        rows_in, gains[0].astype(jnp.float32), offsets[0].astype(jnp.float32)
    ).astype(jnp.bfloat16)
    packed = jnp.dot(normed_one, qkv_weight, preferred_element_type=jnp.float32).astype(
        jnp.bfloat16
    )
    packed = packed.reshape(seq_count, local_len, 3, model_width)
    queries = packed[:, :, 0]
    keys_all, values_all = (
        lax.all_gather(packed[:, :, 1], "seq", axis=1, tiled=True),
        lax.all_gather(packed[:, :, 2], "seq", axis=1, tiled=True),
    )
    key_len = keys_all.shape[1]
    query_pos = lax.axis_index("seq") * local_len + jnp.arange(local_len, dtype=jnp.int32)
    key_pos = jnp.arange(key_len, dtype=jnp.int32)
    allowed = (key_pos[None, None, :] <= query_pos[None, :, None]) & (
        labels_of(key_pos, doc_starts)[:, None, :] == labels_of(query_pos, doc_starts)[:, :, None]
    )
    allowed = allowed[:, None]
    query_heads = queries.reshape(seq_count, local_len, head_count, head_width)
    key_heads = keys_all.reshape(seq_count, key_len, head_count, head_width)
    value_heads = values_all.reshape(seq_count, key_len, head_count, head_width)
    scores = (
        jnp.einsum("sqhd,skhd->shqk", query_heads, key_heads, preferred_element_type=jnp.float32)
        * score_scale
    )
    scores = jnp.where(allowed, scores, masked_score)
    row_max = jnp.max(scores, axis=-1, keepdims=True)
    weights = jnp.exp(scores - row_max)
    row_sum = jnp.sum(weights, axis=-1, keepdims=True)
    log_total = row_max + jnp.log(row_sum)
    probs_low = (weights / row_sum).astype(jnp.bfloat16)
    mixed = jnp.einsum(
        "shqk,skhd->sqhd", probs_low, value_heads, preferred_element_type=jnp.float32
    )
    mixed = mixed.reshape(tok_rows, model_width).astype(jnp.bfloat16)
    after = rows_in + jnp.dot(mixed, out_weight, preferred_element_type=jnp.float32)
    normed_two = norm_rows(
        after, gains[1].astype(jnp.float32), offsets[1].astype(jnp.float32)
    ).astype(jnp.bfloat16)
    pre_dense = jnp.dot(normed_two, up_weight, preferred_element_type=jnp.float32)
    acted = jax.nn.gelu(pre_dense).astype(jnp.bfloat16)
    hidden = (after + jnp.dot(acted, down_weight, preferred_element_type=jnp.float32)).astype(
        jnp.bfloat16
    )
    expert_count = lax.axis_size("fsdp")
    slot_of = route.reshape(tok_rows)
    placing = (jnp.arange(tok_rows, dtype=jnp.int32)[:, None] == slot_of[None, :]).astype(
        jnp.bfloat16
    )
    sending = jnp.dot(placing, hidden, preferred_element_type=jnp.float32).astype(jnp.bfloat16)
    arrived = lax.all_to_all(
        sending.reshape(expert_count, tok_rows // expert_count, model_width),
        "fsdp",
        split_axis=0,
        concat_axis=0,
        tiled=True,
    )
    arrived = arrived.reshape(tok_rows, model_width)
    arrived_rows = arrived.astype(jnp.float32)
    stream = arrived_rows
    saved_rows = []
    for sublayer in range(2):
        expert_normed = norm_rows(
            stream,
            exp_gain[0, sublayer].astype(jnp.float32),
            exp_bias[0, sublayer].astype(jnp.float32),
        ).astype(jnp.bfloat16)
        every_row = lax.all_gather(expert_normed, "seq", axis=0, tiled=True)
        expert_pre = jnp.dot(every_row, exp_in[0, sublayer], preferred_element_type=jnp.float32)
        expert_acted = jax.nn.gelu(expert_pre).astype(jnp.bfloat16)
        branch = lax.psum_scatter(
            row_product(expert_acted, exp_out[0, sublayer], "rf,fd->rd").astype(jnp.bfloat16),
            "seq",
            scatter_dimension=0,
            tiled=True,
        ).astype(jnp.float32)
        saved_rows.append((stream, every_row, expert_pre, expert_acted))
        stream = stream + branch
    gating = jax.nn.sigmoid(jnp.dot(arrived, centroid[0], preferred_element_type=jnp.float32))[
        :, None
    ]
    mixed_out = (arrived_rows + gating * (stream - arrived_rows)).astype(jnp.bfloat16)
    returned = lax.all_to_all(
        mixed_out.reshape(expert_count, tok_rows // expert_count, model_width),
        "fsdp",
        split_axis=0,
        concat_axis=0,
        tiled=True,
    )
    returned = returned.reshape(tok_rows, model_width)
    result = returned[slot_of].reshape(seq_count, local_len, model_width)
    grad_result = cotangent.reshape(tok_rows, model_width)
    grad_slots = jnp.dot(placing, grad_result, preferred_element_type=jnp.float32).astype(
        jnp.bfloat16
    )
    grad_arrived = lax.all_to_all(
        grad_slots.reshape(expert_count, tok_rows // expert_count, model_width),
        "fsdp",
        split_axis=0,
        concat_axis=0,
        tiled=True,
    )
    grad_arrived = grad_arrived.reshape(tok_rows, model_width).astype(jnp.float32)
    grad_gating = jnp.sum(grad_arrived * (stream - arrived_rows), axis=1, keepdims=True)
    grad_logit = gating * (1.0 - gating) * grad_gating
    grad_centre = jnp.sum(grad_logit * arrived_rows, axis=0)
    grad_stream = gating * grad_arrived
    gain_grads = [None, None]
    bias_grads = [None, None]
    in_grads = [None, None]
    out_grads = [None, None]
    for sublayer in (1, 0):
        before, every_row, expert_pre, expert_acted = saved_rows[sublayer]
        grad_every = lax.all_gather(grad_stream.astype(jnp.bfloat16), "seq", axis=0, tiled=True)
        out_grads[sublayer] = jnp.einsum(
            "rf,rd->fd", expert_acted, grad_every, preferred_element_type=jnp.float32
        )
        grad_act = jnp.einsum(
            "rd,fd->rf", grad_every, exp_out[0, sublayer], preferred_element_type=jnp.float32
        )
        grad_pre = gelu_back(expert_pre, grad_act).astype(jnp.bfloat16)
        in_grads[sublayer] = jnp.einsum(
            "rd,rf->df", every_row, grad_pre, preferred_element_type=jnp.float32
        )
        grad_normed = lax.psum_scatter(
            row_product(grad_pre, exp_in[0, sublayer], "rf,df->rd").astype(jnp.bfloat16),
            "seq",
            scatter_dimension=0,
            tiled=True,
        ).astype(jnp.float32)
        unused, norm_pull = jax.vjp(
            norm_rows,
            before,
            exp_gain[0, sublayer].astype(jnp.float32),
            exp_bias[0, sublayer].astype(jnp.float32),
        )
        grad_before, gain_grads[sublayer], bias_grads[sublayer] = norm_pull(grad_normed)
        grad_stream = grad_stream + grad_before
    grad_arrived_in = (
        grad_stream + (1.0 - gating) * grad_arrived + grad_logit * centroid[0].astype(jnp.float32)
    ).astype(jnp.bfloat16)
    sent_back = lax.all_to_all(
        grad_arrived_in.reshape(expert_count, tok_rows // expert_count, model_width),
        "fsdp",
        split_axis=0,
        concat_axis=0,
        tiled=True,
    )
    grad_hidden = sent_back.reshape(tok_rows, model_width)[slot_of]
    gains, offsets, qkv_weight, out_weight, up_weight, down_weight = (
        lax.all_gather(norm_gain, "fsdp", axis=1, tiled=True),
        lax.all_gather(norm_bias, "fsdp", axis=1, tiled=True),
        lax.all_gather(w_qkv, "fsdp", axis=0, tiled=True),
        lax.all_gather(w_out, "fsdp", axis=0, tiled=True),
        lax.all_gather(w_up, "fsdp", axis=0, tiled=True),
        lax.all_gather(w_down, "fsdp", axis=0, tiled=True),
    )
    grad_down = jnp.einsum("rf,rd->fd", acted, grad_hidden, preferred_element_type=jnp.float32)
    grad_acted = jnp.einsum(
        "rd,fd->rf", grad_hidden, down_weight, preferred_element_type=jnp.float32
    )
    grad_pre_dense = gelu_back(pre_dense, grad_acted).astype(jnp.bfloat16)
    grad_up = jnp.einsum(
        "rd,rf->df", normed_two, grad_pre_dense, preferred_element_type=jnp.float32
    )
    grad_normed_two = jnp.einsum(
        "rf,df->rd", grad_pre_dense, up_weight, preferred_element_type=jnp.float32
    )
    unused, norm_pull = jax.vjp(
        norm_rows, after, gains[1].astype(jnp.float32), offsets[1].astype(jnp.float32)
    )
    grad_after_norm, gain_two_grad, bias_two_grad = norm_pull(grad_normed_two)
    grad_after = grad_hidden.astype(jnp.float32) + grad_after_norm
    grad_attn = grad_after.astype(jnp.bfloat16)
    grad_out = jnp.einsum("rd,re->de", mixed, grad_attn, preferred_element_type=jnp.float32)
    grad_mixed = jnp.einsum(
        "re,de->rd", grad_attn, out_weight, preferred_element_type=jnp.float32
    ).astype(jnp.bfloat16)
    grad_mixed = grad_mixed.reshape(seq_count, local_len, head_count, head_width)
    scores = (
        jnp.einsum("sqhd,skhd->shqk", query_heads, key_heads, preferred_element_type=jnp.float32)
        * score_scale
    )
    scores = jnp.where(allowed, scores, masked_score)
    probs = jnp.exp(scores - log_total)
    grad_probs = jnp.einsum(
        "sqhd,skhd->shqk", grad_mixed, value_heads, preferred_element_type=jnp.float32
    )
    grad_values = jnp.einsum(
        "shqk,sqhd->skhd",
        probs.astype(jnp.bfloat16),
        grad_mixed,
        preferred_element_type=jnp.float32,
    )
    row_dot = jnp.sum(grad_probs * probs, axis=-1, keepdims=True)
    grad_scores = (probs * (grad_probs - row_dot)).astype(jnp.bfloat16)
    grad_queries = (
        jnp.einsum("shqk,skhd->sqhd", grad_scores, key_heads, preferred_element_type=jnp.float32)
        * score_scale
    )
    grad_keys = (
        jnp.einsum("shqk,sqhd->skhd", grad_scores, query_heads, preferred_element_type=jnp.float32)
        * score_scale
    )
    grad_keys, grad_values = (
        lax.psum_scatter(
            grad_keys.reshape(seq_count, key_len, model_width).astype(jnp.bfloat16),
            "seq",
            scatter_dimension=1,
            tiled=True,
        ).astype(jnp.float32),
        lax.psum_scatter(
            grad_values.reshape(seq_count, key_len, model_width).astype(jnp.bfloat16),
            "seq",
            scatter_dimension=1,
            tiled=True,
        ).astype(jnp.float32),
    )
    grad_queries = grad_queries.reshape(seq_count, local_len, model_width).astype(jnp.bfloat16)
    grad_packed = jnp.stack(
        [grad_queries, grad_keys.astype(jnp.bfloat16), grad_values.astype(jnp.bfloat16)], axis=2
    )
    grad_packed = grad_packed.reshape(tok_rows, 3 * model_width)
    grad_qkv = jnp.einsum("rd,re->de", normed_one, grad_packed, preferred_element_type=jnp.float32)
    grad_normed_one = jnp.einsum(
        "re,de->rd", grad_packed, qkv_weight, preferred_element_type=jnp.float32
    )
    unused, norm_pull = jax.vjp(
        norm_rows, rows_in, gains[0].astype(jnp.float32), offsets[0].astype(jnp.float32)
    )
    grad_rows_in, gain_one_grad, bias_one_grad = norm_pull(grad_normed_one)
    grad_input = (grad_after + grad_rows_in).reshape(seq_count, local_len, model_width)
    grad_exp_in = jnp.stack(in_grads)[None]
    grad_exp_out = jnp.stack(out_grads)[None]
    dense_terms = (
        jnp.stack([gain_one_grad, gain_two_grad]),
        jnp.stack([bias_one_grad, bias_two_grad]),
        grad_qkv,
        grad_out,
        grad_up,
        grad_down,
    )
    shard_gain, shard_bias, shard_qkv, shard_out, shard_up, shard_down = (
        lax.psum_scatter(
            dense_terms[0].astype(jnp.bfloat16), "fsdp", scatter_dimension=1, tiled=True
        ).astype(jnp.float32),
        lax.psum_scatter(
            dense_terms[1].astype(jnp.bfloat16), "fsdp", scatter_dimension=1, tiled=True
        ).astype(jnp.float32),
        lax.psum_scatter(
            dense_terms[2].astype(jnp.bfloat16), "fsdp", scatter_dimension=0, tiled=True
        ).astype(jnp.float32),
        lax.psum_scatter(
            dense_terms[3].astype(jnp.bfloat16), "fsdp", scatter_dimension=0, tiled=True
        ).astype(jnp.float32),
        lax.psum_scatter(
            dense_terms[4].astype(jnp.bfloat16), "fsdp", scatter_dimension=0, tiled=True
        ).astype(jnp.float32),
        lax.psum_scatter(
            dense_terms[5].astype(jnp.bfloat16), "fsdp", scatter_dimension=0, tiled=True
        ).astype(jnp.float32),
    )
    summed = (
        lax.psum(shard_gain.astype(jnp.bfloat16), "seq").astype(jnp.float32),
        lax.psum(shard_bias.astype(jnp.bfloat16), "seq").astype(jnp.float32),
        lax.psum(shard_qkv.astype(jnp.bfloat16), "seq").astype(jnp.float32),
        lax.psum(shard_out.astype(jnp.bfloat16), "seq").astype(jnp.float32),
        lax.psum(shard_up.astype(jnp.bfloat16), "seq").astype(jnp.float32),
        lax.psum(shard_down.astype(jnp.bfloat16), "seq").astype(jnp.float32),
        lax.psum(jnp.stack(gain_grads)[None].astype(jnp.bfloat16), "seq").astype(jnp.float32),
        lax.psum(jnp.stack(bias_grads)[None].astype(jnp.bfloat16), "seq").astype(jnp.float32),
        lax.psum(grad_centre[None].astype(jnp.bfloat16), "seq").astype(jnp.float32),
    )
    return (
        result,
        grad_input,
        summed[0],
        summed[1],
        summed[2],
        summed[3],
        summed[4],
        summed[5],
        summed[6],
        summed[7],
        grad_exp_in,
        grad_exp_out,
        summed[8],
    )


def solution(mesh):
    in_specs = (
        P("fsdp", "seq", None),
        P("fsdp", None),
        P("fsdp", "seq", None),
        P(None, "fsdp"),
        P(None, "fsdp"),
        P("fsdp", None),
        P("fsdp", None),
        P("fsdp", None),
        P("fsdp", None),
        P("fsdp", None, None),
        P("fsdp", None, None),
        P("fsdp", None, None, "seq"),
        P("fsdp", None, "seq", None),
        P("fsdp", None),
        P("fsdp", "seq", None),
    )
    out_specs = (
        P("fsdp", "seq", None),
        P("fsdp", "seq", None),
        P(None, "fsdp"),
        P(None, "fsdp"),
        P("fsdp", None),
        P("fsdp", None),
        P("fsdp", None),
        P("fsdp", None),
        P("fsdp", None, None),
        P("fsdp", None, None),
        P("fsdp", None, None, "seq"),
        P("fsdp", None, "seq", None),
        P("fsdp", None),
    )
    return jax.shard_map(
        on_device, mesh=mesh, in_specs=in_specs, out_specs=out_specs, check_vma=False
    )
```

profile of v0, /device:TPU:4, one launch (start us, length us, event | category | flops | bytes accessed | tf_op | source)
XLA Modules:
  0.0 1607.5 jit_solution(14741375839222765928)
XLA Ops:
  8.0 16.7 %all-gather.2 = bf16[16,64,2]{1,2,0:T(2,128)(2,1)S(1)} all-gather(bf16[1,64,2]{1,2,0:T(2,128)(2,1)} %bitcast.298), channel_id=1, replica_groups=mesh['seq'=8,'fsdp'=16] {'fsdp'}, dimensions={0}, use_global_device_ids=true | all-gather | bytes 4352 | tf_op jit(solution)/shard_map/all_gather | solution.py:58
  24.8 16.3 %all-gather.3 = bf16[16,64,2]{1,2,0:T(2,128)(2,1)S(1)} all-gather(bf16[1,64,2]{1,2,0:T(2,128)(2,1)} %bitcast.299), channel_id=1, replica_groups=mesh['seq'=8,'fsdp'=16] {'fsdp'}, dimensions={0}, use_global_device_ids=true | all-gather | bytes 4352 | tf_op jit(solution)/shard_map/all_gather | solution.py:59
  43.4 10.6 all-gather.15.cloned.1.call-done
  65.1 50.1 %all-gather.33.cloned.1.call-done = bf16[1,1024,1,1024]{1,3,2,0:T(8,128)(2,1)} async-done(((bf16[1,128,1,1024]{1,3,2,0:T(8,128)(2,1)}), bf16[1,1024,1,1024]{1,3,2,0:T(8,128)(2,1)}) %all-gather.33.cloned.1.call-update) | async-done | bytes 2097168 | tf_op jit(solution)/shard_map/all_gather | solution.py:75
  123.6 46.8 %all-gather.31.cloned.1.call-done = bf16[1,1024,1,1024]{1,3,2,0:T(8,128)(2,1)} async-done(((bf16[1,128,1,1024]{1,3,2,0:T(8,128)(2,1)}), bf16[1,1024,1,1024]{1,3,2,0:T(8,128)(2,1)}) %all-gather.31.cloned.1.call-update) | async-done | bytes 2097168 | tf_op jit(solution)/shard_map/all_gather | solution.py:76
  176.3 26.6 %all-gather.17.cloned.1.call-done = bf16[1024,1024]{1,0:T(8,128)(2,1)} async-done(((bf16[64,1024]{1,0:T(8,128)(2,1)}), bf16[1024,1024]{1,0:T(8,128)(2,1)}) %all-gather.17.cloned.1.call-update) | async-done | bytes 2097168 | tf_op jit(solution)/shard_map/all_gather | solution.py:61
  205.2 51.9 %all-gather.19.cloned.1.call-done = bf16[1024,4096]{1,0:T(8,128)(2,1)} async-done(((bf16[64,4096]{1,0:T(8,128)(2,1)}), bf16[1024,4096]{1,0:T(8,128)(2,1)}) %all-gather.19.cloned.1.call-update) | async-done | bytes 8388624 | tf_op jit(solution)/shard_map/all_gather | solution.py:62
  261.8 49.8 %all-gather.21.cloned.1.call-done = bf16[4096,1024]{1,0:T(8,128)(2,1)} async-done(((bf16[256,1024]{1,0:T(8,128)(2,1)}), bf16[4096,1024]{1,0:T(8,128)(2,1)}) %all-gather.21.cloned.1.call-update) | async-done | bytes 8388624 | tf_op jit(solution)/shard_map/all_gather | solution.py:63
  330.2 55.2 %all-gather.23.cloned.1.call-done = bf16[1024,1024]{1,0:T(8,128)(2,1)} async-done(((bf16[128,1024]{1,0:T(8,128)(2,1)}), bf16[1024,1024]{1,0:T(8,128)(2,1)}) %all-gather.23.cloned.1.call-update) | async-done | bytes 2097168 | tf_op jit(solution)/shard_map/all_gather | solution.py:134
  392.9 72.9 %reduce-scatter.21.cloned.1.call-done = bf16[128,1024]{1,0:T(8,128)(2,1)} async-done(((bf16[1024,1024]{1,0:T(8,128)(2,1)}), bf16[128,1024]{1,0:T(8,128)(2,1)}) %reduce-scatter.21.cloned.1.call-update) | async-done | bytes 262160 | tf_op jit(solution)/shard_map/reduce_scatter | solution.py:137
  481.6 41.2 %all-gather.25.cloned.1.call-done = bf16[1024,1024]{1,0:T(8,128)(2,1)} async-done(((bf16[128,1024]{1,0:T(8,128)(2,1)}), bf16[1024,1024]{1,0:T(8,128)(2,1)}) %all-gather.25.cloned.1.call-update) | async-done | bytes 2097168 | tf_op jit(solution)/shard_map/all_gather | solution.py:134
  530.3 47.2 %all-gather.27.cloned.1.call-done = bf16[1024,1024]{1,0:T(8,128)(2,1)} async-done(((bf16[128,1024]{1,0:T(8,128)(2,1)}), bf16[1024,1024]{1,0:T(8,128)(2,1)}) %all-gather.27.cloned.1.call-update) | async-done | bytes 2097168 | tf_op jit(solution)/shard_map/all_gather | solution.py:180
  586.2 68.5 %reduce-scatter.23.cloned.1.call-done = bf16[128,1024]{1,0:T(8,128)(2,1)} async-done(((bf16[1024,1024]{1,0:T(8,128)(2,1)}), bf16[128,1024]{1,0:T(8,128)(2,1)}) %reduce-scatter.23.cloned.1.call-update) | async-done | bytes 262160 | tf_op jit(solution)/shard_map/reduce_scatter | solution.py:137
  654.7 78.1 %reduce-scatter.25.cloned.1.call-done = bf16[128,1024]{1,0:T(8,128)(2,1)} async-done(((bf16[1024,1024]{1,0:T(8,128)(2,1)}), bf16[128,1024]{1,0:T(8,128)(2,1)}) %reduce-scatter.25.cloned.1.call-update) | async-done | bytes 262160 | tf_op jit(solution)/shard_map/reduce_scatter | solution.py:191
  738.1 52.8 %all-gather.29.cloned.1.call-done = bf16[1024,1024]{1,0:T(8,128)(2,1)} async-done(((bf16[128,1024]{1,0:T(8,128)(2,1)}), bf16[1024,1024]{1,0:T(8,128)(2,1)}) %all-gather.29.cloned.1.call-update) | async-done | bytes 2097168 | tf_op jit(solution)/shard_map/all_gather | solution.py:180
  799.7 73.0 %reduce-scatter.27.cloned.1.call-done = bf16[128,1024]{1,0:T(8,128)(2,1)} async-done(((bf16[1024,1024]{1,0:T(8,128)(2,1)}), bf16[128,1024]{1,0:T(8,128)(2,1)}) %reduce-scatter.27.cloned.1.call-update) | async-done | bytes 262160 | tf_op jit(solution)/shard_map/reduce_scatter | solution.py:191
  888.8 7.0 fusion.12
  895.8 6.8 multiply_reduce_fusion.1
  907.9 6.4 fusion.27
  914.3 10.7 copy.43
  929.9 6.5 multiply_reduce_fusion
  943.7 10.8 copy.41
  967.1 37.7 %reduce-scatter.39.cloned.1.call-done = bf16[128,1024]{1,0:T(8,128)(2,1)} async-done(((bf16[1024,1024]{1,0:T(8,128)(2,1)}), bf16[128,1024]{1,0:T(8,128)(2,1)}) %reduce-scatter.39.cloned.1.call-update) | async-done | bytes 262160
  1008.7 73.6 %reduce-scatter.37.cloned.1.call-done = bf16[128,1024]{1,0:T(8,128)(2,1)} async-done(((bf16[1024,1024]{1,0:T(8,128)(2,1)}), bf16[128,1024]{1,0:T(8,128)(2,1)}) %reduce-scatter.37.cloned.1.call-update) | async-done | bytes 262160
  1128.2 13.5 reduce-scatter.31.cloned.1.call-done
  1141.7 70.9 %reduce-scatter.29.cloned.1.call-done = bf16[64,3072]{1,0:T(8,128)(2,1)} async-done(((bf16[1024,3072]{1,0:T(8,128)(2,1)}), bf16[64,3072]{1,0:T(8,128)(2,1)}) %reduce-scatter.29.cloned.1.call-update) | async-done | bytes 393232 | tf_op jit(solution)/shard_map/reduce_scatter | solution.py:316
  1212.6 75.0 %reduce-scatter.35.cloned.1.call-done = bf16[256,1024]{1,0:T(8,128)(2,1)} async-done(((bf16[4096,1024]{1,0:T(8,128)(2,1)}), bf16[256,1024]{1,0:T(8,128)(2,1)}) %reduce-scatter.35.cloned.1.call-update) | async-done | bytes 524304 | tf_op jit(solution)/shard_map/reduce_scatter | solution.py:325
  1287.6 75.9 %reduce-scatter.33.cloned.1.call-done = bf16[64,4096]{1,0:T(8,128)(2,1)} async-done(((bf16[1024,4096]{1,0:T(8,128)(2,1)}), bf16[64,4096]{1,0:T(8,128)(2,1)}) %reduce-scatter.33.cloned.1.call-update) | async-done | bytes 524304 | tf_op jit(solution)/shard_map/reduce_scatter | solution.py:322
  1375.4 50.6 %reduce-scatter.41.cloned.1.call-done = bf16[64,2]{1,0:T(8,128)(2,1)} async-done(((bf16[1024,2]{1,0:T(8,128)(2,1)}), bf16[64,2]{1,0:T(8,128)(2,1)}) %reduce-scatter.41.cloned.1.call-update) | async-done | bytes 272
  1426.7 61.2 %reduce-scatter.43.cloned.1.call-done = bf16[64,2]{1,0:T(8,128)(2,1)} async-done(((bf16[1024,2]{1,0:T(8,128)(2,1)}), bf16[64,2]{1,0:T(8,128)(2,1)}) %reduce-scatter.43.cloned.1.call-update) | async-done | bytes 272
  1488.7 42.2 %all-reduce = (bf16[2,64]{1,0:T(2,128)(2,1)S(1)}, bf16[2,64]{1,0:T(2,128)(2,1)S(1)}, bf16[1,2,1024]{2,1,0:T(2,128)(2,1)S(1)}, bf16[1,2,1024]{2,1,0:T(2,128)(2,1)S(1)}, bf16[1,1024]{1,0:T(2,128)(2,1)S(1)}) all-reduce(bf16[2,64]{1,0:T(2,128)(2,1)S(1)} %copy.46, ...), channel_id=1, replica_groups=mesh['seq'=8,'fsdp'=16] {'seq'}, use_global_device_ids=true, to_apply=%region_29.30 | all-reduce | flops 5376 | bytes 21504 | tf_op jit(solution)/shard_map/psum | solution.py:330
  1533.9 60.1 %all-reduce.4.cloned.1.call-done = (bf16[64,3072]{1,0:T(8,128)(2,1)}, bf16[64,1024]{1,0:T(8,128)(2,1)}, bf16[64,4096]{1,0:T(8,128)(2,1)}, bf16[256,1024]{1,0:T(8,128)(2,1)}) async-done(((bf16[64,3072]{1,0:T(8,128)(2,1)}, bf16[64,1024]{1,0:T(8,128)(2,1)}, bf16[64,4096]{1,0:T(8,128)(2,1)}, bf16[256,1024]{1,0:T(8,128)(2,1)}), (bf16[64,3072]{1,0:T(8,128)(2,1)}, bf16[64,1024]{1,0:T(8,128)(2,1)}, ...) | async-done | bytes 1572880 | tf_op jit(solution)/shard_map/psum | solution.py:332
  (279 shorter events, 225.8 us)
Async XLA Ops:
  7.2 462.7 %copy-start = (bf16[1,128,1024]{2,1,0:T(8,128)(2,1)S(1)}, bf16[1,128,1024]{2,1,0:T(8,128)(2,1)}, u32[]{:S(2)}) copy-start(bf16[1,128,1024]{2,1,0:T(8,128)(2,1)} %param.29) | copy-start | bytes 786436
  7.2 46.8 %all-gather.15.cloned.1.call-start = ((), (), s32[]{:S(2)}) async-start(), calls=%async_computation.16 | async-start | bytes 6684672 | tf_op jit(solution)/shard_map/all_gather | solution.py:60
  7.9 107.3 %all-gather.33.cloned.1.call-start = ((), (), s32[]{:S(2)}) async-start(), calls=%async_computation.33 | async-start | bytes 2359296 | tf_op jit(solution)/shard_map/all_gather | solution.py:75
  59.2 111.2 %all-gather.31.cloned.1.call-start = ((), (), s32[]{:S(2)}) async-start(), calls=%async_computation.32 | async-start | bytes 2359296 | tf_op jit(solution)/shard_map/all_gather | solution.py:76
  60.0 142.9 %all-gather.17.cloned.1.call-start = ((), (), s32[]{:S(2)}) async-start(), calls=%async_computation.17 | async-start | bytes 2228224 | tf_op jit(solution)/shard_map/all_gather | solution.py:61
  60.5 196.5 %all-gather.19.cloned.1.call-start = ((), (), s32[]{:S(2)}) async-start(), calls=%async_computation.18 | async-start | bytes 8912896 | tf_op jit(solution)/shard_map/all_gather | solution.py:62
  61.1 250.5 %all-gather.21.cloned.1.call-start = ((), (), s32[]{:S(2)}) async-start(), calls=%async_computation.19 | async-start | bytes 8912896 | tf_op jit(solution)/shard_map/all_gather | solution.py:63
  176.3 85.5 %copy-start.26 = (bf16[16,64,128]{2,1,0:T(8,128)(2,1)}, bf16[16,64,128]{2,1,0:T(8,128)(2,1)S(1)}, u32[]{:S(2)}) copy-start(bf16[16,64,128]{2,1,0:T(8,128)(2,1)S(1)} %fusion.33) | copy-start | bytes 786436
  317.5 10.7 all-to-all-start
  323.3 62.2 %all-gather.23.cloned.1.call-start = ((), (), s32[]{:S(2)}) async-start(), calls=%async_computation.20 | async-start | bytes 2359296 | tf_op jit(solution)/shard_map/all_gather | solution.py:134
  329.7 136.1 %reduce-scatter.21.cloned.1.call-start = ((), (), s32[]{:S(2)}) async-start(), calls=%async_computation.21 | async-start | bytes 2359296 | tf_op jit(solution)/shard_map/reduce_scatter | solution.py:137
  392.8 83.0 %copy-start.28 = (bf16[1,1024]{1,0:T(2,128)(2,1)S(1)}, bf16[1,1024]{1,0:T(2,128)(2,1)}, u32[]{:S(2)}) copy-start(bf16[1,1024]{1,0:T(2,128)(2,1)} %param.28) | copy-start | bytes 6148
  392.8 129.9 %all-gather.25.cloned.1.call-start = ((), (), s32[]{:S(2)}) async-start(), calls=%async_computation.22 | async-start | bytes 2359296 | tf_op jit(solution)/shard_map/all_gather | solution.py:134
  470.8 9.8 all-to-all-start.2
  475.8 101.7 %all-gather.27.cloned.1.call-start = ((), (), s32[]{:S(2)}) async-start(), calls=%async_computation.24 | async-start | bytes 2359296 | tf_op jit(solution)/shard_map/all_gather | solution.py:180
  481.5 173.2 %reduce-scatter.23.cloned.1.call-start = ((), (), s32[]{:S(2)}) async-start(), calls=%async_computation.23 | async-start | bytes 2359296 | tf_op jit(solution)/shard_map/reduce_scatter | solution.py:137
  530.2 202.6 %reduce-scatter.25.cloned.1.call-start = ((), (), s32[]{:S(2)}) async-start(), calls=%async_computation.25 | async-start | bytes 2359296 | tf_op jit(solution)/shard_map/reduce_scatter | solution.py:191
  586.1 146.6 %copy-start.8 = (bf16[128,1024]{1,0:T(8,128)(2,1)S(1)}, bf16[128,1024]{1,0:T(8,128)(2,1)}, u32[]{:S(2)}) copy-start(bf16[128,1024]{1,0:T(8,128)(2,1)} %reduce-scatter.21.cloned.1.call-done) | copy-start | bytes 786436
  586.1 204.8 %all-gather.29.cloned.1.call-start = ((), (), s32[]{:S(2)}) async-start(), calls=%async_computation.26 | async-start | bytes 2359296 | tf_op jit(solution)/shard_map/all_gather | solution.py:180
  737.9 134.8 %reduce-scatter.27.cloned.1.call-start = ((), (), s32[]{:S(2)}) async-start(), calls=%async_computation.27 | async-start | bytes 2359296 | tf_op jit(solution)/shard_map/reduce_scatter | solution.py:191
  877.4 9.7 all-to-all-start.3
  882.3 122.6 %reduce-scatter.39.cloned.1.call-start = ((), (), s32[]{:S(2)}) async-start(), calls=%async_computation.35 | async-start | bytes 2359296
  929.5 152.9 %reduce-scatter.37.cloned.1.call-start = ((), (), s32[]{:S(2)}) async-start(), calls=%async_computation.34 | async-start | bytes 2359296
  958.8 182.9 %reduce-scatter.31.cloned.1.call-start = ((), (), s32[]{:S(2)}) async-start(), calls=%async_computation.29 | async-start | bytes 2228224 | tf_op jit(solution)/shard_map/reduce_scatter | solution.py:319
  962.0 250.6 %reduce-scatter.29.cloned.1.call-start = ((), (), s32[]{:S(2)}) async-start(), calls=%async_computation.28 | async-start | bytes 6684672 | tf_op jit(solution)/shard_map/reduce_scatter | solution.py:316
  1092.9 194.7 %reduce-scatter.35.cloned.1.call-start = ((), (), s32[]{:S(2)}) async-start(), calls=%async_computation.31 | async-start | bytes 8912896 | tf_op jit(solution)/shard_map/reduce_scatter | solution.py:325
  1098.6 264.9 %reduce-scatter.33.cloned.1.call-start = ((), (), s32[]{:S(2)}) async-start(), calls=%async_computation.30 | async-start | bytes 8912896 | tf_op jit(solution)/shard_map/reduce_scatter | solution.py:322
  1114.0 12.6 all-to-all-start.1
  1118.9 307.1 %reduce-scatter.41.cloned.1.call-start = ((), (), s32[]{:S(2)}) async-start(), calls=%async_computation.36 | async-start | bytes 278528
  1125.3 362.6 %reduce-scatter.43.cloned.1.call-start = ((), (), s32[]{:S(2)}) async-start(), calls=%async_computation.37 | async-start | bytes 278528
  1126.3 467.7 %all-reduce.4.cloned.1.call-start = ((), (), s32[]{:S(2)}) async-start(), calls=%async_computation.38 | async-start | bytes 3145728 | tf_op jit(solution)/shard_map/psum | solution.py:332
  1126.6 237.0 %copy-start.38 = (bf16[1024,1024]{1,0:T(8,128)(2,1)S(1)}, bf16[1024,1024]{1,0:T(8,128)(2,1)}, u32[]{:S(2)}) copy-start(bf16[1024,1024]{1,0:T(8,128)(2,1)} %all-gather.29.cloned.1.call-done) | copy-start | bytes 6291460
  (42 other events, 405.2 us)
Sparse Core Ops, SparseCore 0:
  9.7 44.2 all-gather.14
  59.4 55.8 all-gather.32
  118.0 52.3 all-gather.30
  172.0 30.8 all-gather.16
  204.4 52.6 all-gather.18
  258.6 52.9 all-gather.20
  329.8 55.5 all-gather.22
  392.9 72.8 reduce-scatter.20
  470.0 52.7 all-gather.24
  525.6 51.8 all-gather.26
  581.8 72.8 reduce-scatter.22
  658.8 73.8 reduce-scatter.24
  738.0 52.8 all-gather.28
  799.8 72.8 reduce-scatter.26
  929.6 75.2 reduce-scatter.38
  1008.4 73.8 reduce-scatter.36
  1085.1 56.5 reduce-scatter.30
  1144.0 68.5 reduce-scatter.28
  1215.0 72.5 reduce-scatter.34
  1289.9 73.6 reduce-scatter.32
  1366.5 59.4 reduce-scatter.40
  1429.0 58.9 reduce-scatter.42
  1490.7 103.1 all-reduce.3
where the time goes:
time: 1620 us; the launch traced here: 1610 us
  waiting for transfers between devices  1260 us (78%)
  matrix products  125 us (8%)
  blocking collectives  75.1 us (5%)
  local copies, waits for them, and re-layouts  63.6 us (4%)
  other arithmetic  45.1 us (3%)
  starting transfers between devices  22.6 us (1%)
    unnamed x27, waiting for transfers between devices  226 us
    reduce_scatter x2, waiting for transfers between devices, on_device(): lax.psum_scatter(row_product(grad_pre, exp_in[0, sublayer], 'rf,df->rd')....  151 us
    reduce_scatter x2, waiting for transfers between devices, on_device(): lax.psum_scatter(row_product(expert_acted, exp_out[0, sublayer], 'rf,fd->...  141 us
    all_gather x2, waiting for transfers between devices, on_device(): lax.all_gather(grad_stream.astype(jnp.bfloat16), 'seq', axis=0, tiled=True)  100 us
    all_gather x2, waiting for transfers between devices, on_device(): every_row = lax.all_gather(expert_normed, 'seq', axis=0, tiled=True)  96.5 us
    reduce_scatter x1, waiting for transfers between devices, on_device(): lax.psum_scatter(dense_terms[4].astype(jnp.bfloat16), 'fsdp', scatter_dim...  75.9 us
    reduce_scatter x1, waiting for transfers between devices, on_device(): lax.psum_scatter(dense_terms[5].astype(jnp.bfloat16), 'fsdp', scatter_dim...  75 us
    reduce_scatter x1, waiting for transfers between devices, on_device(): lax.psum_scatter(dense_terms[2].astype(jnp.bfloat16), 'fsdp', scatter_dim...  70.9 us
  transfers between devices with their start and end apart: 27, of which 26 were waited for; matrix products, arithmetic and copies ran while one was open for 8% of the time, Pallas kernels for 0%

commit v1 on v0

--- a/solution.py
+++ b/solution.py
@@ -1,11 +1,14 @@
 import jax
 import jax.numpy as jnp
 from jax import lax
+from jax.experimental import pallas as pl
+from jax.experimental.pallas import tpu as pltpu
 from jax.sharding import PartitionSpec as P
 
 HEADS = 16
 
 
+MESH = pl.DeviceIdType.MESH
 epsilon = 1e-05
 masked_score = -1e30
 
@@ -30,6 +33,491 @@
 def gelu_back(pre_act, grad_acted):
     unused, slope_pull = jax.vjp(jax.nn.gelu, pre_act)
     return slope_pull(grad_acted)[0]
+
+
+def split_sum(values):
+    return jnp.sum(values, axis=-1, keepdims=True)
+
+
+def norm_parts(values):
+    average = split_sum(values) * (1.0 / values.shape[-1])
+    centered = values - average
+    spread = split_sum(centered * centered) * (1.0 / values.shape[-1])
+    scale = lax.rsqrt(spread + epsilon)
+    return centered * scale, scale
+
+
+def norm_back(grad_normed, gain, xhat, scale):
+    width = 1.0 / xhat.shape[-1]
+    u = grad_normed * gain
+    return scale * (u - split_sum(u) * width - xhat * (split_sum(u * xhat) * width))
+
+
+def gelu_parts(pre):
+    inner = 0.7978845608028654
+    cubic = 0.044715
+    square = pre * pre
+    t = jnp.tanh(inner * pre * (1.0 + cubic * square))
+    half = 0.5 * (1.0 + t)
+    slope = half + 0.5 * pre * (1.0 - t * t) * (inner * (1.0 + 3.0 * cubic * square))
+    return pre * half, slope
+
+
+def nn(a, b):
+    return lax.dot_general(a, b, (((1,), (0,)), ((), ())), preferred_element_type=jnp.float32)
+
+
+def nt(a, b):
+    return lax.dot_general(a, b, (((1,), (1,)), ((), ())), preferred_element_type=jnp.float32)
+
+
+def tn(a, b):
+    return lax.dot_general(a, b, (((0,), (0,)), ((), ())), preferred_element_type=jnp.float32)
+
+
+def place():
+    s, f = lax.axis_index("seq"), lax.axis_index("fsdp")
+    return lax.div(s, 2), lax.rem(s, 2), f, lax.rem(f, 2)
+
+
+def block(index):
+    return pl.ds(pl.multiple_of(index * 128, 128), 128)
+
+
+def order(i):
+    return i + lax.div(i, 2) - 2 * lax.div(i, 3)
+
+
+class Line:
+    def __init__(self, send, recv):
+        self.z, self.yh, self.f, self.c = place()
+        self.send, self.recv = send, recv
+
+    def index(self, d):
+        return lax.rem(self.z + d, 4)
+
+    def copy(self, phase, d, src, dst):
+        return pltpu.make_async_remote_copy(
+            src_ref=src,
+            dst_ref=dst,
+            send_sem=self.send.at[phase, d - 1],
+            recv_sem=self.recv.at[phase, d - 1],
+            device_id=(2 * self.index(d) + self.yh, self.f),
+            device_id_type=MESH,
+        )
+
+    def spread(self, phase, buf):
+        for d in (1, 3, 2):
+            self.copy(phase, d, buf.at[block(self.z)], buf.at[block(self.z)]).start()
+
+    def arrived(self, phase, d, buf):
+        dst = buf.at[block(self.index(d))]
+        pltpu.make_async_remote_copy(
+            src_ref=dst,
+            dst_ref=dst,
+            send_sem=self.send.at[phase, 3 - d],
+            recv_sem=self.recv.at[phase, 3 - d],
+            device_id=(2 * self.index(d) + self.yh, self.f),
+            device_id_type=MESH,
+        ).wait_recv()
+
+    def give(self, phase, d, src, dst):
+        self.copy(phase, d, src.at[block(self.index(d))], dst.at[block(self.z)]).start()
+
+    def sent(self, phase, buf):
+        for d in (1, 3, 2):
+            self.copy(phase, d, buf.at[block(self.z)], buf.at[block(self.z)]).wait_send()
+
+    def total(self, phase, own, parts):
+        acc = own[block(self.z), :].astype(jnp.float32)
+        for d in (1, 3, 2):
+            self.arrived(phase, d, parts)
+            acc += parts[block(self.index(d)), :].astype(jnp.float32)
+        return acc
+
+
+class Columns:
+    def __init__(self, send, recv):
+        self.z, self.yh, self.f, self.c = place()
+        self.m = self.f - self.c + self.yh
+        self.send, self.recv = send, recv
+
+    def device(self, q):
+        return (2 * self.z + lax.rem(q, 2), q - lax.rem(q, 2) + self.c)
+
+    def piece(self, q):
+        return pl.ds(pl.multiple_of(q * 16, 16), 16)
+
+    def copy(self, phase, d, src, dst):
+        q = lax.rem(self.m + d, 16)
+        return pltpu.make_async_remote_copy(
+            src_ref=src.at[self.piece(q)],
+            dst_ref=dst.at[self.piece(self.m)],
+            send_sem=self.send.at[phase, d - 1],
+            recv_sem=self.recv.at[phase, d - 1],
+            device_id=self.device(q),
+            device_id_type=MESH,
+        )
+
+    def start(self, phase, src, dst):
+        def one(i, carry):
+            self.copy(phase, i + 1, src, dst).start()
+            return carry
+
+        lax.fori_loop(0, 15, one, 0)
+        dst[self.piece(self.m), :] = src[self.piece(self.m), :]
+
+    def wait(self, phase, src, dst):
+        def one(i, carry):
+            q = lax.rem(self.m + 15 - i, 16)
+            pltpu.make_async_remote_copy(
+                src_ref=dst.at[self.piece(q)],
+                dst_ref=dst.at[self.piece(q)],
+                send_sem=self.send.at[phase, i],
+                recv_sem=self.recv.at[phase, i],
+                device_id=self.device(q),
+                device_id_type=MESH,
+            ).wait_recv()
+            return carry
+
+        lax.fori_loop(0, 15, one, 0)
+
+    def sent(self, phase, src, dst):
+        def one(i, carry):
+            self.copy(phase, i + 1, src, dst).wait_send()
+            return carry
+
+        lax.fori_loop(0, 15, one, 0)
+
+
+def placings(route):
+    row = lax.broadcasted_iota(jnp.int32, (256, 128), 0)
+    inner = row & 15
+    slot = (row >> 4) * 8 + (inner & 7)
+    hit = slot == route
+    left = jnp.where(hit & (inner < 8), 1.0, 0.0).astype(jnp.bfloat16)
+    right = jnp.where(hit & (inner >= 8), 1.0, 0.0).astype(jnp.bfloat16)
+    return left, right
+
+
+def to_pieces(left, right, rows):
+    half = rows.shape[1] // 2
+    return (nn(left, rows[:, :half]) + nn(right, rows[:, half:])).astype(jnp.bfloat16)
+
+
+def from_pieces(left, right, pieces):
+    return jnp.concatenate([tn(left, pieces), tn(right, pieces)], axis=1).astype(jnp.bfloat16)
+
+
+def rows_of(pieces):
+    wide = pieces.astype(jnp.float32).reshape(16, 2, 8, 512)
+    return jnp.concatenate([wide[:, 0].reshape(128, 512), wide[:, 1].reshape(128, 512)], axis=1)
+
+
+def pieces_of(rows):
+    left = rows[:, :512].reshape(16, 1, 8, 512)
+    right = rows[:, 512:].reshape(16, 1, 8, 512)
+    return jnp.concatenate([left, right], axis=1).reshape(256, 512).astype(jnp.bfloat16)
+
+
+def expert_kernel(
+    hid, cot, route, vec, in_a, in_b, out_a, out_b,
+    res, gh, vecg, gin, gout,
+    w_in, w_out, sendh, sendc, sendr, sendg, arrh, arrc, arrr, arrg,
+    e0, e1, g0, g1, ps0, ps1, pr0, pr1, pb0, pb1,
+    act0, act1, dg0, dg1, gp0, gp1,
+    arrived, cota, base, xh0, xh1, sc,
+    ga_in, ga_out, sb_in, sb_out, rb_in, rb_out,
+    wsem, zs, zr, cs, cr, ks, kr, osem,
+):
+    line, cols = Line(zs, zr), Columns(cs, cr)
+    z, yh, f, c = place()
+    other = (lax.axis_index("seq"), f + 1 - 2 * c)
+    bar = pltpu.get_barrier_semaphore()
+
+    def greet(i, carry):
+        pl.semaphore_signal(bar, inc=1, device_id=cols.device(lax.rem(cols.m + i + 1, 16)), device_id_type=MESH)
+        return carry
+
+    lax.fori_loop(0, 15, greet, 0)
+    for d in (1, 2, 3):
+        pl.semaphore_signal(bar, inc=1, device_id=(2 * line.index(d) + yh, f), device_id_type=MESH)
+    pl.semaphore_signal(bar, inc=1, device_id=other, device_id_type=MESH)
+    loads = []
+    for k in range(2):
+        loads += [
+            pltpu.make_async_copy(in_a.at[k], w_in.at[k, :, 0:512], wsem.at[k, 0]),
+            pltpu.make_async_copy(in_b.at[k], w_in.at[k, :, 512:1024], wsem.at[k, 1]),
+            pltpu.make_async_copy(out_a.at[k], w_out.at[k, 0:512, :], wsem.at[k, 2]),
+            pltpu.make_async_copy(out_b.at[k], w_out.at[k, 512:1024, :], wsem.at[k, 3]),
+        ]
+    for load in loads:
+        load.start()
+    left, right = placings(route[0:1, :])
+    sendh[...] = to_pieces(left, right, hid[...])
+    sendc[...] = to_pieces(left, right, cot[...])
+    pl.semaphore_wait(bar, 19)
+    cols.start(0, sendh, arrh)
+    cols.start(1, sendc, arrc)
+    cols.wait(0, sendh, arrh)
+    gain = [vec[0:1, :], vec[1:2, :]]
+    bias = [vec[2:3, :], vec[3:4, :]]
+    rows = rows_of(arrh[...])
+    arrived[...] = rows
+    xhat, scale = norm_parts(rows)
+    xh0[...] = xhat
+    sc[0] = jnp.broadcast_to(scale, (128, 128))
+    e0[block(z), :] = (xhat * gain[0] + bias[0]).astype(jnp.bfloat16)
+    line.spread(0, e0)
+    cols.wait(1, sendc, arrc)
+    coti = rows_of(arrc[...])
+    cota[...] = coti
+    gating = jax.nn.sigmoid(split_sum(arrived[...] * vec[4:5, :]))
+    sc[2] = jnp.broadcast_to(gating, (128, 128))
+    g1[block(z), :] = (gating * coti).astype(jnp.bfloat16)
+    line.spread(3, g1)
+    for load in loads:
+        load.wait()
+
+    def forward(k, j, rows_in, act, dg):
+        values = rows_in[block(j), :]
+        for n in range(4):
+            tile = slice(n * 256, (n + 1) * 256)
+            pre = nn(values, w_in[k, :, tile])
+            acted, slope = gelu_parts(pre)
+            act[block(j), tile] = acted.astype(jnp.bfloat16)
+            dg[block(j), tile] = slope
+
+    def project(k, j, act, part):
+        values = act[block(j), :]
+        for n in range(4):
+            tile = slice(n * 256, (n + 1) * 256)
+            part[block(j), tile] = nn(values, w_out[k, :, tile]).astype(jnp.bfloat16)
+
+    def backward(k, j, grad, dg, gp, part):
+        values = grad[block(j), :]
+        for n in range(4):
+            tile = slice(n * 256, (n + 1) * 256)
+            slope = dg[block(j), tile] * nt(values, w_out[k, tile, :])
+            gp[block(j), tile] = slope.astype(jnp.bfloat16)
+        pres = gp[block(j), :]
+        for n in range(4):
+            tile = slice(n * 256, (n + 1) * 256)
+            part[block(j), tile] = nt(pres, w_in[k, tile, :]).astype(jnp.bfloat16)
+
+    def sub0(i, carry):
+        d = order(i)
+        j = line.index(d)
+
+        @pl.when(i > 0)
+        def _():
+            line.arrived(0, d, e0)
+
+        forward(0, j, e0, act0, dg0)
+        project(0, j, act0, ps0)
+
+        @pl.when(i > 0)
+        def _():
+            line.give(1, d, ps0, pr0)
+
+        return carry
+
+    lax.fori_loop(0, 4, sub0, 0)
+    stream = arrived[...] + line.total(1, ps0, pr0)
+    base[...] = stream
+    xhat, scale = norm_parts(stream)
+    xh1[...] = xhat
+    sc[1] = jnp.broadcast_to(scale, (128, 128))
+    e1[block(z), :] = (xhat * gain[1] + bias[1]).astype(jnp.bfloat16)
+    line.spread(2, e1)
+    line.sent(1, ps0)
+
+    def sub1(i, carry):
+        d = order(i)
+        j = line.index(d)
+
+        @pl.when(i > 0)
+        def _():
+            line.arrived(2, d, e1)
+            line.arrived(3, d, g1)
+
+        forward(1, j, e1, act1, dg1)
+        backward(1, j, g1, dg1, gp1, ps0)
+
+        @pl.when(i > 0)
+        def _():
+            line.give(4, d, ps0, pb1)
+
+        project(1, j, act1, ps1)
+
+        @pl.when(i > 0)
+        def _():
+            line.give(5, d, ps1, pr1)
+
+        return carry
+
+    lax.fori_loop(0, 4, sub1, 0)
+
+    def weight_grads(k, rows_in, gp, act, grad):
+        def one(n, carry):
+            tile = pl.ds(pl.multiple_of(n * 256, 256), 256)
+            tile_b = pl.ds(pl.multiple_of(n * 256 + 512, 256), 256)
+            ga_out[k, tile, :] = tn(act[:, tile], grad[...])
+            sb_out[k, tile, :] = tn(act[:, tile_b], grad[...]).astype(jnp.bfloat16)
+            return carry
+
+        lax.fori_loop(0, 2, one, 0)
+
+        def two(n, carry):
+            tile = pl.ds(pl.multiple_of(n * 256, 256), 256)
+            ga_in[k, tile, :] = tn(rows_in[:, tile], gp[:, 0:512])
+            sb_in[k, tile, :] = tn(rows_in[:, tile], gp[:, 512:1024]).astype(jnp.bfloat16)
+            return carry
+
+        lax.fori_loop(0, 4, two, 0)
+
+    def swap(k, i, src, dst):
+        return pltpu.make_async_remote_copy(
+            src_ref=src.at[k],
+            dst_ref=dst.at[k],
+            send_sem=ks.at[k, i],
+            recv_sem=kr.at[k, i],
+            device_id=other,
+            device_id_type=MESH,
+        )
+
+    weight_grads(1, e1, gp1, act1, g1)
+    swap(1, 0, sb_in, rb_in).start()
+    swap(1, 1, sb_out, rb_out).start()
+    grad_normed = line.total(4, ps0, pb1)
+    grad_stream = sc[2][:, 0:1] * cota[...]
+    grad_stream += norm_back(grad_normed, gain[1], xh1[...], sc[1][:, 0:1])
+    g0[block(z), :] = grad_stream.astype(jnp.bfloat16)
+    line.spread(6, g0)
+    vecg[1:2, :] = jnp.sum(grad_normed * xh1[...], axis=0, keepdims=True)
+    vecg[3:4, :] = jnp.sum(grad_normed, axis=0, keepdims=True)
+    line.sent(4, ps0)
+    stream = base[...] + line.total(5, ps1, pr1)
+    base[...] = grad_stream
+    gate = sc[2][:, 0:1]
+    diff = stream - arrived[...]
+    sendr[...] = pieces_of(arrived[...] + gate * diff)
+    grad_gating = split_sum(cota[...] * diff)
+    grad_logit = gate * (1.0 - gate) * grad_gating
+    vecg[4:5, :] = jnp.sum(grad_logit * arrived[...], axis=0, keepdims=True)
+    sc[3] = jnp.broadcast_to(grad_logit, (128, 128))
+
+    def sub0_back(i, carry):
+        d = order(i)
+        j = line.index(d)
+
+        @pl.when(i > 0)
+        def _():
+            line.arrived(6, d, g0)
+
+        backward(0, j, g0, dg0, gp0, ps0)
+
+        @pl.when(i > 0)
+        def _():
+            line.give(7, d, ps0, pb0)
+
+        return carry
+
+    lax.fori_loop(0, 4, sub0_back, 0)
+    cols.start(2, sendr, arrr)
+    weight_grads(0, e0, gp0, act0, g0)
+    swap(0, 0, sb_in, rb_in).start()
+    swap(0, 1, sb_out, rb_out).start()
+    grad_normed = line.total(7, ps0, pb0)
+    vecg[0:1, :] = jnp.sum(grad_normed * xh0[...], axis=0, keepdims=True)
+    vecg[2:3, :] = jnp.sum(grad_normed, axis=0, keepdims=True)
+    grad_stream = base[...] + norm_back(grad_normed, gain[0], xh0[...], sc[0][:, 0:1])
+    grad_stream += (1.0 - sc[2][:, 0:1]) * cota[...] + sc[3][:, 0:1] * vec[4:5, :]
+    sendg[...] = pieces_of(grad_stream)
+    cols.start(3, sendg, arrg)
+    cols.wait(3, sendg, arrg)
+    left, right = placings(route[0:1, :])
+    gh[...] = from_pieces(left, right, arrg[...])
+    cols.wait(2, sendr, arrr)
+    res[...] = from_pieces(left, right, arrr[...])
+    stores = []
+    for k in (1, 0):
+        swap(k, 0, sb_in, rb_in).wait_recv()
+        swap(k, 1, sb_out, rb_out).wait_recv()
+        ga_in[k] += rb_in[k].astype(jnp.float32)
+        ga_out[k] += rb_out[k].astype(jnp.float32)
+        stores += [
+            pltpu.make_async_copy(ga_in.at[k], gin.at[k], osem.at[k, 0]),
+            pltpu.make_async_copy(ga_out.at[k], gout.at[k], osem.at[k, 1]),
+        ]
+        stores[-1].start()
+        stores[-2].start()
+    vecg[5:8, :] = jnp.zeros((3, 1024), jnp.float32)
+    for k in (0, 1):
+        swap(k, 0, sb_in, rb_in).wait_send()
+        swap(k, 1, sb_out, rb_out).wait_send()
+    line.sent(0, e0)
+    line.sent(2, e1)
+    line.sent(3, g1)
+    line.sent(5, ps1)
+    line.sent(6, g0)
+    line.sent(7, ps0)
+    cols.sent(0, sendh, arrh)
+    cols.sent(1, sendc, arrc)
+    cols.sent(2, sendr, arrr)
+    cols.sent(3, sendg, arrg)
+    for store in stores:
+        store.wait()
+
+
+def expert_call(hid, cot, route, vec, in_a, in_b, out_a, out_b):
+    bf, f32 = jnp.bfloat16, jnp.float32
+    vmem, anywhere = pl.BlockSpec(memory_space=pltpu.VMEM), pl.BlockSpec(memory_space=pl.ANY)
+    line = [pltpu.VMEM((512, 1024), bf)]
+    rows = [pltpu.VMEM((128, 1024), f32)]
+    piece = [pltpu.VMEM((256, 512), bf)]
+    wide = [pltpu.VMEM((512, 1024), f32)]
+    return pl.pallas_call(
+        expert_kernel,
+        out_shape=(
+            jax.ShapeDtypeStruct((128, 1024), bf),
+            jax.ShapeDtypeStruct((128, 1024), bf),
+            jax.ShapeDtypeStruct((8, 1024), f32),
+            jax.ShapeDtypeStruct((2, 1024, 512), f32),
+            jax.ShapeDtypeStruct((2, 512, 1024), f32),
+        ),
+        in_specs=[vmem] * 4 + [anywhere] * 4,
+        out_specs=(vmem, vmem, vmem, anywhere, anywhere),
+        scratch_shapes=[
+            pltpu.VMEM((2, 1024, 1024), bf),
+            pltpu.VMEM((2, 1024, 1024), bf),
+            *(piece * 8),
+            *(line * 10),
+            *(line * 2),
+            *(wide * 2),
+            *(line * 2),
+            *(rows * 5),
+            pltpu.VMEM((4, 128, 128), f32),
+            pltpu.VMEM((2, 1024, 512), f32),
+            pltpu.VMEM((2, 512, 1024), f32),
+            pltpu.VMEM((2, 1024, 512), bf),
+            pltpu.VMEM((2, 512, 1024), bf),
+            pltpu.VMEM((2, 1024, 512), bf),
+            pltpu.VMEM((2, 512, 1024), bf),
+            pltpu.SemaphoreType.DMA((2, 4)),
+            pltpu.SemaphoreType.DMA((8, 3)),
+            pltpu.SemaphoreType.DMA((8, 3)),
+            pltpu.SemaphoreType.DMA((4, 15)),
+            pltpu.SemaphoreType.DMA((4, 15)),
+            pltpu.SemaphoreType.DMA((2, 2)),
+            pltpu.SemaphoreType.DMA((2, 2)),
+            pltpu.SemaphoreType.DMA((2, 2)),
+        ],
+        compiler_params=pltpu.CompilerParams(
+            collective_id=1, has_side_effects=True, vmem_limit_bytes=60 << 20
+        ),
+        name="experts",
+    )(hid, cot, route, vec, in_a, in_b, out_a, out_b)
 
 
 def on_device(
@@ -108,111 +596,37 @@
     hidden = (after + jnp.dot(acted, down_weight, preferred_element_type=jnp.float32)).astype(
         jnp.bfloat16
     )
-    expert_count = lax.axis_size("fsdp")
-    slot_of = route.reshape(tok_rows)
-    placing = (jnp.arange(tok_rows, dtype=jnp.int32)[:, None] == slot_of[None, :]).astype(
-        jnp.bfloat16
-    )
-    sending = jnp.dot(placing, hidden, preferred_element_type=jnp.float32).astype(jnp.bfloat16)
-    arrived = lax.all_to_all(
-        sending.reshape(expert_count, tok_rows // expert_count, model_width),
-        "fsdp",
-        split_axis=0,
-        concat_axis=0,
-        tiled=True,
-    )
-    arrived = arrived.reshape(tok_rows, model_width)
-    arrived_rows = arrived.astype(jnp.float32)
-    stream = arrived_rows
-    saved_rows = []
-    for sublayer in range(2):
-        expert_normed = norm_rows(
-            stream,
-            exp_gain[0, sublayer].astype(jnp.float32),
-            exp_bias[0, sublayer].astype(jnp.float32),
-        ).astype(jnp.bfloat16)
-        every_row = lax.all_gather(expert_normed, "seq", axis=0, tiled=True)
-        expert_pre = jnp.dot(every_row, exp_in[0, sublayer], preferred_element_type=jnp.float32)
-        expert_acted = jax.nn.gelu(expert_pre).astype(jnp.bfloat16)
-        branch = lax.psum_scatter(
-            row_product(expert_acted, exp_out[0, sublayer], "rf,fd->rd").astype(jnp.bfloat16),
-            "seq",
-            scatter_dimension=0,
-            tiled=True,
-        ).astype(jnp.float32)
-        saved_rows.append((stream, every_row, expert_pre, expert_acted))
-        stream = stream + branch
-    gating = jax.nn.sigmoid(jnp.dot(arrived, centroid[0], preferred_element_type=jnp.float32))[
-        :, None
-    ]
-    mixed_out = (arrived_rows + gating * (stream - arrived_rows)).astype(jnp.bfloat16)
-    returned = lax.all_to_all(
-        mixed_out.reshape(expert_count, tok_rows // expert_count, model_width),
-        "fsdp",
-        split_axis=0,
-        concat_axis=0,
-        tiled=True,
-    )
-    returned = returned.reshape(tok_rows, model_width)
-    result = returned[slot_of].reshape(seq_count, local_len, model_width)
-    grad_result = cotangent.reshape(tok_rows, model_width)
-    grad_slots = jnp.dot(placing, grad_result, preferred_element_type=jnp.float32).astype(
-        jnp.bfloat16
-    )
-    grad_arrived = lax.all_to_all(
-        grad_slots.reshape(expert_count, tok_rows // expert_count, model_width),
-        "fsdp",
-        split_axis=0,
-        concat_axis=0,
-        tiled=True,
-    )
-    grad_arrived = grad_arrived.reshape(tok_rows, model_width).astype(jnp.float32)
-    grad_gating = jnp.sum(grad_arrived * (stream - arrived_rows), axis=1, keepdims=True)
-    grad_logit = gating * (1.0 - gating) * grad_gating
-    grad_centre = jnp.sum(grad_logit * arrived_rows, axis=0)
-    grad_stream = gating * grad_arrived
-    gain_grads = [None, None]
-    bias_grads = [None, None]
-    in_grads = [None, None]
-    out_grads = [None, None]
-    for sublayer in (1, 0):
-        before, every_row, expert_pre, expert_acted = saved_rows[sublayer]
-        grad_every = lax.all_gather(grad_stream.astype(jnp.bfloat16), "seq", axis=0, tiled=True)
-        out_grads[sublayer] = jnp.einsum(
-            "rf,rd->fd", expert_acted, grad_every, preferred_element_type=jnp.float32
-        )
-        grad_act = jnp.einsum(
-            "rd,fd->rf", grad_every, exp_out[0, sublayer], preferred_element_type=jnp.float32
-        )
-        grad_pre = gelu_back(expert_pre, grad_act).astype(jnp.bfloat16)
-        in_grads[sublayer] = jnp.einsum(
-            "rd,rf->df", every_row, grad_pre, preferred_element_type=jnp.float32
-        )
-        grad_normed = lax.psum_scatter(
-            row_product(grad_pre, exp_in[0, sublayer], "rf,df->rd").astype(jnp.bfloat16),
-            "seq",
-            scatter_dimension=0,
-            tiled=True,
-        ).astype(jnp.float32)
-        unused, norm_pull = jax.vjp(
-            norm_rows,
-            before,
-            exp_gain[0, sublayer].astype(jnp.float32),
-            exp_bias[0, sublayer].astype(jnp.float32),
-        )
-        grad_before, gain_grads[sublayer], bias_grads[sublayer] = norm_pull(grad_normed)
-        grad_stream = grad_stream + grad_before
-    grad_arrived_in = (
-        grad_stream + (1.0 - gating) * grad_arrived + grad_logit * centroid[0].astype(jnp.float32)
-    ).astype(jnp.bfloat16)
-    sent_back = lax.all_to_all(
-        grad_arrived_in.reshape(expert_count, tok_rows // expert_count, model_width),
-        "fsdp",
-        split_axis=0,
-        concat_axis=0,
-        tiled=True,
-    )
-    grad_hidden = sent_back.reshape(tok_rows, model_width)[slot_of]
+    swap_pairs = []
+    core_pairs = []
+    for s in range(8):
+        for f in range(16):
+            same = s % 2 == f % 2
+            partner = s * 16 + f if same else (s + 1 - 2 * (s % 2)) * 16 + f + 1 - 2 * (f % 2)
+            swap_pairs.append((s * 16 + f, partner))
+            core_pairs.append((s * 16 + f, s * 16 + f + 1 - 2 * (f % 2)))
+    both = ("seq", "fsdp")
+    in_a = lax.ppermute(exp_in[0], both, swap_pairs)
+    out_a = lax.ppermute(exp_out[0], both, swap_pairs)
+    in_b = lax.ppermute(in_a, both, core_pairs)
+    out_b = lax.ppermute(out_a, both, core_pairs)
+    mine = lax.rem(lax.axis_index("seq"), 2) == lax.rem(lax.axis_index("fsdp"), 2)
+    vec = jnp.concatenate([exp_gain[0], exp_bias[0], centroid], axis=0)
+    vec = jnp.where(mine, vec, lax.ppermute(vec, both, core_pairs)).astype(jnp.float32)
+    vec = jnp.pad(vec, ((0, 3), (0, 0)))
+    result, grad_hidden, vec_grads, grad_in, grad_out_e = expert_call(
+        hidden, cotangent.reshape(tok_rows, model_width), route.reshape(1, tok_rows), vec, in_a, in_b, out_a, out_b
+    )
+    result = result.reshape(seq_count, local_len, model_width)
+    grad_exp_in = jnp.where(
+        mine, grad_in, lax.ppermute(grad_in.astype(jnp.bfloat16), both, swap_pairs).astype(jnp.float32)
+    )[None]
+    grad_exp_out = jnp.where(
+        mine, grad_out_e, lax.ppermute(grad_out_e.astype(jnp.bfloat16), both, swap_pairs).astype(jnp.float32)
+    )[None]
+    vec_grads = vec_grads[:5].astype(jnp.bfloat16)
+    vec_grads = vec_grads.astype(jnp.float32) + lax.ppermute(vec_grads, both, core_pairs).astype(jnp.float32)
+    upper = lax.rem(lax.axis_index("seq"), 2) == 1
+    vec_grads = jnp.stack([jnp.where(upper, 0.0, vec_grads), jnp.where(upper, vec_grads, 0.0)])
     gains, offsets, qkv_weight, out_weight, up_weight, down_weight = (
         lax.all_gather(norm_gain, "fsdp", axis=1, tiled=True),
         lax.all_gather(norm_bias, "fsdp", axis=1, tiled=True),
@@ -296,8 +710,6 @@
     )
     grad_rows_in, gain_one_grad, bias_one_grad = norm_pull(grad_normed_one)
     grad_input = (grad_after + grad_rows_in).reshape(seq_count, local_len, model_width)
-    grad_exp_in = jnp.stack(in_grads)[None]
-    grad_exp_out = jnp.stack(out_grads)[None]
     dense_terms = (
         jnp.stack([gain_one_grad, gain_two_grad]),
         jnp.stack([bias_one_grad, bias_two_grad]),
@@ -333,10 +745,9 @@
         lax.psum(shard_out.astype(jnp.bfloat16), "seq").astype(jnp.float32),
         lax.psum(shard_up.astype(jnp.bfloat16), "seq").astype(jnp.float32),
         lax.psum(shard_down.astype(jnp.bfloat16), "seq").astype(jnp.float32),
-        lax.psum(jnp.stack(gain_grads)[None].astype(jnp.bfloat16), "seq").astype(jnp.float32),
-        lax.psum(jnp.stack(bias_grads)[None].astype(jnp.bfloat16), "seq").astype(jnp.float32),
-        lax.psum(grad_centre[None].astype(jnp.bfloat16), "seq").astype(jnp.float32),
-    )
+        lax.psum(vec_grads.astype(jnp.bfloat16), "seq").astype(jnp.float32),
+    )
+    own = jnp.where(lax.rem(lax.axis_index("fsdp"), 2) == 1, summed[6][1], summed[6][0])
     return (
         result,
         grad_input,
@@ -346,11 +757,11 @@
         summed[3],
         summed[4],
         summed[5],
-        summed[6],
-        summed[7],
+        own[None, 0:2],
+        own[None, 2:4],
         grad_exp_in,
         grad_exp_out,
-        summed[8],
+        own[4:5],
     )
 
 

time: 1620 us -> 1180 us (0.73)
  waiting for transfers between devices: 1260 us -> 674 us
  Pallas kernels: 0 us -> 123 us
  starting transfers between devices: 22.6 us -> 97.1 us
  matrix products: 125 us -> 86.5 us
    reduce_scatter x4 -> x0, waiting for transfers between devices: 292 us -> none  [the longest x2 151 us: on_device(): lax.psum_scatter(row_product(grad_pre, exp_in[0, sublayer], 'rf,df->rd')....]
    all_gather x4 -> x0, waiting for transfers between devices: 196 us -> none  [the longest x2 100 us: on_device(): lax.all_gather(grad_stream.astype(jnp.bfloat16), 'seq', axis=0, tiled=True)]
    pallas_call x0 -> x1, Pallas kernels: none -> 123 us  [expert_call(): pl.pallas_call(expert_kernel, out_shape=(jax.ShapeDtypeStruct((128, 1024)...]
    ppermute x0 -> x8, starting transfers between devices: none -> 96.3 us  [the longest x1 26.8 us: on_device(): out_b = lax.ppermute(out_a, both, core_pairs)]
    all_gather x1, waiting for transfers between devices: 50.1 us -> 0.01 us  [on_device(): lax.all_gather(packed[:, :, 1], 'seq', axis=1, tiled=True)]
    dot_general x15 -> x1, matrix products: 45.4 us -> 5.63 us  [on_device(): jnp.dot(acted, down_weight, preferred_element_type=jnp.float32)]
    all_to_all x4 -> x0, starting transfers between devices: 20.4 us -> none  [the longest x1 5.82 us: on_device(): lax.all_to_all(sending.reshape(expert_count, tok_rows // expert_count, mo...]
    reduce_scatter x1, waiting for transfers between devices: 70.9 us -> 50.8 us  [on_device(): lax.psum_scatter(dense_terms[2].astype(jnp.bfloat16), 'fsdp', scatter_dim...]
  transfers between devices with their start and end apart: 27 -> 23, of which waited for: 26 -> 14; matrix products, arithmetic and copies ran while one was open for 8% -> 11% of each run, Pallas kernels for 0% -> 0%
where the time goes in v1:
time: 1180 us; the launch traced here: 1170 us
  waiting for transfers between devices  674 us (57%)
  Pallas kernels  123 us (10%)
  starting transfers between devices  97.1 us (8%)
  matrix products  86.5 us (7%)
  blocking collectives  76.2 us (6%)
  local copies, waits for them, and re-layouts  54 us (5%)
  other arithmetic  41.4 us (4%)
  between operations  14.9 us (1%)
    unnamed x19, waiting for transfers between devices  232 us
    pallas_call x1, Pallas kernels, expert_call(): pl.pallas_call(expert_kernel, out_shape=(jax.ShapeDtypeStruct((128, 1024)...  123 us
    reduce_scatter x1, waiting for transfers between devices, on_device(): lax.psum_scatter(dense_terms[4].astype(jnp.bfloat16), 'fsdp', scatter_dim...  75.4 us
    reduce_scatter x1, waiting for transfers between devices, on_device(): lax.psum_scatter(dense_terms[5].astype(jnp.bfloat16), 'fsdp', scatter_dim...  75.4 us
    psum x1, waiting for transfers between devices, on_device(): lax.psum(shard_qkv.astype(jnp.bfloat16), 'seq').astype(jnp.float32)  59.9 us
    all_gather x1, waiting for transfers between devices, on_device(): lax.all_gather(w_up, 'fsdp', axis=0, tiled=True)  51.9 us
    reduce_scatter x1, waiting for transfers between devices, on_device(): lax.psum_scatter(dense_terms[2].astype(jnp.bfloat16), 'fsdp', scatter_dim...  50.8 us
    all_gather x1, waiting for transfers between devices, on_device(): lax.all_gather(w_down, 'fsdp', axis=0, tiled=True)  49.8 us
  transfers between devices with their start and end apart: 23, of which 14 were waited for; matrix products, arithmetic and copies ran while one was open for 11% of the time, Pallas kernels for 0%

profile of v1, /device:TPU:4, one launch (start us, length us, event | category | flops | bytes accessed | tf_op | source)
XLA Modules:
  0.0 1167.4 jit_solution(14153367283008415263)
XLA Ops:
  8.0 16.7 %all-gather.2 = bf16[16,64,2]{1,2,0:T(2,128)(2,1)S(1)} all-gather(bf16[1,64,2]{1,2,0:T(2,128)(2,1)} %bitcast.197), channel_id=1, replica_groups=mesh['seq'=8,'fsdp'=16] {'fsdp'}, dimensions={0}, use_global_device_ids=true | all-gather | bytes 4352 | tf_op jit(solution)/shard_map/all_gather | solution.py:546
  24.7 16.3 %all-gather.3 = bf16[16,64,2]{1,2,0:T(2,128)(2,1)S(1)} all-gather(bf16[1,64,2]{1,2,0:T(2,128)(2,1)} %bitcast.198), channel_id=1, replica_groups=mesh['seq'=8,'fsdp'=16] {'fsdp'}, dimensions={0}, use_global_device_ids=true | all-gather | bytes 4352 | tf_op jit(solution)/shard_map/all_gather | solution.py:547
  43.4 10.6 all-gather.11.cloned.1.call-done
  61.8 17.2 %collective-permute-start.1 = (bf16[2,1024,512]{2,1,0:T(8,128)(2,1)}, bf16[2,1024,512]{2,1,0:T(8,128)(2,1)}, u32[]{:S(2)}, u32[]{:S(2)}) collective-permute-start(bf16[2,1024,512]{2,1,0:T(8,128)(2,1)} %bitcast.199), channel_id=1, source_target_pairs={{0,0},{1,16},{2,2},{3,18},{4,4},{5,20},{6,6},{7,22},{8,8},{9,24},{... | collective-permute-start | bytes 6291464 | tf_op jit(solution)/shard_map/ppermute | solution.py:608
  79.0 17.2 %collective-permute-start.3 = (bf16[2,512,1024]{2,1,0:T(8,128)(2,1)}, bf16[2,512,1024]{2,1,0:T(8,128)(2,1)}, u32[]{:S(2)}, u32[]{:S(2)}) collective-permute-start(bf16[2,512,1024]{2,1,0:T(8,128)(2,1)} %bitcast.200), channel_id=1, source_target_pairs={{0,0},{1,16},{2,2},{3,18},{4,4},{5,20},{6,6},{7,22},{8,8},{9,24},{... | collective-permute-start | bytes 6291464 | tf_op jit(solution)/shard_map/ppermute | solution.py:609
  100.8 26.8 %collective-permute-start.4 = (bf16[2,512,1024]{2,1,0:T(8,128)(2,1)}, bf16[2,512,1024]{2,1,0:T(8,128)(2,1)}, u32[]{:S(2)}, u32[]{:S(2)}) collective-permute-start(bf16[2,512,1024]{2,1,0:T(8,128)(2,1)} %collective-permute-done.3.out_a), channel_id=1, source_target_pairs={{0,1},{1,0},{2,3},{3,2},{4,5},{5,4},{6,7},{7,6},{8,9},{9,8},{10,11... | collective-permute-start | bytes 6291464 | tf_op jit(solution)/shard_map/ppermute | solution.py:611
  136.5 41.4 %all-gather.19.cloned.1.call-done = bf16[1,1024,1,1024]{1,3,2,0:T(8,128)(2,1)} async-done(((bf16[1,128,1,1024]{1,3,2,0:T(8,128)(2,1)}), bf16[1,1024,1,1024]{1,3,2,0:T(8,128)(2,1)}) %all-gather.19.cloned.1.call-update) | async-done | bytes 2097168 | tf_op jit(solution)/shard_map/all_gather | solution.py:564
  178.0 5.8 fusion.17
  183.8 26.6 %all-gather.13.cloned.1.call-done = bf16[1024,1024]{1,0:T(8,128)(2,1)} async-done(((bf16[64,1024]{1,0:T(8,128)(2,1)}), bf16[1024,1024]{1,0:T(8,128)(2,1)}) %all-gather.13.cloned.1.call-update) | async-done | bytes 2097168 | tf_op jit(solution)/shard_map/all_gather | solution.py:549
  212.8 51.9 %all-gather.15.cloned.1.call-done = bf16[1024,4096]{1,0:T(8,128)(2,1)} async-done(((bf16[64,4096]{1,0:T(8,128)(2,1)}), bf16[1024,4096]{1,0:T(8,128)(2,1)}) %all-gather.15.cloned.1.call-update) | async-done | bytes 8388624 | tf_op jit(solution)/shard_map/all_gather | solution.py:550
  269.3 49.8 %all-gather.17.cloned.1.call-done = bf16[4096,1024]{1,0:T(8,128)(2,1)} async-done(((bf16[256,1024]{1,0:T(8,128)(2,1)}), bf16[4096,1024]{1,0:T(8,128)(2,1)}) %all-gather.17.cloned.1.call-update) | async-done | bytes 8388624 | tf_op jit(solution)/shard_map/all_gather | solution.py:551
  324.8 122.8 %experts.1 = (bf16[128,1024]{1,0:T(8,128)(2,1)}, bf16[128,1024]{1,0:T(8,128)(2,1)}, f32[8,1024]{1,0:T(8,128)}, f32[2,1024,512]{2,1,0:T(8,128)}, f32[2,512,1024]{2,1,0:T(8,128)}) custom-call(bf16[128,1024]{1,0:T(8,128)(2,1)} %fusion.16.hid, bf16[128,1024]{1,0:T(8,128)(2,1)} %bitcast.186, s32[1,128]{1,0:T(1,128)} %bitcast.196, f32[8,1024]{1,0:T(8,128)} %pad_convert_fusion.vec, ...), custom_call_target="tpu_custom_call" | custom-call | tf_op jit(solution)/shard_map/experts/pallas_call | solution.py:480
  447.6 7.0 fusion.12
  454.7 6.8 multiply_reduce_fusion.1
  466.5 6.4 fusion.13
  473.0 10.9 copy.43
  488.3 6.5 multiply_reduce_fusion
  502.1 10.8 copy.41
  525.5 38.1 %reduce-scatter.27.cloned.1.call-done = bf16[128,1024]{1,0:T(8,128)(2,1)} async-done(((bf16[1024,1024]{1,0:T(8,128)(2,1)}), bf16[128,1024]{1,0:T(8,128)(2,1)}) %reduce-scatter.27.cloned.1.call-update) | async-done | bytes 262160
  567.5 73.7 %reduce-scatter.25.cloned.1.call-done = bf16[128,1024]{1,0:T(8,128)(2,1)} async-done(((bf16[1024,1024]{1,0:T(8,128)(2,1)}), bf16[128,1024]{1,0:T(8,128)(2,1)}) %reduce-scatter.25.cloned.1.call-update) | async-done | bytes 262160
  652.2 6.6 convolution_convert_fusion
  669.8 17.2 %collective-permute-start.7 = (bf16[2,512,1024]{2,1,0:T(8,128)(2,1)}, bf16[2,512,1024]{2,1,0:T(8,128)(2,1)}, u32[]{:S(2)}, u32[]{:S(2)}) collective-permute-start(bf16[2,512,1024]{2,1,0:T(8,128)(2,1)} %convert_element_type.295), channel_id=1, source_target_pairs={{0,0},{1,16},{2,2},{3,18},{4,4},{5,20},{6,6},{7,22},{8,8},{9,24},{... | collective-permute-start | bytes 6291464 | tf_op jit(solution)/shard_map/ppermute | solution.py:624
  688.6 17.2 %collective-permute-start.6 = (bf16[2,1024,512]{2,1,0:T(8,128)(2,1)}, bf16[2,1024,512]{2,1,0:T(8,128)(2,1)}, u32[]{:S(2)}, u32[]{:S(2)}) collective-permute-start(bf16[2,1024,512]{2,1,0:T(8,128)(2,1)} %convert_element_type.293), channel_id=1, source_target_pairs={{0,0},{1,16},{2,2},{3,18},{4,4},{5,20},{6,6},{7,22},{8,8},{9,24},{... | collective-permute-start | bytes 6291464 | tf_op jit(solution)/shard_map/ppermute | solution.py:621
  714.5 6.2 select_bitcast_fusion
  720.7 50.8 %reduce-scatter.17.cloned.1.call-done = bf16[64,3072]{1,0:T(8,128)(2,1)} async-done(((bf16[1024,3072]{1,0:T(8,128)(2,1)}), bf16[64,3072]{1,0:T(8,128)(2,1)}) %reduce-scatter.17.cloned.1.call-update) | async-done | bytes 393232 | tf_op jit(solution)/shard_map/reduce_scatter | solution.py:728
  771.5 75.4 %reduce-scatter.23.cloned.1.call-done = bf16[256,1024]{1,0:T(8,128)(2,1)} async-done(((bf16[4096,1024]{1,0:T(8,128)(2,1)}), bf16[256,1024]{1,0:T(8,128)(2,1)}) %reduce-scatter.23.cloned.1.call-update) | async-done | bytes 524304 | tf_op jit(solution)/shard_map/reduce_scatter | solution.py:737
  846.8 75.4 %reduce-scatter.21.cloned.1.call-done = bf16[64,4096]{1,0:T(8,128)(2,1)} async-done(((bf16[1024,4096]{1,0:T(8,128)(2,1)}), bf16[64,4096]{1,0:T(8,128)(2,1)}) %reduce-scatter.21.cloned.1.call-update) | async-done | bytes 524304 | tf_op jit(solution)/shard_map/reduce_scatter | solution.py:734
  922.3 5.8 select_bitcast_fusion.1
  929.1 55.9 %reduce-scatter.29.cloned.1.call-done = bf16[64,2]{1,0:T(8,128)(2,1)} async-done(((bf16[1024,2]{1,0:T(8,128)(2,1)}), bf16[64,2]{1,0:T(8,128)(2,1)}) %reduce-scatter.29.cloned.1.call-update) | async-done | bytes 272
  985.8 60.7 %reduce-scatter.31.cloned.1.call-done = bf16[64,2]{1,0:T(8,128)(2,1)} async-done(((bf16[1024,2]{1,0:T(8,128)(2,1)}), bf16[64,2]{1,0:T(8,128)(2,1)}) %reduce-scatter.31.cloned.1.call-update) | async-done | bytes 272
  1047.3 43.2 %all-reduce.1 = (bf16[2,64]{1,0:T(2,128)(2,1)S(1)}, bf16[2,64]{1,0:T(2,128)(2,1)S(1)}, bf16[2,5,1024]{2,1,0:T(8,128)(2,1)S(1)}) all-reduce(bf16[2,64]{1,0:T(2,128)(2,1)S(1)} %copy.46, bf16[2,64]{1,0:T(2,128)(2,1)S(1)} %copy.48, bf16[2,5,1024]{2,1,0:T(8,128)(2,1)S(1)} %pad_maximum_fusion.1), channel_id=1, replica_groups=mesh['seq'=8,'fsdp'=16] {'seq'}, use_global_device_ids=true, to_apply=%region_16.17 | all-reduce | flops 10496 | bytes 41984 | tf_op jit(solution)/shard_map/psum | solution.py:742
  1092.9 59.9 %all-reduce.5.cloned.1.call-done = (bf16[64,3072]{1,0:T(8,128)(2,1)}, bf16[64,1024]{1,0:T(8,128)(2,1)}, bf16[64,4096]{1,0:T(8,128)(2,1)}, bf16[256,1024]{1,0:T(8,128)(2,1)}) async-done(((bf16[64,3072]{1,0:T(8,128)(2,1)}, bf16[64,1024]{1,0:T(8,128)(2,1)}, bf16[64,4096]{1,0:T(8,128)(2,1)}, bf16[256,1024]{1,0:T(8,128)(2,1)}), (bf16[64,3072]{1,0:T(8,128)(2,1)}, bf16[64,1024]{1,0:T(8,128)(2,1)}, ...) | async-done | bytes 1572880 | tf_op jit(solution)/shard_map/psum | solution.py:744
  (166 shorter events, 114.8 us)
Async XLA Ops:
  7.2 46.8 %all-gather.11.cloned.1.call-start = ((), (), s32[]{:S(2)}) async-start(), calls=%async_computation.8 | async-start | bytes 6684672 | tf_op jit(solution)/shard_map/all_gather | solution.py:548
  7.9 119.8 %all-gather.21.cloned.1.call-start = ((), (), s32[]{:S(2)}) async-start(), calls=%async_computation.17 | async-start | bytes 2359296 | tf_op jit(solution)/shard_map/all_gather | solution.py:563
  58.0 38.2 %copy-start.18 = (bf16[1,1024]{1,0:T(2,128)(2,1)S(1)}, bf16[1,1024]{1,0:T(2,128)(2,1)}, u32[]{:S(2)}) copy-start(bf16[1,1024]{1,0:T(2,128)(2,1)} %param.28) | copy-start | bytes 6148
  58.0 38.2 %copy-start.19 = (bf16[1,2,1024]{2,1,0:T(2,128)(2,1)S(1)}, bf16[1,2,1024]{2,1,0:T(2,128)(2,1)}, u32[]{:S(2)}) copy-start(bf16[1,2,1024]{2,1,0:T(2,128)(2,1)} %param.25) | copy-start | bytes 12292
  58.0 38.2 %copy-start.20 = (bf16[1,2,1024]{2,1,0:T(2,128)(2,1)S(1)}, bf16[1,2,1024]{2,1,0:T(2,128)(2,1)}, u32[]{:S(2)}) copy-start(bf16[1,2,1024]{2,1,0:T(2,128)(2,1)} %param.24) | copy-start | bytes 12292
  58.0 38.3 %copy-start.21 = (s32[1,2]{1,0:T(1,128)S(1)}, s32[1,2]{1,0:T(1,128)}, u32[]{:S(2)}) copy-start(s32[1,2]{1,0:T(1,128)} %param.16) | copy-start | bytes 28
  59.2 71.7 %copy-start.11 = (bf16[1,128,1,1024]{1,3,2,0:T(8,128)(2,1)}, bf16[1,128,1,1024]{1,3,2,0:T(8,128)(2,1)S(1)}, u32[]{:S(2)}) copy-start(bf16[1,128,1,1024]{1,3,2,0:T(8,128)(2,1)S(1)} %get-tuple-element.40) | copy-start | bytes 786436
  59.2 118.7 %all-gather.19.cloned.1.call-start = ((), (), s32[]{:S(2)}) async-start(), calls=%async_computation.16 | async-start | bytes 2359296 | tf_op jit(solution)/shard_map/all_gather | solution.py:564
  60.0 150.4 %all-gather.13.cloned.1.call-start = ((), (), s32[]{:S(2)}) async-start(), calls=%async_computation.9 | async-start | bytes 2228224 | tf_op jit(solution)/shard_map/all_gather | solution.py:549
  60.6 204.1 %all-gather.15.cloned.1.call-start = ((), (), s32[]{:S(2)}) async-start(), calls=%async_computation.10 | async-start | bytes 8912896 | tf_op jit(solution)/shard_map/all_gather | solution.py:550
  61.2 258.0 %all-gather.17.cloned.1.call-start = ((), (), s32[]{:S(2)}) async-start(), calls=%async_computation.11 | async-start | bytes 8912896 | tf_op jit(solution)/shard_map/all_gather | solution.py:551
  61.7 501.9 %reduce-scatter.27.cloned.1.call-start = ((), (), s32[]{:S(2)}) async-start(), calls=%async_computation.19 | async-start | bytes 2359296
  61.8 38.6 %collective-permute-start.1 = (bf16[2,1024,512]{2,1,0:T(8,128)(2,1)}, bf16[2,1024,512]{2,1,0:T(8,128)(2,1)}, u32[]{:S(2)}, u32[]{:S(2)}) collective-permute-start(bf16[2,1024,512]{2,1,0:T(8,128)(2,1)} %bitcast.199), channel_id=1, source_target_pairs={{0,0},{1,16},{2,2},{3,18},{4,4},{5,20},{6,6},{7,22},{8,8},{9,24},{... | collective-permute-start | bytes 6291464 | tf_op jit(solution)/shard_map/ppermute | solution.py:608
  79.0 21.9 %collective-permute-start.3 = (bf16[2,512,1024]{2,1,0:T(8,128)(2,1)}, bf16[2,512,1024]{2,1,0:T(8,128)(2,1)}, u32[]{:S(2)}, u32[]{:S(2)}) collective-permute-start(bf16[2,512,1024]{2,1,0:T(8,128)(2,1)} %bitcast.200), channel_id=1, source_target_pairs={{0,0},{1,16},{2,2},{3,18},{4,4},{5,20},{6,6},{7,22},{8,8},{9,24},{... | collective-permute-start | bytes 6291464 | tf_op jit(solution)/shard_map/ppermute | solution.py:609
  96.2 3.5 collective-permute-start
  100.4 224.5 %collective-permute-start.2 = (bf16[2,1024,512]{2,1,0:T(8,128)(2,1)}, bf16[2,1024,512]{2,1,0:T(8,128)(2,1)}, u32[]{:S(2)}, u32[]{:S(2)}) collective-permute-start(bf16[2,1024,512]{2,1,0:T(8,128)(2,1)} %collective-permute-done.1.in_a), channel_id=1, source_target_pairs={{0,1},{1,0},{2,3},{3,2},{4,5},{5,4},{6,7},{7,6},{8,9},{9,8},{10,11... | collective-permute-start | bytes 6291464 | tf_op jit(solution)/shard_map/ppermute | solution.py:610
  100.8 224.0 %collective-permute-start.4 = (bf16[2,512,1024]{2,1,0:T(8,128)(2,1)}, bf16[2,512,1024]{2,1,0:T(8,128)(2,1)}, u32[]{:S(2)}, u32[]{:S(2)}) collective-permute-start(bf16[2,512,1024]{2,1,0:T(8,128)(2,1)} %collective-permute-done.3.out_a), channel_id=1, source_target_pairs={{0,1},{1,0},{2,3},{3,2},{4,5},{5,4},{6,7},{7,6},{8,9},{9,8},{10,11... | collective-permute-start | bytes 6291464 | tf_op jit(solution)/shard_map/ppermute | solution.py:611
  177.9 32.4 %copy-start.2 = (bf16[1,128,1024]{2,1,0:T(8,128)(2,1)S(1)}, bf16[1,128,1024]{2,1,0:T(8,128)(2,1)}, u32[]{:S(2)}) copy-start(bf16[1,128,1024]{2,1,0:T(8,128)(2,1)} %param.15) | copy-start | bytes 786436
  183.8 80.8 %copy-start.14 = (bf16[16,64,128]{2,1,0:T(8,128)(2,1)}, bf16[16,64,128]{2,1,0:T(8,128)(2,1)S(1)}, u32[]{:S(2)}) copy-start(bf16[16,64,128]{2,1,0:T(8,128)(2,1)S(1)} %fusion.17) | copy-start | bytes 786436
  488.2 153.0 %reduce-scatter.25.cloned.1.call-start = ((), (), s32[]{:S(2)}) async-start(), calls=%async_computation.18 | async-start | bytes 2359296
  517.2 203.5 %reduce-scatter.19.cloned.1.call-start = ((), (), s32[]{:S(2)}) async-start(), calls=%async_computation.13 | async-start | bytes 2228224 | tf_op jit(solution)/shard_map/reduce_scatter | solution.py:731
  520.4 251.1 %reduce-scatter.17.cloned.1.call-start = ((), (), s32[]{:S(2)}) async-start(), calls=%async_computation.12 | async-start | bytes 6684672 | tf_op jit(solution)/shard_map/reduce_scatter | solution.py:728
  651.9 194.9 %reduce-scatter.23.cloned.1.call-start = ((), (), s32[]{:S(2)}) async-start(), calls=%async_computation.15 | async-start | bytes 8912896 | tf_op jit(solution)/shard_map/reduce_scatter | solution.py:737
  658.8 263.4 %reduce-scatter.21.cloned.1.call-start = ((), (), s32[]{:S(2)}) async-start(), calls=%async_computation.14 | async-start | bytes 8912896 | tf_op jit(solution)/shard_map/reduce_scatter | solution.py:734
  665.7 319.2 %reduce-scatter.29.cloned.1.call-start = ((), (), s32[]{:S(2)}) async-start(), calls=%async_computation.20 | async-start | bytes 278528
  665.8 21.2 %copy-start.3 = (f32[2,1024,512]{2,1,0:T(8,128)S(1)}, f32[2,1024,512]{2,1,0:T(8,128)}, u32[]{:S(2)}) copy-start(f32[2,1024,512]{2,1,0:T(8,128)} %get-tuple-element.21) | copy-start | bytes 12582916
  669.8 44.7 %collective-permute-start.7 = (bf16[2,512,1024]{2,1,0:T(8,128)(2,1)}, bf16[2,512,1024]{2,1,0:T(8,128)(2,1)}, u32[]{:S(2)}, u32[]{:S(2)}) collective-permute-start(bf16[2,512,1024]{2,1,0:T(8,128)(2,1)} %convert_element_type.295), channel_id=1, source_target_pairs={{0,0},{1,16},{2,2},{3,18},{4,4},{5,20},{6,6},{7,22},{8,8},{9,24},{... | collective-permute-start | bytes 6291464 | tf_op jit(solution)/shard_map/ppermute | solution.py:624
  687.0 20.1 %copy-start.6 = (bf16[1,128,3,1024]{1,3,2,0:T(8,128)(2,1)S(1)}, bf16[1,128,3,1024]{1,3,2,0:T(8,128)(2,1)}, u32[]{:S(2)}) copy-start(bf16[1,128,3,1024]{1,3,2,0:T(8,128)(2,1)} %copy-done.5) | copy-start | bytes 2359300
  688.6 233.7 %collective-permute-start.6 = (bf16[2,1024,512]{2,1,0:T(8,128)(2,1)}, bf16[2,1024,512]{2,1,0:T(8,128)(2,1)}, u32[]{:S(2)}, u32[]{:S(2)}) collective-permute-start(bf16[2,1024,512]{2,1,0:T(8,128)(2,1)} %convert_element_type.293), channel_id=1, source_target_pairs={{0,0},{1,16},{2,2},{3,18},{4,4},{5,20},{6,6},{7,22},{8,8},{9,24},{... | collective-permute-start | bytes 6291464 | tf_op jit(solution)/shard_map/ppermute | solution.py:621
  705.8 1.3 collective-permute-start.5
  713.5 333.1 %reduce-scatter.31.cloned.1.call-start = ((), (), s32[]{:S(2)}) async-start(), calls=%async_computation.21 | async-start | bytes 278528
  714.5 438.4 %all-reduce.5.cloned.1.call-start = ((), (), s32[]{:S(2)}) async-start(), calls=%async_computation.22 | async-start | bytes 3145728 | tf_op jit(solution)/shard_map/psum | solution.py:744
  (13 other events, 64.4 us)
Sparse Core Ops, SparseCore 0:
  9.7 44.2 all-gather.10
  59.4 63.3 all-gather.20
  125.6 52.3 all-gather.18
  179.5 30.8 all-gather.12
  211.9 52.6 all-gather.14
  266.2 52.9 all-gather.16
  488.4 75.2 reduce-scatter.26
  567.3 73.8 reduce-scatter.24
  643.6 55.3 reduce-scatter.18
  701.3 70.1 reduce-scatter.16
  773.9 72.9 reduce-scatter.22
  849.1 73.1 reduce-scatter.20
  925.2 59.7 reduce-scatter.28
  987.9 58.6 reduce-scatter.30
  1049.2 103.6 all-reduce.4

commit v2 on v1

v2 whole, which is shorter than its diff:
```python
import jax
import jax.numpy as jnp
from jax import lax
from jax.experimental import pallas as pl
from jax.experimental.pallas import tpu as pltpu
from jax.sharding import PartitionSpec as P

MESH = pl.DeviceIdType.MESH
epsilon = 1e-05
masked_score = -1e30


def split_sum(values):
    return jnp.sum(values, axis=-1, keepdims=True)


def norm_parts(values):
    average = split_sum(values) * (1.0 / values.shape[-1])
    centered = values - average
    spread = split_sum(centered * centered) * (1.0 / values.shape[-1])
    scale = lax.rsqrt(spread + epsilon)
    return centered * scale, scale


def norm_back(grad_normed, gain, xhat, scale):
    width = 1.0 / xhat.shape[-1]
    u = grad_normed * gain
    return scale * (u - split_sum(u) * width - xhat * (split_sum(u * xhat) * width))


def gelu_parts(pre):
    inner = 0.7978845608028654
    cubic = 0.044715
    square = pre * pre
    t = jnp.tanh(inner * pre * (1.0 + cubic * square))
    half = 0.5 * (1.0 + t)
    slope = half + 0.5 * pre * (1.0 - t * t) * (inner * (1.0 + 3.0 * cubic * square))
    return pre * half, slope


def nn(a, b):
    return lax.dot_general(a, b, (((1,), (0,)), ((), ())), preferred_element_type=jnp.float32)


def nt(a, b):
    return lax.dot_general(a, b, (((1,), (1,)), ((), ())), preferred_element_type=jnp.float32)


def tn(a, b):
    return lax.dot_general(a, b, (((0,), (0,)), ((), ())), preferred_element_type=jnp.float32)


def place():
    s, f = lax.axis_index("seq"), lax.axis_index("fsdp")
    return lax.div(s, 2), lax.rem(s, 2), f, lax.rem(f, 2)


def block(index):
    return pl.ds(pl.multiple_of(index * 128, 128), 128)


def order(i):
    return i + lax.div(i, 2) - 2 * lax.div(i, 3)


class Line:
    def __init__(self, send, recv):
        self.z, self.yh, self.f, self.c = place()
        self.send, self.recv = send, recv

    def index(self, d):
        return lax.rem(self.z + d, 4)

    def copy(self, phase, d, src, dst):
        return pltpu.make_async_remote_copy(
            src_ref=src,
            dst_ref=dst,
            send_sem=self.send.at[phase, d - 1],
            recv_sem=self.recv.at[phase, d - 1],
            device_id=(2 * self.index(d) + self.yh, self.f),
            device_id_type=MESH,
        )

    def spread(self, phase, buf):
        for d in (1, 3, 2):
            self.copy(phase, d, buf.at[block(self.z)], buf.at[block(self.z)]).start()

    def arrived(self, phase, d, buf):
        dst = buf.at[block(self.index(d))]
        pltpu.make_async_remote_copy(
            src_ref=dst,
            dst_ref=dst,
            send_sem=self.send.at[phase, 3 - d],
            recv_sem=self.recv.at[phase, 3 - d],
            device_id=(2 * self.index(d) + self.yh, self.f),
            device_id_type=MESH,
        ).wait_recv()

    def give(self, phase, d, src, dst):
        self.copy(phase, d, src.at[block(self.index(d))], dst.at[block(self.z)]).start()

    def sent(self, phase, buf):
        for d in (1, 3, 2):
            self.copy(phase, d, buf.at[block(self.z)], buf.at[block(self.z)]).wait_send()

    def total(self, phase, own, parts):
        acc = own[block(self.z), :].astype(jnp.float32)
        for d in (1, 3, 2):
            self.arrived(phase, d, parts)
            acc += parts[block(self.index(d)), :].astype(jnp.float32)
        return acc


class Columns:
    def __init__(self, send, recv):
        self.z, self.yh, self.f, self.c = place()
        self.m = self.f - self.c + self.yh
        self.send, self.recv = send, recv

    def device(self, q):
        return (2 * self.z + lax.rem(q, 2), q - lax.rem(q, 2) + self.c)

    def piece(self, q):
        return pl.ds(pl.multiple_of(q * 16, 16), 16)

    def copy(self, phase, d, src, dst):
        q = lax.rem(self.m + d, 16)
        return pltpu.make_async_remote_copy(
            src_ref=src.at[self.piece(q)],
            dst_ref=dst.at[self.piece(self.m)],
            send_sem=self.send.at[phase, d - 1],
            recv_sem=self.recv.at[phase, d - 1],
            device_id=self.device(q),
            device_id_type=MESH,
        )

    def start(self, phase, src, dst):
        def one(i, carry):
            self.copy(phase, i + 1, src, dst).start()
            return carry

        lax.fori_loop(0, 15, one, 0)
        dst[self.piece(self.m), :] = src[self.piece(self.m), :]

    def wait(self, phase, src, dst):
        def one(i, carry):
            q = lax.rem(self.m + 15 - i, 16)
            pltpu.make_async_remote_copy(
                src_ref=dst.at[self.piece(q)],
                dst_ref=dst.at[self.piece(q)],
                send_sem=self.send.at[phase, i],
                recv_sem=self.recv.at[phase, i],
                device_id=self.device(q),
                device_id_type=MESH,
            ).wait_recv()
            return carry

        lax.fori_loop(0, 15, one, 0)

    def sent(self, phase, src, dst):
        def one(i, carry):
            self.copy(phase, i + 1, src, dst).wait_send()
            return carry

        lax.fori_loop(0, 15, one, 0)


def placings(route):
    row = lax.broadcasted_iota(jnp.int32, (256, 128), 0)
    inner = row & 15
    slot = (row >> 4) * 8 + (inner & 7)
    hit = slot == route
    left = jnp.where(hit & (inner < 8), 1.0, 0.0).astype(jnp.bfloat16)
    right = jnp.where(hit & (inner >= 8), 1.0, 0.0).astype(jnp.bfloat16)
    return left, right


def to_pieces(left, right, rows):
    half = rows.shape[1] // 2
    return (nn(left, rows[:, :half]) + nn(right, rows[:, half:])).astype(jnp.bfloat16)


def from_pieces(left, right, pieces):
    return jnp.concatenate([tn(left, pieces), tn(right, pieces)], axis=1).astype(jnp.bfloat16)


def rows_of(pieces):
    wide = pieces.astype(jnp.float32).reshape(16, 2, 8, 512)
    return jnp.concatenate([wide[:, 0].reshape(128, 512), wide[:, 1].reshape(128, 512)], axis=1)


def pieces_of(rows):
    left = rows[:, :512].reshape(16, 1, 8, 512)
    right = rows[:, 512:].reshape(16, 1, 8, 512)
    return jnp.concatenate([left, right], axis=1).reshape(256, 512).astype(jnp.bfloat16)


def expert_kernel(
    hid, cot, route, vec, exp_in, exp_out, in_a, out_a,
    res, gh, vecg, gin, gout,
    w_in, w_out, sendh, sendc, sendr, sendg, arrh, arrc, arrr, arrg,
    e0, e1, g0, g1, ps0, ps1, pr0, pr1, pb0, pb1,
    act0, act1, dg0, dg1, gp0, gp1,
    arrived, cota, base, xh0, xh1, sc,
    ga_in, ga_out, sb_in, sb_out, rb_in, rb_out, vmine, vcore, vline, vsum, vswap,
    wsem, zs, zr, cs, cr, ks, kr, osem, bs, br, ss, sr, vs, vr,
):
    line, cols = Line(zs, zr), Columns(cs, cr)
    z, yh, f, c = place()
    other = (lax.axis_index("seq"), f + 1 - 2 * c)
    swap_mate = (2 * z + 1 - yh, f + 1 - 2 * c)
    bar = pltpu.get_barrier_semaphore()

    def meet(i, carry):
        greet(bar, cols.device(lax.rem(cols.m + i + 1, 16)))
        return carry

    lax.fori_loop(0, 15, meet, 0)
    for d in (1, 2, 3):
        greet(bar, (2 * line.index(d) + yh, f))
    greet(bar, other)
    greet(bar, swap_mate)
    same = c == yh

    def slot(k, i, half):
        return w_in.at[k, :, half] if i == 0 else w_out.at[k, half, :]

    low, high = slice(0, 512), slice(512, 1024)

    def load(k, i):
        src = (exp_in, exp_out)[i].at[k]
        return pltpu.make_async_copy(src, slot(k, i, low), wsem.at[k, i])

    def swapped(i):
        return pltpu.make_async_copy((in_a, out_a)[i], slot(0, i, low), wsem.at[0, i])

    def swap_in(i):
        return remote((exp_in, exp_out)[i].at[1], slot(1, i, low), ss.at[i], sr.at[i], swap_mate)

    def share(k, i):
        return remote(slot(k, i, low), slot(k, i, high), bs.at[k, i], br.at[k, i], other)

    @pl.when(same)
    def _():
        for i in range(2):
            load(0, i).start()
            load(1, i).start()

    @pl.when(jnp.logical_not(same))
    def _():
        for i in range(2):
            swapped(i).start()

    left, right = placings(route[0:1, :])
    sendh[...] = to_pieces(left, right, hid[...])
    sendc[...] = to_pieces(left, right, cot[...])
    pl.semaphore_wait(bar, 20)
    cols.start(0, sendh, arrh)

    @pl.when(same)
    def _():
        for i in range(2):
            load(0, i).wait()

    @pl.when(jnp.logical_not(same))
    def _():
        for i in range(2):
            swapped(i).wait()

    for i in range(2):
        share(0, i).start()
    cols.start(1, sendc, arrc)

    @pl.when(jnp.logical_not(same))
    def _():
        for i in range(2):
            swap_in(i).start()

    cols.wait(0, sendh, arrh)
    gain = [vec[0:1, :], vec[1:2, :]]
    bias = [vec[2:3, :], vec[3:4, :]]
    rows = rows_of(arrh[...])
    arrived[...] = rows
    xhat, scale = norm_parts(rows)
    xh0[...] = xhat
    sc[0] = jnp.broadcast_to(scale, (128, 128))
    e0[block(z), :] = (xhat * gain[0] + bias[0]).astype(jnp.bfloat16)
    line.spread(0, e0)
    cols.wait(1, sendc, arrc)
    coti = rows_of(arrc[...])
    cota[...] = coti
    gating = jax.nn.sigmoid(split_sum(arrived[...] * vec[4:5, :]))
    sc[2] = jnp.broadcast_to(gating, (128, 128))
    g1[block(z), :] = (gating * coti).astype(jnp.bfloat16)
    line.spread(3, g1)
    for i in range(2):
        share(0, i).wait_recv()

    def forward(k, j, rows_in, act, dg):
        values = rows_in[block(j), :]
        for n in range(4):
            tile = slice(n * 256, (n + 1) * 256)
            pre = nn(values, w_in[k, :, tile])
            acted, slope = gelu_parts(pre)
            act[block(j), tile] = acted.astype(jnp.bfloat16)
            dg[block(j), tile] = slope

    def project(k, j, act, part):
        values = act[block(j), :]
        for n in range(4):
            tile = slice(n * 256, (n + 1) * 256)
            part[block(j), tile] = nn(values, w_out[k, :, tile]).astype(jnp.bfloat16)

    def backward(k, j, grad, dg, gp, part):
        values = grad[block(j), :]
        for n in range(4):
            tile = slice(n * 256, (n + 1) * 256)
            slope = dg[block(j), tile] * nt(values, w_out[k, tile, :])
            gp[block(j), tile] = slope.astype(jnp.bfloat16)
        pres = gp[block(j), :]
        for n in range(4):
            tile = slice(n * 256, (n + 1) * 256)
            part[block(j), tile] = nt(pres, w_in[k, tile, :]).astype(jnp.bfloat16)

    def sub0(i, carry):
        d = order(i)
        j = line.index(d)

        @pl.when(i > 0)
        def _():
            line.arrived(0, d, e0)

        forward(0, j, e0, act0, dg0)
        project(0, j, act0, ps0)

        @pl.when(i > 0)
        def _():
            line.give(1, d, ps0, pr0)

        return carry

    lax.fori_loop(0, 4, sub0, 0)

    @pl.when(same)
    def _():
        for i in range(2):
            load(1, i).wait()

    @pl.when(jnp.logical_not(same))
    def _():
        for i in range(2):
            swap_in(i).wait()

    for i in range(2):
        share(1, i).start()
    stream = arrived[...] + line.total(1, ps0, pr0)
    base[...] = stream
    xhat, scale = norm_parts(stream)
    xh1[...] = xhat
    sc[1] = jnp.broadcast_to(scale, (128, 128))
    e1[block(z), :] = (xhat * gain[1] + bias[1]).astype(jnp.bfloat16)
    line.spread(2, e1)
    line.sent(1, ps0)
    for i in range(2):
        share(1, i).wait_recv()

    def sub1(i, carry):
        d = order(i)
        j = line.index(d)

        @pl.when(i > 0)
        def _():
            line.arrived(2, d, e1)
            line.arrived(3, d, g1)

        forward(1, j, e1, act1, dg1)
        backward(1, j, g1, dg1, gp1, ps0)

        @pl.when(i > 0)
        def _():
            line.give(4, d, ps0, pb1)

        project(1, j, act1, ps1)

        @pl.when(i > 0)
        def _():
            line.give(5, d, ps1, pr1)

        return carry

    lax.fori_loop(0, 4, sub1, 0)

    def weight_grads(k, rows_in, gp, act, grad):
        def one(n, carry):
            tile = pl.ds(pl.multiple_of(n * 256, 256), 256)
            tile_b = pl.ds(pl.multiple_of(n * 256 + 512, 256), 256)
            ga_out[k, tile, :] = tn(act[:, tile], grad[...])
            sb_out[k, tile, :] = tn(act[:, tile_b], grad[...]).astype(jnp.bfloat16)
            return carry

        lax.fori_loop(0, 2, one, 0)

        def two(n, carry):
            tile = pl.ds(pl.multiple_of(n * 256, 256), 256)
            ga_in[k, tile, :] = tn(rows_in[:, tile], gp[:, 0:512])
            sb_in[k, tile, :] = tn(rows_in[:, tile], gp[:, 512:1024]).astype(jnp.bfloat16)
            return carry

        lax.fori_loop(0, 4, two, 0)

    def swap(k, i, src, dst):
        return pltpu.make_async_remote_copy(
            src_ref=src.at[k],
            dst_ref=dst.at[k],
            send_sem=ks.at[k, i],
            recv_sem=kr.at[k, i],
            device_id=other,
            device_id_type=MESH,
        )

    weight_grads(1, e1, gp1, act1, g1)
    swap(1, 0, sb_in, rb_in).start()
    swap(1, 1, sb_out, rb_out).start()
    grad_normed = line.total(4, ps0, pb1)
    grad_stream = sc[2][:, 0:1] * cota[...]
    grad_stream += norm_back(grad_normed, gain[1], xh1[...], sc[1][:, 0:1])
    g0[block(z), :] = grad_stream.astype(jnp.bfloat16)
    line.spread(6, g0)
    vmine[1:2, :] = jnp.sum(grad_normed * xh1[...], axis=0, keepdims=True)
    vmine[3:4, :] = jnp.sum(grad_normed, axis=0, keepdims=True)
    line.sent(4, ps0)
    stream = base[...] + line.total(5, ps1, pr1)
    base[...] = grad_stream
    gate = sc[2][:, 0:1]
    diff = stream - arrived[...]
    sendr[...] = pieces_of(arrived[...] + gate * diff)
    grad_gating = split_sum(cota[...] * diff)
    grad_logit = gate * (1.0 - gate) * grad_gating
    vmine[4:5, :] = jnp.sum(grad_logit * arrived[...], axis=0, keepdims=True)
    sc[3] = jnp.broadcast_to(grad_logit, (128, 128))

    def sub0_back(i, carry):
        d = order(i)
        j = line.index(d)

        @pl.when(i > 0)
        def _():
            line.arrived(6, d, g0)

        backward(0, j, g0, dg0, gp0, ps0)

        @pl.when(i > 0)
        def _():
            line.give(7, d, ps0, pb0)

        return carry

    lax.fori_loop(0, 4, sub0_back, 0)
    cols.start(2, sendr, arrr)
    weight_grads(0, e0, gp0, act0, g0)
    swap(0, 0, sb_in, rb_in).start()
    swap(0, 1, sb_out, rb_out).start()
    grad_normed = line.total(7, ps0, pb0)
    vmine[0:1, :] = jnp.sum(grad_normed * xh0[...], axis=0, keepdims=True)
    vmine[2:3, :] = jnp.sum(grad_normed, axis=0, keepdims=True)
    grad_stream = base[...] + norm_back(grad_normed, gain[0], xh0[...], sc[0][:, 0:1])
    grad_stream += (1.0 - sc[2][:, 0:1]) * cota[...] + sc[3][:, 0:1] * vec[4:5, :]
    sendg[...] = pieces_of(grad_stream)
    cols.start(3, sendg, arrg)
    vmine[5:8, :] = jnp.zeros((3, 1024), jnp.float32)
    give_core = remote(vmine, vcore, vs.at[0], vr.at[0], other)
    give_core.start()
    give_core.wait_recv()
    vline[z] = vmine[...] + vcore[...]

    def give_line(d, at):
        return remote(vline.at[at], vline.at[at], vs.at[4 - d], vr.at[4 - d], (2 * line.index(4 - d) + yh, f))

    for d in (1, 2, 3):
        give_line(d, z).start()
    cols.wait(3, sendg, arrg)
    left, right = placings(route[0:1, :])
    gh[...] = from_pieces(left, right, arrg[...])
    for d in (1, 2, 3):
        give_line(d, line.index(d)).wait_recv()
    vsum[...] = vline[0] + vline[1] + vline[2] + vline[3]
    give_mate = remote(vsum, vswap, vs.at[4], vr.at[4], swap_mate)

    @pl.when(jnp.logical_not(same))
    def _():
        give_mate.start()

    cols.wait(2, sendr, arrr)
    res[...] = from_pieces(left, right, arrr[...])
    for k in (0, 1):
        swap(k, 0, sb_in, rb_in).wait()
        swap(k, 1, sb_out, rb_out).wait()
    stores = []
    for k in (1, 0):
        sb_in[k] = (ga_in[k] + rb_in[k].astype(jnp.float32)).astype(jnp.bfloat16)
        sb_out[k] = (ga_out[k] + rb_out[k].astype(jnp.float32)).astype(jnp.bfloat16)
        stores += [
            pltpu.make_async_copy(sb_in.at[k], gin.at[k], osem.at[k, 0]),
            pltpu.make_async_copy(sb_out.at[k], gout.at[k], osem.at[k, 1]),
        ]
        stores[-1].start()
        stores[-2].start()

    @pl.when(same)
    def _():
        vecg[...] = vsum[...]

    @pl.when(jnp.logical_not(same))
    def _():
        give_mate.wait()
        vecg[...] = vswap[...]

    give_core.wait_send()
    for d in (1, 2, 3):
        give_line(d, z).wait_send()
    for k in (0, 1):
        for i in range(2):
            share(k, i).wait_send()
    line.sent(0, e0)
    line.sent(2, e1)
    line.sent(3, g1)
    line.sent(5, ps1)
    line.sent(6, g0)
    line.sent(7, ps0)
    cols.sent(0, sendh, arrh)
    cols.sent(1, sendc, arrc)
    cols.sent(2, sendr, arrr)
    cols.sent(3, sendg, arrg)
    for store in stores:
        store.wait()


def expert_call(hid, cot, route, vec, exp_in, exp_out, in_a, out_a):
    bf, f32 = jnp.bfloat16, jnp.float32
    vmem, anywhere = pl.BlockSpec(memory_space=pltpu.VMEM), pl.BlockSpec(memory_space=pl.ANY)
    line = [pltpu.VMEM((512, 1024), bf)]
    rows = [pltpu.VMEM((128, 1024), f32)]
    piece = [pltpu.VMEM((256, 512), bf)]
    wide = [pltpu.VMEM((512, 1024), f32)]
    return pl.pallas_call(
        expert_kernel,
        out_shape=(
            jax.ShapeDtypeStruct((128, 1024), bf),
            jax.ShapeDtypeStruct((128, 1024), bf),
            jax.ShapeDtypeStruct((8, 1024), f32),
            jax.ShapeDtypeStruct((2, 1024, 512), bf),
            jax.ShapeDtypeStruct((2, 512, 1024), bf),
        ),
        in_specs=[vmem] * 4 + [anywhere] * 4,
        out_specs=(vmem, vmem, vmem, anywhere, anywhere),
        scratch_shapes=[
            pltpu.VMEM((2, 1024, 1024), bf),
            pltpu.VMEM((2, 1024, 1024), bf),
            *(piece * 8),
            *(line * 10),
            *(line * 2),
            *(wide * 2),
            *(line * 2),
            *(rows * 5),
            pltpu.VMEM((4, 128, 128), f32),
            pltpu.VMEM((2, 1024, 512), f32),
            pltpu.VMEM((2, 512, 1024), f32),
            pltpu.VMEM((2, 1024, 512), bf),
            pltpu.VMEM((2, 512, 1024), bf),
            pltpu.VMEM((2, 1024, 512), bf),
            pltpu.VMEM((2, 512, 1024), bf),
            pltpu.VMEM((8, 1024), f32),
            pltpu.VMEM((8, 1024), f32),
            pltpu.VMEM((4, 8, 1024), f32),
            pltpu.VMEM((8, 1024), f32),
            pltpu.VMEM((8, 1024), f32),
            pltpu.SemaphoreType.DMA((2, 2)),
            pltpu.SemaphoreType.DMA((8, 3)),
            pltpu.SemaphoreType.DMA((8, 3)),
            pltpu.SemaphoreType.DMA((4, 15)),
            pltpu.SemaphoreType.DMA((4, 15)),
            pltpu.SemaphoreType.DMA((2, 2)),
            pltpu.SemaphoreType.DMA((2, 2)),
            pltpu.SemaphoreType.DMA((2, 2)),
            pltpu.SemaphoreType.DMA((2, 2)),
            pltpu.SemaphoreType.DMA((2, 2)),
            pltpu.SemaphoreType.DMA((2,)),
            pltpu.SemaphoreType.DMA((2,)),
            pltpu.SemaphoreType.DMA((5,)),
            pltpu.SemaphoreType.DMA((5,)),
        ],
        compiler_params=pltpu.CompilerParams(
            collective_id=1, has_side_effects=True, vmem_limit_bytes=60 << 20
        ),
        name="experts",
    )(hid, cot, route, vec, exp_in, exp_out, in_a, out_a)


def remote(src, dst, send, recv, device):
    return pltpu.make_async_remote_copy(
        src_ref=src, dst_ref=dst, send_sem=send, recv_sem=recv, device_id=device, device_id_type=MESH
    )


def greet(bar, device):
    pl.semaphore_signal(bar, inc=1, device_id=device, device_id_type=MESH)


class Owners:
    def __init__(self, send, recv, core_send, core_recv):
        self.s, self.f = lax.axis_index("seq"), lax.axis_index("fsdp")
        self.c, self.col = lax.rem(self.f, 2), lax.div(self.f, 2)
        self.send, self.recv = send, recv
        self.core_send, self.core_recv = core_send, core_recv

    def device(self, col):
        return (self.s, 2 * col + self.c)

    def copy(self, phase, i, src, dst):
        return remote(
            src, dst, self.send.at[phase, i], self.recv.at[phase, i], self.device(lax.rem(self.col + i + 1, 8))
        )

    def start(self, phase, src, full):
        def one(i, carry):
            self.copy(phase, i, src, full.at[self.col, self.c]).start()
            return carry

        lax.fori_loop(0, 7, one, 0)

    def wait(self, phase, full):
        def one(i, carry):
            q = lax.rem(self.col + 7 - i, 8)
            dst = full.at[q, self.c]
            remote(dst, dst, self.send.at[phase, i], self.recv.at[phase, i], self.device(q)).wait_recv()
            return carry

        lax.fori_loop(0, 7, one, 0)

    def sent(self, phase, src, full):
        def one(i, carry):
            self.copy(phase, i, src, full.at[self.col, self.c]).wait_send()
            return carry

        lax.fori_loop(0, 7, one, 0)

    def core(self, phase, full):
        own = full.at[:, self.c]
        return remote(
            own, own, self.core_send.at[phase], self.core_recv.at[phase], (self.s, self.f + 1 - 2 * self.c)
        )

    def core_wait(self, phase, full):
        dst = full.at[:, 1 - self.c]
        remote(
            dst, dst, self.core_send.at[phase], self.core_recv.at[phase], (self.s, self.f + 1 - 2 * self.c)
        ).wait_recv()


def labels(position, first, second):
    return jnp.where(position >= first, 1, 0) + jnp.where(position >= second, 1, 0)


def masks(j, yh, docs):
    first, second = docs[0, 0], docs[0, 1]
    wide = 128 * (j + 1)
    row = lax.broadcasted_iota(jnp.int32, (128, wide), 0) + 128 * (2 * j + yh)
    lane = lax.broadcasted_iota(jnp.int32, (128, wide), 1)
    start = (lane >> 7) * 256 + (lane & 127)
    row_label = labels(row, first, second)
    found = []
    for parity in (yh, 1 - yh):
        key = start + 128 * parity
        found.append((key <= row) & (labels(key, first, second) == row_label))
    return found


def probabilities(q, keys, seen):
    scores = [jnp.where(ok, nt(q, k) * 0.125, masked_score) for k, ok in zip(keys, seen)]
    top = jnp.maximum(
        jnp.max(scores[0], axis=-1, keepdims=True), jnp.max(scores[1], axis=-1, keepdims=True)
    )
    weights = [jnp.exp(s - top) for s in scores]
    inverse = 1.0 / (split_sum(weights[0]) + split_sum(weights[1]))
    return [w * inverse for w in weights]


def head_lanes(h):
    lane = lax.broadcasted_iota(jnp.int32, (128, 128), 1)
    return lane < 64 if h == 0 else lane >= 64


def only(keep, values):
    return jnp.where(keep, values.astype(jnp.float32), 0.0).astype(jnp.bfloat16)


def wide_tile(full, tile):
    part = full[:, :, :, tile]
    return part.reshape(1024, part.shape[-1])


def dense_forward_kernel(
    x, gain_tile, docs, w_qkv, w_out, w_up, w_down, exp_in, exp_out,
    hid, mixed, after, gains, o_n1, o_n2, o_act, o_dg, o_q, o_kv, o_kvo, o_wq, o_wo, o_wu, o_wd, o_ain, o_aout,
    sq, su, wq, wo, wu, wd, gmine, gother,
    n1, n2, qb, kvb, kvo, mixs, act, dg, ps, pr,
    zs, zr, ys, yr, fs, fr, ks, kr, gs, gr, ss, sr, osem,
):
    line, own = Line(zs, zr), Owners(fs, fr, ks, kr)
    z, yh, f, c = place()
    s = lax.axis_index("seq")
    col = lax.div(f, 2)
    bar = pltpu.get_barrier_semaphore()
    other = (s, f + 1 - 2 * c)
    mate = (2 * z + 1 - yh, f)
    swap_mate = (2 * z + 1 - yh, f + 1 - 2 * c)
    for d in (1, 2, 3):
        greet(bar, (2 * line.index(d) + yh, f))
    for device in (other, mate, swap_mate):
        greet(bar, device)

    def meet(i, carry):
        greet(bar, own.device(lax.rem(col + i + 1, 8)))
        return carry

    lax.fori_loop(0, 7, meet, 0)
    for part in range(3):
        sq[:, 256 * part : 256 * part + 256] = w_qkv[:, pl.ds(pl.multiple_of(1024 * part + 256 * z, 256), 256)]
    low = lax.broadcasted_iota(jnp.int32, (64, 128), 1) < 64
    odd = lax.rem(z, 2) == 1
    for n in range(8):
        at = 512 * n + 128 * lax.div(z, 2)
        a = w_up[:, pl.ds(pl.multiple_of(at, 128), 128)].astype(jnp.float32)
        b = w_up[:, pl.ds(pl.multiple_of(at + 256, 128), 128)].astype(jnp.float32)
        kept = jnp.where(low, a, pltpu.roll(b, 64, 1))
        moved = jnp.where(low, pltpu.roll(a, 64, 1), b)
        su[:, 128 * n : 128 * n + 128] = jnp.where(odd, moved, kept).astype(jnp.bfloat16)
    xhat = norm_parts(x[...].astype(jnp.float32))[0]
    pl.semaphore_wait(bar, 13)
    tile_at = pl.ds(pl.multiple_of(128 * col, 128), 128)

    def gain_copy(i):
        return remote(
            gain_tile, gmine.at[:, tile_at], gs.at[i], gr.at[i], own.device(lax.rem(col + i + 1, 8))
        )

    def push_gain(i, carry):
        gain_copy(i).start()
        return carry

    lax.fori_loop(0, 7, push_gain, 0)
    gmine[:, tile_at] = gain_tile[...]
    own.start(0, sq, wq)
    wq[col, c] = sq[...]

    def wait_gain(i, carry):
        q = lax.rem(col + 7 - i, 8)
        dst = gmine.at[:, pl.ds(pl.multiple_of(128 * q, 128), 128)]
        remote(dst, dst, gs.at[i], gr.at[i], own.device(q)).wait_recv()
        return carry

    lax.fori_loop(0, 7, wait_gain, 0)
    gain_core = remote(gmine, gother, gs.at[7], gr.at[7], other)
    gain_core.start()
    gain_core.wait_recv()
    vectors = gmine[...].astype(jnp.float32) + gother[...].astype(jnp.float32)
    gains[...] = vectors[0:8]
    n1[block(z), :] = (xhat * gains[0:1, :] + gains[2:3, :]).astype(jnp.bfloat16)
    line.spread(0, n1)
    own.start(1, w_out, wo)
    wo[col, c] = w_out[...]
    own.start(2, su, wu)
    wu[col, c] = su[...]
    down_rows = w_down.at[pl.ds(pl.multiple_of(64 * z, 64), 64)]
    own.start(3, down_rows, wd)
    wd[col, c] = down_rows[...]
    own.wait(0, wq)
    own.core(0, wq).start()
    own.core_wait(0, wq)

    def kv_copy(i, j):
        return remote(kvb.at[block(j)], kvo.at[block(j)], ys.at[i], yr.at[i], mate)

    def project_qkv(i, carry):
        d = order(i)
        j = line.index(d)

        @pl.when(i > 0)
        def _():
            line.arrived(0, d, n1)

        values = n1[block(j), :]
        qb[block(j), :] = nn(values, wide_tile(wq, slice(0, 256))).astype(jnp.bfloat16)
        kvb[block(j), 0:256] = nn(values, wide_tile(wq, slice(256, 512))).astype(jnp.bfloat16)
        kvb[block(j), 256:512] = nn(values, wide_tile(wq, slice(512, 768))).astype(jnp.bfloat16)
        kv_copy(i, j).start()
        return carry

    lax.fori_loop(0, 4, project_qkv, 0)
    own.wait(1, wo)
    own.core(1, wo).start()
    for i in range(4):
        kv_copy(i, line.index(order(i))).wait_recv()
    swaps = [
        remote(exp_in.at[0], o_ain, ss.at[0], sr.at[0], swap_mate),
        remote(exp_out.at[0], o_aout, ss.at[1], sr.at[1], swap_mate),
    ]

    @pl.when(c != yh)
    def _():
        for swap in swaps:
            swap.start()

    for j in range(4):
        seen = masks(j, yh, docs)
        wide = slice(0, 128 * (j + 1))
        for p in range(2):
            lanes = slice(128 * p, 128 * p + 128)
            value_lanes = slice(256 + 128 * p, 384 + 128 * p)
            q = qb[128 * j : 128 * j + 128, lanes]
            keys = [kvb[wide, lanes], kvo[wide, lanes]]
            values = [kvb[wide, value_lanes], kvo[wide, value_lanes]]
            outs = []
            for h in range(2):
                probs = probabilities(only(head_lanes(h), q), keys, seen)
                outs.append(
                    nn(probs[0].astype(jnp.bfloat16), values[0]) + nn(probs[1].astype(jnp.bfloat16), values[1])
                )
            mixs[128 * j : 128 * j + 128, lanes] = jnp.where(head_lanes(0), outs[0], outs[1]).astype(jnp.bfloat16)
    my_lanes = pl.ds(pl.multiple_of(256 * z, 256), 256)
    for d in (1, 3, 2):
        line.copy(1, d, mixs.at[block(line.index(d))], mixed.at[:, my_lanes]).start()
    mixed[:, my_lanes] = mixs[block(z), :]
    own.wait(2, wu)
    own.core(2, wu).start()
    own.wait(3, wd)
    own.core(3, wd).start()
    own.core_wait(1, wo)
    for d in (1, 3, 2):
        j = line.index(d)
        dst = mixed.at[:, pl.ds(pl.multiple_of(256 * j, 256), 256)]
        remote(dst, dst, zs.at[1, 3 - d], zr.at[1, 3 - d], (2 * j + yh, f)).wait_recv()
    for n in range(4):
        tile = slice(256 * n, 256 * n + 256)
        after[:, tile] = x[:, tile].astype(jnp.float32) + nn(mixed[...], wide_tile(wo, tile))
    xhat = norm_parts(after[...])[0]
    n2[block(z), :] = (xhat * gains[1:2, :] + gains[3:4, :]).astype(jnp.bfloat16)
    line.spread(2, n2)
    own.core_wait(2, wu)
    own.core_wait(3, wd)
    stores = [
        pltpu.make_async_copy(src, dst, osem.at[k])
        for k, (src, dst) in enumerate(
            [(n1, o_n1), (qb, o_q), (kvb, o_kv), (kvo, o_kvo), (wq, o_wq), (wo, o_wo), (wu, o_wu), (wd, o_wd)]
        )
    ]
    for store in stores:
        store.start()

    def feed(i, carry):
        d = order(i)
        j = line.index(d)

        @pl.when(i > 0)
        def _():
            line.arrived(2, d, n2)

        values = n2[block(j), :]
        for n in range(4):
            tile = slice(n * 256, (n + 1) * 256)
            acted, slope = gelu_parts(nn(values, wide_tile(wu, tile)))
            act[block(j), tile] = acted.astype(jnp.bfloat16)
            dg[block(j), tile] = slope
        values = act[block(j), :]
        for n in range(4):
            tile = slice(n * 256, (n + 1) * 256)
            ps[block(j), tile] = nn(values, wide_tile(wd, tile)).astype(jnp.bfloat16)

        @pl.when(i > 0)
        def _():
            line.give(3, d, ps, pr)

        return carry

    lax.fori_loop(0, 4, feed, 0)
    late = [
        pltpu.make_async_copy(src, dst, osem.at[8 + k])
        for k, (src, dst) in enumerate([(n2, o_n2), (act, o_act), (dg, o_dg)])
    ]
    for store in late:
        store.start()
    hid[...] = (after[...] + line.total(3, ps, pr)).astype(jnp.bfloat16)
    gain_core.wait_send()

    def sent_gain(i, carry):
        gain_copy(i).wait_send()
        return carry

    lax.fori_loop(0, 7, sent_gain, 0)
    own.sent(0, sq, wq)
    own.sent(1, w_out, wo)
    own.sent(2, su, wu)
    own.sent(3, down_rows, wd)
    for phase, full in enumerate((wq, wo, wu, wd)):
        own.core(phase, full).wait_send()
    for i in range(4):
        kv_copy(i, line.index(order(i))).wait_send()
    line.sent(0, n1)
    for d in (1, 3, 2):
        line.copy(1, d, mixs.at[block(line.index(d))], mixed.at[:, my_lanes]).wait_send()
    line.sent(2, n2)
    line.sent(3, ps)

    @pl.when(c != yh)
    def _():
        for swap in swaps:
            swap.wait()

    for store in stores + late:
        store.wait()


def dense_forward_call(x, gain_tile, docs, w_qkv, w_out, w_up, w_down, exp_in, exp_out):
    bf, f32 = jnp.bfloat16, jnp.float32
    vmem, anywhere = pl.BlockSpec(memory_space=pltpu.VMEM), pl.BlockSpec(memory_space=pl.ANY)
    smem = pl.BlockSpec(memory_space=pltpu.SMEM)
    shape = jax.ShapeDtypeStruct
    line = [pltpu.VMEM((512, 1024), bf)]
    weight = [(8, 2, 64, 768), (8, 2, 64, 1024), (8, 2, 64, 1024), (8, 2, 64, 1024)]
    saved = [
        shape((512, 1024), bf), shape((512, 1024), bf), shape((512, 1024), bf), shape((512, 1024), f32),
        shape((512, 256), bf), shape((512, 512), bf), shape((512, 512), bf),
    ] + [shape(w, bf) for w in weight] + [shape((1024, 512), bf), shape((512, 1024), bf)]
    dma = pltpu.SemaphoreType.DMA
    return pl.pallas_call(
        dense_forward_kernel,
        out_shape=[shape((128, 1024), bf), shape((128, 1024), bf), shape((128, 1024), f32), shape((8, 1024), f32)]
        + saved,
        in_specs=[vmem, vmem, smem, vmem, vmem, vmem, vmem, anywhere, anywhere],
        out_specs=[vmem] * 4 + [anywhere] * len(saved),
        scratch_shapes=[
            pltpu.VMEM((64, 768), bf),
            pltpu.VMEM((64, 1024), bf),
            *[pltpu.VMEM(w, bf) for w in weight],
            pltpu.VMEM((16, 1024), bf),
            pltpu.VMEM((16, 1024), bf),
            *(line * 2),
            pltpu.VMEM((512, 256), bf),
            pltpu.VMEM((512, 512), bf),
            pltpu.VMEM((512, 512), bf),
            pltpu.VMEM((512, 256), bf),
            *line,
            pltpu.VMEM((512, 1024), f32),
            *(line * 2),
            dma((4, 3)), dma((4, 3)), dma((4,)), dma((4,)), dma((4, 7)), dma((4, 7)),
            dma((4,)), dma((4,)), dma((8,)), dma((8,)), dma((2,)), dma((2,)), dma((11,)),
        ],
        compiler_params=pltpu.CompilerParams(collective_id=2, has_side_effects=True, vmem_limit_bytes=60 << 20),
        name="dense_forward",
    )(x, gain_tile, docs, w_qkv, w_out, w_up, w_down, exp_in, exp_out)


class Plane:
    def __init__(self, cols, send, recv):
        self.cols, self.send, self.recv = cols, send, recv

    def copy(self, phase, i, src_of, dst):
        q = lax.rem(self.cols.m + i + 1, 16)
        return remote(
            src_of(q), dst.at[self.cols.m], self.send.at[phase, i], self.recv.at[phase, i], self.cols.device(q)
        )

    def start(self, phase, src_of, dst):
        def one(i, carry):
            self.copy(phase, i, src_of, dst).start()
            return carry

        lax.fori_loop(0, 15, one, 0)

    def wait(self, phase, dst):
        def one(i, carry):
            q = lax.rem(self.cols.m + 15 - i, 16)
            piece = dst.at[q]
            remote(piece, piece, self.send.at[phase, i], self.recv.at[phase, i], self.cols.device(q)).wait_recv()
            return carry

        lax.fori_loop(0, 15, one, 0)

    def sent(self, phase, src_of, dst):
        def one(i, carry):
            self.copy(phase, i, src_of, dst).wait_send()
            return carry

        lax.fori_loop(0, 15, one, 0)


class Everyone:
    def __init__(self, send, recv):
        self.s, self.f = lax.axis_index("seq"), lax.axis_index("fsdp")
        self.send, self.recv = send, recv

    def copy(self, phase, i, buf):
        own = buf.at[self.s]
        return remote(
            own, own, self.send.at[phase, i], self.recv.at[phase, i], (lax.rem(self.s + i + 1, 8), self.f)
        )

    def start(self, phase, buf):
        for i in range(7):
            self.copy(phase, i, buf).start()

    def wait(self, phase, buf):
        for i in range(7):
            q = lax.rem(self.s + 7 - i, 8)
            dst = buf.at[q]
            remote(dst, dst, self.send.at[phase, i], self.recv.at[phase, i], (q, self.f)).wait_recv()

    def sent(self, phase, buf):
        for i in range(7):
            self.copy(phase, i, buf).wait_send()


def dense_backward_kernel(
    gh, x, after, docs, gains, mixed, n1_h, n2_h, act_h, dg_h, q_h, kv_h, kvo_h, wq_h, wo_h, wu_h, wd_h, gin, gout,
    gx, gq, go, gu, gd, gvec, rin, rout,
    ghs, n1, n2, act, dg, gp, qb, kvb, kvo, wq, wo, wu, wd,
    ps, pr, ps2, pr2, gms, gm, dp, dkv, dkvo, kvs, kvr,
    md, mu, mo, mq, td, tu, to, tq, rd, ru, ro, rq,
    gad, gaf, vmine, vcore, vplane, vline, outz, bd, bu, bo, bq,
    lsem, zs, zr, ys, yr, ks, kr, cs, cr, qs, qr, ss, sr, vs, vr,
):
    line = Line(zs, zr)
    cols = Columns(cs, cr)
    plane, everyone = Plane(cols, cs, cr), Everyone(qs, qr)
    z, yh, f, c = place()
    s = lax.axis_index("seq")
    col, m = lax.div(f, 2), cols.m
    bar = pltpu.get_barrier_semaphore()
    other = (s, f + 1 - 2 * c)
    mate = (2 * z + 1 - yh, f)
    swap_mate = (2 * z + 1 - yh, f + 1 - 2 * c)

    def meet(i, carry):
        greet(bar, cols.device(lax.rem(m + i + 1, 16)))
        return carry

    lax.fori_loop(0, 15, meet, 0)
    for i in range(7):
        greet(bar, (lax.rem(s + i + 1, 8), f))
    greet(bar, other)
    greet(bar, swap_mate)
    loads = [
        pltpu.make_async_copy(src, dst, lsem.at[k])
        for k, (src, dst) in enumerate(
            [
                (wd_h, wd), (dg_h, dg), (wu_h, wu), (act_h, act), (n2_h, n2), (wo_h, wo), (q_h, qb), (kv_h, kvb),
                (kvo_h, kvo), (wq_h, wq), (n1_h, n1),
            ]
        )
    ]
    for load in loads:
        load.start()
    ghs[block(z), :] = gh[...]
    pl.semaphore_wait(bar, 24)
    line.spread(0, ghs)
    swaps = [
        remote(gin, rin, ss.at[0], sr.at[0], swap_mate),
        remote(gout, rout, ss.at[1], sr.at[1], swap_mate),
    ]

    @pl.when(c != yh)
    def _():
        for swap in swaps:
            swap.start()

    for load in loads[:3]:
        load.wait()

    def feed(i, carry):
        d = order(i)
        j = line.index(d)

        @pl.when(i > 0)
        def _():
            line.arrived(0, d, ghs)

        values = ghs[block(j), :]
        for n in range(4):
            tile = slice(n * 256, (n + 1) * 256)
            rows = wd[2 * n : 2 * n + 2].reshape(256, 1024)
            gp[block(j), tile] = (dg[block(j), tile] * nt(values, rows)).astype(jnp.bfloat16)
        pres = gp[block(j), :]
        for n in range(4):
            tile = slice(n * 256, (n + 1) * 256)
            rows = wu[2 * n : 2 * n + 2].reshape(256, 1024)
            ps[block(j), tile] = nt(pres, rows).astype(jnp.bfloat16)

        @pl.when(i > 0)
        def _():
            line.give(1, d, ps, pr)

        return carry

    lax.fori_loop(0, 4, feed, 0)
    for load in loads[3:6]:
        load.wait()

    def weight_grad(lhs, rhs, mine, theirs):
        def one(n, carry):
            rows = lhs[:, pl.ds(pl.multiple_of(n * 256, 256), 256)]
            grad = tn(rows, rhs[...])
            for half in range(2):
                first = grad[128 * half : 128 * half + 64].astype(jnp.bfloat16)
                second = grad[128 * half + 64 : 128 * half + 128].astype(jnp.bfloat16)
                low = c == 0
                mine[2 * n + half] = jnp.where(low, first, second)
                theirs[2 * n + half] = jnp.where(low, second, first)
            return carry

        lax.fori_loop(0, 4, one, 0)

    def core_copy(phase, src, dst):
        return remote(src, dst, ks.at[phase], kr.at[phase], other)

    def piece_of(mine):
        return lambda q: mine.at[lax.div(q, 2), pl.ds(pl.multiple_of(32 * lax.rem(q, 2), 32), 32)]

    def reduce_core(phase, mine, theirs, got, dst):
        core_copy(phase, theirs, got).wait()

        def one(n, carry):
            mine[n] = (mine[n].astype(jnp.float32) + got[n].astype(jnp.float32)).astype(jnp.bfloat16)
            return carry

        lax.fori_loop(0, 8, one, 0)
        plane.start(phase, piece_of(mine), dst)
        dst[m] = mine[col, pl.ds(pl.multiple_of(32 * yh, 32), 32), :]

    def plane_total(phase, dst):
        plane.wait(phase, dst)
        acc = dst[0].astype(jnp.float32)
        for q in range(1, 16):
            acc += dst[q].astype(jnp.float32)
        return acc

    weight_grad(act, ghs, md, td)
    core_copy(0, td, rd).start()
    weight_grad(n2, gp, mu, tu)
    core_copy(1, tu, ru).start()
    reduce_core(0, md, td, rd, gad.at[0])
    grad_normed = line.total(1, ps, pr)
    xhat, scale = norm_parts(after[...])
    vmine[1:2, :] = jnp.sum(grad_normed * xhat, axis=0, keepdims=True)
    vmine[3:4, :] = jnp.sum(grad_normed, axis=0, keepdims=True)
    grad_after = gh[...].astype(jnp.float32) + norm_back(grad_normed, gains[1:2, :], xhat, scale)
    gx[...] = grad_after
    grad_attn = grad_after.astype(jnp.bfloat16)
    for n in range(4):
        gms[:, 256 * n : 256 * n + 256] = nt(grad_attn, wo[2 * n : 2 * n + 2].reshape(256, 1024)).astype(
            jnp.bfloat16
        )

    def gm_copy(d):
        lanes = pl.ds(pl.multiple_of(256 * line.index(d), 256), 256)
        return line.copy(2, d, gms.at[:, lanes], gm.at[block(z)])

    for d in (1, 3, 2):
        gm_copy(d).start()
    gm[block(z), :] = gms[:, pl.ds(pl.multiple_of(256 * z, 256), 256)]
    reduce_core(1, mu, tu, ru, gad.at[1])
    gp[block(0), :] = grad_attn
    weight_grad(mixed, gp.at[block(0)], mo, to)
    core_copy(2, to, ro).start()
    for load in loads[6:]:
        load.wait()
    for d in (1, 3, 2):
        line.arrived(2, d, gm)
    dkv[...] = jnp.zeros_like(dkv)
    dkvo[...] = jnp.zeros_like(dkvo)

    def kv_copy(j):
        return remote(kvs.at[block(j)], kvr.at[block(j)], ys.at[j], yr.at[j], mate)

    for j in (3, 2, 1, 0):
        seen = masks(j, yh, docs)
        wide = slice(0, 128 * (j + 1))
        rows = slice(128 * j, 128 * j + 128)
        for p in range(2):
            lanes = slice(128 * p, 128 * p + 128)
            value_lanes = slice(256 + 128 * p, 384 + 128 * p)
            q, grad = qb[rows, lanes], gm[rows, lanes]
            keys = [kvb[wide, lanes], kvo[wide, lanes]]
            values = [kvb[wide, value_lanes], kvo[wide, value_lanes]]
            outs = []
            for h in range(2):
                q_h, grad_h = only(head_lanes(h), q), only(head_lanes(h), grad)
                probs = probabilities(q_h, keys, seen)
                back = [nt(grad_h, v) for v in values]
                dot = split_sum(probs[0] * back[0]) + split_sum(probs[1] * back[1])
                slopes = [(pr_ * (b - dot)).astype(jnp.bfloat16) for pr_, b in zip(probs, back)]
                outs.append(nn(slopes[0], keys[0]) + nn(slopes[1], keys[1]))
                for k, acc in enumerate((dkv, dkvo)):
                    acc[wide, lanes] += tn(slopes[k], q_h) * 0.125
                    acc[wide, value_lanes] += tn(probs[k].astype(jnp.bfloat16), grad_h)
            dp[rows, lanes] = (jnp.where(head_lanes(0), outs[0], outs[1]) * 0.125).astype(jnp.bfloat16)
        kvs[rows, :] = dkvo[rows, :].astype(jnp.bfloat16)
        kv_copy(j).start()
    reduce_core(2, mo, to, ro, gad.at[2])
    for j in (3, 2, 1, 0):
        rows = slice(128 * j, 128 * j + 128)
        kv_copy(j).wait_recv()
        dp[rows, 256:768] = (dkv[rows, :] + kvr[rows, :].astype(jnp.float32)).astype(jnp.bfloat16)

    def last(i, carry):
        d = order(3 - i)
        j = line.index(d)
        values = dp[block(j), :]
        for n in range(4):
            tile = slice(n * 256, (n + 1) * 256)
            rows = wq[2 * n : 2 * n + 2].reshape(256, 768)
            ps2[block(j), tile] = nt(values, rows).astype(jnp.bfloat16)

        @pl.when(i < 3)
        def _():
            line.give(3, d, ps2, pr2)

        return carry

    lax.fori_loop(0, 4, last, 0)
    weight_grad(n1, dp, mq, tq)
    core_copy(3, tq, rq).start()
    bd[s] = plane_total(0, gad.at[0]).astype(jnp.bfloat16)
    everyone.start(0, bd)
    bu[s] = plane_total(1, gad.at[1]).astype(jnp.bfloat16)
    everyone.start(1, bu)
    reduce_core(3, mq, tq, rq, gaf)
    grad_normed = line.total(3, ps2, pr2)
    xhat, scale = norm_parts(x[...].astype(jnp.float32))
    vmine[0:1, :] = jnp.sum(grad_normed * xhat, axis=0, keepdims=True)
    vmine[2:3, :] = jnp.sum(grad_normed, axis=0, keepdims=True)
    vmine[4:8, :] = jnp.zeros((4, 1024), jnp.float32)
    give_core = remote(vmine, vcore, vs.at[0], vr.at[0], other)
    give_core.start()
    gx[...] += norm_back(grad_normed, gains[0:1, :], xhat, scale)
    total_out = plane_total(2, gad.at[2])
    for n in range(4):
        outz[4 + n] = total_out[:, 256 * n : 256 * n + 256].astype(jnp.bfloat16)

    def out_copy(d):
        return line.copy(4, d, outz.at[4 + line.index(d)], outz.at[z])

    for d in (1, 3, 2):
        out_copy(d).start()
    give_core.wait()
    vmine[...] += vcore[...]

    def tile_of(q):
        return vmine.at[:, pl.ds(pl.multiple_of(128 * lax.div(q, 2), 128), 128)]

    plane.start(4, tile_of, vplane)
    vplane[m] = vmine[:, pl.ds(pl.multiple_of(128 * col, 128), 128)]
    acc = outz[4 + z].astype(jnp.float32)
    for d in (1, 3, 2):
        dst = outz.at[line.index(d)]
        remote(dst, dst, zs.at[4, 3 - d], zr.at[4, 3 - d], (2 * line.index(d) + yh, f)).wait_recv()
        acc += outz[line.index(d)].astype(jnp.float32)
    bo[s] = acc.astype(jnp.bfloat16)
    everyone.start(2, bo)
    bq[s] = plane_total(3, gaf).astype(jnp.bfloat16)
    everyone.start(3, bq)
    plane.wait(4, vplane)
    vline[z] = jnp.sum(vplane[...], axis=0)

    def vec_copy(d):
        return line.copy(5, d, vline.at[z], vline.at[z])

    for d in (1, 3, 2):
        vec_copy(d).start()
    everyone.wait(0, bd)
    everyone.wait(1, bu)
    for zz in range(4):
        for half in range(2):
            gd[64 * zz + 32 * half : 64 * zz + 32 * half + 32, :] = bd[2 * zz + half].astype(jnp.float32)
    for half in range(2):
        rows = slice(32 * half, 32 * half + 32)
        lane = lax.broadcasted_iota(jnp.int32, (32, 128), 1) < 64
        for n in range(8):
            tile = slice(128 * n, 128 * n + 128)
            quarter = [bu[2 * zz + half, :, tile].astype(jnp.float32) for zz in range(4)]
            turned = [pltpu.roll(v, 64, 1) for v in quarter]
            at = 512 * n
            gu[rows, at : at + 128] = jnp.where(lane, quarter[0], turned[1])
            gu[rows, at + 128 : at + 256] = jnp.where(lane, quarter[2], turned[3])
            gu[rows, at + 256 : at + 384] = jnp.where(lane, turned[0], quarter[1])
            gu[rows, at + 384 : at + 512] = jnp.where(lane, turned[2], quarter[3])
    everyone.wait(2, bo)
    for zz in range(4):
        for half in range(2):
            go[32 * half : 32 * half + 32, 256 * zz : 256 * zz + 256] = bo[2 * zz + half].astype(jnp.float32)
    everyone.wait(3, bq)
    for zz in range(4):
        for half in range(2):
            for part in range(3):
                gq[32 * half : 32 * half + 32, 1024 * part + 256 * zz : 1024 * part + 256 * zz + 256] = bq[
                    2 * zz + half, :, 256 * part : 256 * part + 256
                ].astype(jnp.float32)
    for d in (1, 3, 2):
        dst = vline.at[line.index(d)]
        remote(dst, dst, zs.at[5, 3 - d], zr.at[5, 3 - d], (2 * line.index(d) + yh, f)).wait_recv()
    gvec[...] = jnp.sum(vline[...], axis=0)
    line.sent(0, ghs)
    line.sent(1, ps)
    for d in (1, 3, 2):
        gm_copy(d).wait_send()
        out_copy(d).wait_send()
        vec_copy(d).wait_send()
    line.sent(3, ps2)
    for j in range(4):
        kv_copy(j).wait_send()
    for phase, (mine, dst) in enumerate(((md, gad.at[0]), (mu, gad.at[1]), (mo, gad.at[2]), (mq, gaf))):
        plane.sent(phase, piece_of(mine), dst)
    plane.sent(4, tile_of, vplane)
    for phase, buf in enumerate((bd, bu, bo, bq)):
        everyone.sent(phase, buf)

    @pl.when(c != yh)
    def _():
        for swap in swaps:
            swap.wait()


def dense_backward_call(gh, x, after, docs, gains, mixed, saved, gin, gout):
    bf, f32 = jnp.bfloat16, jnp.float32
    vmem, anywhere = pl.BlockSpec(memory_space=pltpu.VMEM), pl.BlockSpec(memory_space=pl.ANY)
    smem = pl.BlockSpec(memory_space=pltpu.SMEM)
    shape, V = jax.ShapeDtypeStruct, pltpu.VMEM
    line = [V((512, 1024), bf)]
    dma = pltpu.SemaphoreType.DMA
    wide, narrow = [V((8, 64, 1024), bf)], [V((8, 64, 768), bf)]
    return pl.pallas_call(
        dense_backward_kernel,
        out_shape=[
            shape((128, 1024), f32), shape((64, 3072), f32), shape((64, 1024), f32), shape((64, 4096), f32),
            shape((256, 1024), f32), shape((8, 128), f32), shape((2, 1024, 512), bf), shape((2, 512, 1024), bf),
        ],
        in_specs=[vmem, vmem, vmem, smem, vmem, vmem] + [anywhere] * 13,
        out_specs=[vmem] * 6 + [anywhere] * 2,
        scratch_shapes=[
            *(line * 4), V((512, 1024), f32), *line,
            V((512, 256), bf), V((512, 512), bf), V((512, 512), bf),
            V((8, 2, 64, 768), bf), V((8, 2, 64, 1024), bf), V((8, 2, 64, 1024), bf), V((8, 2, 64, 1024), bf),
            *(line * 4),
            V((128, 1024), bf), V((512, 256), bf), V((512, 768), bf), V((512, 512), f32), V((512, 512), f32),
            V((512, 512), bf), V((512, 512), bf),
            *(wide * 3), *narrow, *(wide * 3), *narrow, *(wide * 3), *narrow,
            V((3, 16, 32, 1024), bf), V((16, 32, 768), bf),
            V((8, 1024), f32), V((8, 1024), f32), V((16, 8, 128), f32), V((4, 8, 128), f32),
            V((8, 32, 256), bf),
            V((8, 32, 1024), bf), V((8, 32, 1024), bf), V((8, 32, 256), bf), V((8, 32, 768), bf),
            dma((11,)), dma((6, 3)), dma((6, 3)), dma((4,)), dma((4,)), dma((4,)), dma((4,)),
            dma((5, 15)), dma((5, 15)), dma((4, 7)), dma((4, 7)), dma((2,)), dma((2,)), dma((1,)), dma((1,)),
        ],
        compiler_params=pltpu.CompilerParams(collective_id=3, has_side_effects=True, vmem_limit_bytes=62 << 20),
        name="dense_backward",
    )(gh, x, after, docs, gains, mixed, *saved, gin, gout)


def on_device(
    inputs,
    doc_starts,
    route,
    norm_gain,
    norm_bias,
    w_qkv,
    w_out,
    w_up,
    w_down,
    exp_gain,
    exp_bias,
    exp_in,
    exp_out,
    centroid,
    cotangent,
):
    tok_rows, width = 128, 1024
    x = inputs.reshape(tok_rows, width)
    core = lax.rem(lax.axis_index("fsdp"), 2)
    mine = lax.rem(lax.axis_index("seq"), 2) == core
    share = jnp.pad(jnp.concatenate([norm_gain, norm_bias]), ((0, 12), (0, 0)))
    none = jnp.zeros_like(share)
    gain_tile = jnp.where(core == 0, jnp.concatenate([share, none], 1), jnp.concatenate([none, share], 1))
    core_pairs = [(i, i + 1 - 2 * (i % 2)) for i in range(128)]
    vec = jnp.concatenate([exp_gain[0], exp_bias[0], centroid], axis=0)
    vec = jnp.where(mine, vec, lax.ppermute(vec, ("seq", "fsdp"), core_pairs)).astype(jnp.float32)
    vec = jnp.pad(vec, ((0, 3), (0, 0)))
    hidden, mixed, after, gains, *saved, in_a, out_a = dense_forward_call(
        x, gain_tile, doc_starts, w_qkv, w_out, w_up, w_down, exp_in[0], exp_out[0]
    )
    result, grad_hidden, vec_grads, grad_in, grad_out = expert_call(
        hidden,
        cotangent.reshape(tok_rows, width),
        route.reshape(1, tok_rows),
        vec,
        exp_in[0],
        exp_out[0],
        in_a,
        out_a,
    )
    grad_x, grad_qkv, grad_wo, grad_up, grad_down, norm_grads, swapped_in, swapped_out = dense_backward_call(
        grad_hidden, x, after, doc_starts, gains, mixed, saved, grad_in, grad_out
    )
    norm_grads = jnp.where(core == 0, norm_grads[:4, :64], norm_grads[:4, 64:])
    return (
        result[None],
        grad_x[None],
        norm_grads[0:2],
        norm_grads[2:4],
        grad_qkv,
        grad_wo,
        grad_up,
        grad_down,
        vec_grads[None, 0:2],
        vec_grads[None, 2:4],
        jnp.where(mine, grad_in, swapped_in).astype(jnp.float32)[None],
        jnp.where(mine, grad_out, swapped_out).astype(jnp.float32)[None],
        vec_grads[4:5],
    )


def solution(mesh):
    in_specs = (
        P("fsdp", "seq", None),
        P("fsdp", None),
        P("fsdp", "seq", None),
        P(None, "fsdp"),
        P(None, "fsdp"),
        P("fsdp", None),
        P("fsdp", None),
        P("fsdp", None),
        P("fsdp", None),
        P("fsdp", None, None),
        P("fsdp", None, None),
        P("fsdp", None, None, "seq"),
        P("fsdp", None, "seq", None),
        P("fsdp", None),
        P("fsdp", "seq", None),
    )
    out_specs = (
        P("fsdp", "seq", None),
        P("fsdp", "seq", None),
        P(None, "fsdp"),
        P(None, "fsdp"),
        P("fsdp", None),
        P("fsdp", None),
        P("fsdp", None),
        P("fsdp", None),
        P("fsdp", None, None),
        P("fsdp", None, None),
        P("fsdp", None, None, "seq"),
        P("fsdp", None, "seq", None),
        P("fsdp", None),
    )
    return jax.shard_map(
        on_device, mesh=mesh, in_specs=in_specs, out_specs=out_specs, check_vma=False
    )
```

time: 1180 us -> 396 us (0.34)
  waiting for transfers between devices: 674 us -> 0.01 us
  Pallas kernels: 123 us -> 376 us
  starting transfers between devices: 97.1 us -> 0.09 us
  matrix products: 86.5 us -> 0 us
  blocking collectives: 76.2 us -> 0 us
  local copies, waits for them, and re-layouts: 54 us -> 8.43 us
  other arithmetic: 41.4 us -> 9.89 us
  between operations: 14.9 us -> 0.76 us
    pallas_call x0 -> x2, Pallas kernels: none -> 243 us  [the longest x1 139 us: dense_backward_call(): pl.pallas_call(dense_backward_kernel, out_shape=[shape((128, 1024), f32),...]
    unnamed x19 -> x0, waiting for transfers between devices: 232 us -> none
    reduce_scatter x4 -> x0, waiting for transfers between devices: 202 us -> none  [the longest x1 75.4 us: on_device(): lax.psum_scatter(dense_terms[4].astype(jnp.bfloat16), 'fsdp', scatter_dim...]
    all_gather x6 -> x0, waiting for transfers between devices: 180 us -> none  [the longest x1 51.9 us: on_device(): lax.all_gather(w_up, 'fsdp', axis=0, tiled=True)]
    ppermute x8 -> x1, starting transfers between devices: 96.3 us -> 0.09 us  [on_device(): lax.ppermute(vec, ('seq', 'fsdp'), core_pairs)]
    dot_general x18 -> x0, matrix products: 86.5 us -> none  [the longest x1 7.05 us: on_device(): jnp.einsum('rd,fd->rf', grad_hidden, down_weight, preferred_element_type=...]
    psum x1 -> x0, waiting for transfers between devices: 59.9 us -> none  [on_device(): lax.psum(shard_qkv.astype(jnp.bfloat16), 'seq').astype(jnp.float32)]
    unnamed x59 -> x28, local copies, waits for them, and re-layouts: 49.2 us -> 5.06 us
  transfers between devices with their start and end apart: 23 -> 1, of which waited for: 14 -> 0; matrix products, arithmetic and copies ran while one was open for 11% -> 0% of each run, Pallas kernels for 0% -> 26%
where the time goes in v2:
time: 396 us; the launch traced here: 395 us
  Pallas kernels  376 us (95%)
  other arithmetic  9.89 us (2%)
  local copies, waits for them, and re-layouts  8.43 us (2%)
    pallas_call x1, Pallas kernels, dense_backward_call(): pl.pallas_call(dense_backward_kernel, out_shape=[shape((128, 1024), f32),...  139 us
    pallas_call x1, Pallas kernels, expert_call(): pl.pallas_call(expert_kernel, out_shape=(jax.ShapeDtypeStruct((128, 1024)...  132 us
    pallas_call x1, Pallas kernels, dense_forward_call(): pl.pallas_call(dense_forward_kernel, out_shape=[shape((128, 1024), bf), s...  104 us
  transfers between devices with their start and end apart: 1, of which 0 were waited for; matrix products, arithmetic and copies ran while one was open for 0% of the time, Pallas kernels for 26%

profile of v2, /device:TPU:4, one launch (start us, length us, event | category | flops | bytes accessed | tf_op | source)
XLA Modules:
  0.0 394.7 jit_solution(12616024836979114694)
XLA Ops:
  0.6 0.7 pad_maximum_fusion
  1.4 0.1 collective-permute-start
  1.5 0.7 fusion.2
  2.2 0.7 pad_select_fusion.gain_tile
  2.8 103.9 %dense_forward.1 = (bf16[128,1024]{1,0:T(8,128)(2,1)}, bf16[128,1024]{1,0:T(8,128)(2,1)}, f32[128,1024]{1,0:T(8,128)}, f32[8,1024]{1,0:T(8,128)}, bf16[512,1024]...) custom-call(bf16[128,1024]{1,0:T(8,128)(2,1)} %bitcast.23, ...), custom_call_target="tpu_custom_call" | custom-call | tf_op jit(solution)/shard_map/dense_forward/pallas_call | solution.py:935
  106.7 0.0 collective-permute-done
  106.7 0.0 copy-done.8
  106.8 0.0 copy-done.9
  106.8 0.0 copy-done.10
  106.8 0.6 pad_convert_fusion.vec
  107.4 132.2 %experts.1 = (bf16[128,1024]{1,0:T(8,128)(2,1)}, bf16[128,1024]{1,0:T(8,128)(2,1)}, f32[8,1024]{1,0:T(8,128)}, bf16[2,1024,512]{2,1,0:T(8,128)(2,1)}, bf16[2,512,1024]{2,1,0:T(8,128)(2,1)}) custom-call(bf16[128,1024]{1,0:T(8,128)(2,1)} %get-tuple-element.43.hid, bf16[128,1024]{1,0:T(8,128)(2,1)} %bitcast.26, s32[1,128]{1,0:T(1,128)} %bitcast.32, ...), custom_call_target="tpu_custom_call" | custom-call | tf_op jit(solution)/shard_map/experts/pallas_call | solution.py:545
  239.6 1.4 slice.27
  241.0 1.4 slice_bitcast_fusion
  242.4 139.4 %dense_backward.1 = (f32[128,1024]{1,0:T(8,128)}, f32[64,3072]{1,0:T(8,128)}, f32[64,1024]{1,0:T(8,128)}, f32[64,4096]{1,0:T(8,128)}, f32[256,1024]{1,0:T(8,128)...) custom-call(bf16[128,1024]{1,0:T(8,128)(2,1)} %get-tuple-element.47.gh, ...), custom_call_target="tpu_custom_call" | custom-call | tf_op jit(solution)/shard_map/dense_backward/pallas_call | solution.py:1340
  381.9 0.8 slice_select_fusion
  382.7 0.6 fusion.3
  383.3 4.0 %bitcast_convert_fusion.1 = f32[1,2,1024,512]{3,2,1,0:T(8,128)} fusion(bf16[2,1024,512]{2,1,0:T(8,128)(2,1)} %get-tuple-element.62.gin, bf16[2,1024,512]{2,1,0:T(8,128)(2,1)} %get-tuple-element.71, pred[]{:T(512)S(6)} %eq.8), kind=kLoop, calls=%fused_computation.1 | loop fusion | flops 2097152 | bytes 8388609 | tf_op jit(solution)/shard_map/broadcast_in_dim | solution.py:1424
  387.3 0.0 copy-done
  387.3 0.0 copy-done.1
  387.3 0.0 copy-start.5
  387.3 0.0 copy-start.4
  387.4 2.3 bitcast_convert_fusion
  389.7 0.0 copy-done.6
  389.7 0.7 copy.34
  390.4 0.0 copy-done.5
  390.4 0.8 copy.35
  391.2 0.0 copy-done.4
  391.2 0.9 copy.36
  392.0 0.0 copy-done.7
  392.0 0.7 copy.37
  392.7 1.0 copy.38
  393.7 1.0 copy.39
  (12 shorter events, 0.0 us)
Async XLA Ops:
  1.4 105.3 %collective-permute-start = (bf16[5,1024]{1,0:T(8,128)(2,1)S(1)}, bf16[5,1024]{1,0:T(8,128)(2,1)S(1)}, u32[]{:S(2)}, u32[]{:S(2)}) collective-permute-start(bf16[5,1024]{1,0:T(8,128)(2,1)S(1)} %pad_maximum_fusion), channel_id=1, source_target_pairs={{0,1},{1,0},{2,3},{3,2},{4,5},{5,4},{6,7},{7,6},{8,9},{9,8},{10,11... | collective-permute-start | bytes 30728 | tf_op jit(solution)/shard_map/ppermute | solution.py:1394
  2.8 103.9 %copy-start.8 = (bf16[1,1024]{1,0:T(2,128)(2,1)S(1)}, bf16[1,1024]{1,0:T(2,128)(2,1)}, u32[]{:S(2)}) copy-start(bf16[1,1024]{1,0:T(2,128)(2,1)} %param.28) | copy-start | bytes 6148
  2.8 103.9 %copy-start.9 = (bf16[1,2,1024]{2,1,0:T(2,128)(2,1)S(1)}, bf16[1,2,1024]{2,1,0:T(2,128)(2,1)}, u32[]{:S(2)}) copy-start(bf16[1,2,1024]{2,1,0:T(2,128)(2,1)} %param.25) | copy-start | bytes 12292
  2.8 103.9 %copy-start.10 = (bf16[1,2,1024]{2,1,0:T(2,128)(2,1)S(1)}, bf16[1,2,1024]{2,1,0:T(2,128)(2,1)}, u32[]{:S(2)}) copy-start(bf16[1,2,1024]{2,1,0:T(2,128)(2,1)} %param.24) | copy-start | bytes 12292
  383.3 4.0 %copy-start = (bf16[2,512,1024]{2,1,0:T(8,128)(2,1)S(1)}, bf16[2,512,1024]{2,1,0:T(8,128)(2,1)}, u32[]{:S(2)}) copy-start(bf16[2,512,1024]{2,1,0:T(8,128)(2,1)} %get-tuple-element.63.gout) | copy-start | bytes 6291460
  383.3 4.0 %copy-start.1 = (bf16[2,512,1024]{2,1,0:T(8,128)(2,1)S(1)}, bf16[2,512,1024]{2,1,0:T(8,128)(2,1)}, u32[]{:S(2)}) copy-start(bf16[2,512,1024]{2,1,0:T(8,128)(2,1)} %get-tuple-element.72) | copy-start | bytes 6291460
  387.3 2.3 copy-start.6
  387.3 3.0 copy-start.5
  387.3 3.8 copy-start.4
  389.6 2.4 copy-start.7
  389.6 3.1 copy-start.3
  391.2 2.6 copy-start.2

commit v3 on v1

v3 whole, which is shorter than its diff:
```python
import jax
import jax.numpy as jnp
from jax import lax
from jax.experimental import pallas as pl
from jax.experimental.pallas import tpu as pltpu
from jax.sharding import PartitionSpec as P

MESH = pl.DeviceIdType.MESH
epsilon = 1e-05
masked_score = -1e30


def split_sum(values):
    return jnp.sum(values, axis=-1, keepdims=True)


def norm_parts(values):
    average = split_sum(values) * (1.0 / values.shape[-1])
    centered = values - average
    spread = split_sum(centered * centered) * (1.0 / values.shape[-1])
    scale = lax.rsqrt(spread + epsilon)
    return centered * scale, scale


def norm_back(grad_normed, gain, xhat, scale):
    width = 1.0 / xhat.shape[-1]
    u = grad_normed * gain
    return scale * (u - split_sum(u) * width - xhat * (split_sum(u * xhat) * width))


def gelu_parts(pre):
    inner = 0.7978845608028654
    cubic = 0.044715
    square = pre * pre
    t = jnp.tanh(inner * pre * (1.0 + cubic * square))
    half = 0.5 * (1.0 + t)
    slope = half + 0.5 * pre * (1.0 - t * t) * (inner * (1.0 + 3.0 * cubic * square))
    return pre * half, slope


def nn(a, b):
    return lax.dot_general(a, b, (((1,), (0,)), ((), ())), preferred_element_type=jnp.float32)


def nt(a, b):
    return lax.dot_general(a, b, (((1,), (1,)), ((), ())), preferred_element_type=jnp.float32)


def tn(a, b):
    return lax.dot_general(a, b, (((0,), (0,)), ((), ())), preferred_element_type=jnp.float32)


def remote(src, dst, send, recv, device):
    return pltpu.make_async_remote_copy(
        src_ref=src, dst_ref=dst, send_sem=send, recv_sem=recv, device_id=device, device_id_type=MESH
    )


def greet(bar, device):
    pl.semaphore_signal(bar, inc=1, device_id=device, device_id_type=MESH)


def block(index):
    return pl.ds(pl.multiple_of(index * 128, 128), 128)


def order(i):
    return i + lax.div(i, 2) - 2 * lax.div(i, 3)


class Place:
    def __init__(self):
        self.s, self.f = lax.axis_index("seq"), lax.axis_index("fsdp")
        self.z, self.yh = lax.div(self.s, 2), lax.rem(self.s, 2)
        self.yl, self.col, self.c = lax.div(self.f, 8), lax.div(self.f, 2), lax.rem(self.f, 2)
        self.x = lax.rem(self.col, 4)
        self.m = self.f - self.c + self.yh
        self.other = (self.s, self.f + 1 - 2 * self.c)
        self.mate = (2 * self.z + 1 - self.yh, self.f)
        self.swap_mate = (2 * self.z + 1 - self.yh, self.f + 1 - 2 * self.c)
        self.same = self.c == self.yh


class Ring:
    def __init__(self, at, axis, send, recv):
        self.at, self.axis, self.send, self.recv = at, axis, send, recv
        self.pos = {"z": at.z, "x": at.x, "y": 2 * at.yh + at.yl}[axis]

    def index(self, d):
        return lax.rem(self.pos + d, 4)

    def device(self, j):
        at = self.at
        if self.axis == "z":
            return (2 * j + at.yh, at.f)
        if self.axis == "x":
            return (at.s, at.f - 2 * at.x + 2 * j)
        return (2 * at.z + lax.div(j, 2), 8 * lax.rem(j, 2) + at.f - 8 * at.yl)

    def copy(self, phase, d, src, dst):
        sems = self.send.at[phase, d - 1], self.recv.at[phase, d - 1]
        return remote(src, dst, *sems, self.device(self.index(d)))

    def got(self, phase, d, dst):
        sems = self.send.at[phase, 3 - d], self.recv.at[phase, 3 - d]
        remote(dst, dst, *sems, self.device(self.index(d))).wait_recv()

    def spread(self, phase, buf):
        own = buf.at[block(self.pos)]
        for d in (1, 3, 2):
            self.copy(phase, d, own, own).start()

    def arrived(self, phase, d, buf):
        self.got(phase, d, buf.at[block(self.index(d))])

    def give(self, phase, d, src, dst):
        self.copy(phase, d, src.at[block(self.index(d))], dst.at[block(self.pos)]).start()

    def sent(self, phase, buf):
        own = buf.at[block(self.pos)]
        for d in (1, 3, 2):
            self.copy(phase, d, own, own).wait_send()

    def total(self, phase, own, parts):
        acc = own[block(self.pos), :].astype(jnp.float32)
        for d in (1, 3, 2):
            self.arrived(phase, d, parts)
            acc += parts[block(self.index(d)), :].astype(jnp.float32)
        return acc


class Plane:
    def __init__(self, at, send, recv):
        self.at, self.m = at, at.m
        self.send, self.recv = send, recv

    def device(self, q):
        return (2 * self.at.z + lax.rem(q, 2), q - lax.rem(q, 2) + self.at.c)

    def greet(self, bar):
        def one(i, carry):
            greet(bar, self.device(lax.rem(self.m + i + 1, 16)))
            return carry

        lax.fori_loop(0, 15, one, 0)

    def copy(self, phase, i, src_of, dst_of):
        q = lax.rem(self.m + i + 1, 16)
        return remote(src_of(q), dst_of(self.m), self.send.at[phase, i], self.recv.at[phase, i], self.device(q))

    def start(self, phase, src_of, dst_of):
        def one(i, carry):
            self.copy(phase, i, src_of, dst_of).start()
            return carry

        lax.fori_loop(0, 15, one, 0)

    def wait(self, phase, dst_of):
        def one(i, carry):
            q = lax.rem(self.m + 15 - i, 16)
            dst = dst_of(q)
            remote(dst, dst, self.send.at[phase, i], self.recv.at[phase, i], self.device(q)).wait_recv()
            return carry

        lax.fori_loop(0, 15, one, 0)

    def sent(self, phase, src_of, dst_of):
        def one(i, carry):
            self.copy(phase, i, src_of, dst_of).wait_send()
            return carry

        lax.fori_loop(0, 15, one, 0)


def piece(buf):
    return lambda q: buf.at[pl.ds(pl.multiple_of(q * 16, 16), 16)]


def keep_piece(at, src, dst):
    own = pl.ds(pl.multiple_of(at.m * 16, 16), 16)
    dst[own, :] = src[own, :]


def placings(route):
    row = lax.broadcasted_iota(jnp.int32, (256, 128), 0)
    inner = row & 15
    slot = (row >> 4) * 8 + (inner & 7)
    hit = slot == route
    left = jnp.where(hit & (inner < 8), 1.0, 0.0).astype(jnp.bfloat16)
    right = jnp.where(hit & (inner >= 8), 1.0, 0.0).astype(jnp.bfloat16)
    return left, right


def to_pieces(left, right, rows):
    half = rows.shape[1] // 2
    return (nn(left, rows[:, :half]) + nn(right, rows[:, half:])).astype(jnp.bfloat16)


def from_pieces(left, right, pieces):
    return jnp.concatenate([tn(left, pieces), tn(right, pieces)], axis=1).astype(jnp.bfloat16)


def rows_of(pieces):
    wide = pieces.astype(jnp.float32).reshape(16, 2, 8, 512)
    return jnp.concatenate([wide[:, 0].reshape(128, 512), wide[:, 1].reshape(128, 512)], axis=1)


def pieces_of(rows):
    left = rows[:, :512].reshape(16, 1, 8, 512)
    right = rows[:, 512:].reshape(16, 1, 8, 512)
    return jnp.concatenate([left, right], axis=1).reshape(256, 512).astype(jnp.bfloat16)


class Owners:
    def __init__(self, at, xs, xr, ys, yr, ks, kr):
        self.at = at
        self.ring_x, self.ring_y = Ring(at, "x", xs, xr), Ring(at, "y", ys, yr)
        self.ks, self.kr = ks, kr

    def along_y(self, phase, d, src, full):
        at = self.at
        return self.ring_y.copy(phase, d, src, full.at[at.yl, at.x, at.c, at.yh])

    def along_x(self, phase, d, full):
        own = full.at[:, self.at.x, self.at.c]
        return self.ring_x.copy(phase, d, own, own)

    def core(self, phase, full, c):
        half = full.at[:, :, c]
        return remote(half, half, self.ks.at[phase], self.kr.at[phase], self.at.other)

    def start(self, phase, src, full):
        at = self.at
        for d in (1, 3, 2):
            self.along_y(phase, d, src, full).start()
        full[at.yl, at.x, at.c, at.yh] = src[...]

    def step_x(self, phase, full):
        at = self.at
        for d in (1, 3, 2):
            j = self.ring_y.index(d)
            self.ring_y.got(phase, d, full.at[lax.rem(j, 2), at.x, at.c, lax.div(j, 2)])
        for d in (1, 3, 2):
            self.along_x(phase, d, full).start()

    def step_core(self, phase, full):
        for d in (1, 3, 2):
            self.ring_x.got(phase, d, full.at[:, self.ring_x.index(d), self.at.c])
        self.core(phase, full, self.at.c).start()

    def wait(self, phase, full):
        self.core(phase, full, 1 - self.at.c).wait_recv()

    def sent(self, phase, src, full):
        for d in (1, 3, 2):
            self.along_y(phase, d, src, full).wait_send()
            self.along_x(phase, d, full).wait_send()
        self.core(phase, full, self.at.c).wait_send()


def labels(position, first, second):
    return jnp.where(position >= first, 1, 0) + jnp.where(position >= second, 1, 0)


def masks(j, yh, docs):
    first, second = docs[0, 0], docs[0, 1]
    wide = 128 * (j + 1)
    row = lax.broadcasted_iota(jnp.int32, (128, wide), 0) + 128 * (2 * j + yh)
    lane = lax.broadcasted_iota(jnp.int32, (128, wide), 1)
    start = (lane >> 7) * 256 + (lane & 127)
    row_label = labels(row, first, second)
    found = []
    for parity in (yh, 1 - yh):
        key = start + 128 * parity
        found.append((key <= row) & (labels(key, first, second) == row_label))
    return found


def probabilities(q, keys, seen):
    scores = [jnp.where(ok, nt(q, k) * 0.125, masked_score) for k, ok in zip(keys, seen)]
    top = jnp.maximum(
        jnp.max(scores[0], axis=-1, keepdims=True), jnp.max(scores[1], axis=-1, keepdims=True)
    )
    weights = [jnp.exp(s - top) for s in scores]
    inverse = 1.0 / (split_sum(weights[0]) + split_sum(weights[1]))
    return [w * inverse for w in weights]


def head_lanes(h):
    lane = lax.broadcasted_iota(jnp.int32, (128, 128), 1)
    return lane < 64 if h == 0 else lane >= 64


def only(keep, values):
    return jnp.where(keep, values.astype(jnp.float32), 0.0).astype(jnp.bfloat16)


def wide_tile(full, tile):
    part = full[:, :, :, :, :, tile]
    return part.reshape(1024, part.shape[-1])


def tall_tile(full, n):
    part = full[n // 2, 2 * (n % 2) : 2 * (n % 2) + 2]
    return part.reshape(256, part.shape[-1])


def dense_forward_kernel(
    x, gain_tile, docs, route, cot, w_qkv, w_out, w_up, w_down, exp_in, exp_out,
    hid, mixed, after, gains,
    o_n1, o_n2, o_act, o_dg, o_q, o_kv, o_kvo, o_wq, o_wo, o_wu, o_wd, o_cz, o_in0, o_out0, o_in1,
    sq, su, wq, wo, wu, wd, gmine, gother,
    n1, n2, cz, qb, kvb, kvo, mixs, act, dg, ps, pr, sendc, arrc,
    zs, zr, xs, xr, ys, yr, kvs, kvr, ks, kr, gs, gr, cs, cr, ss, sr, osem,
):
    at = Place()
    z, yh, c, col = at.z, at.yh, at.c, at.col
    line, plane = Ring(at, "z", zs, zr), Plane(at, cs, cr)
    own = Owners(at, xs, xr, ys, yr, ks, kr)
    bar = pltpu.get_barrier_semaphore()
    for d in (1, 2, 3):
        greet(bar, line.device(line.index(d)))
    greet(bar, at.other)
    greet(bar, at.swap_mate)
    plane.greet(bar)
    for part in range(3):
        sq[:, 256 * part : 256 * part + 256] = w_qkv[:, pl.ds(pl.multiple_of(1024 * part + 256 * z, 256), 256)]
    xhat = norm_parts(x[...].astype(jnp.float32))[0]
    pl.semaphore_wait(bar, 20)
    tile_at = pl.ds(pl.multiple_of(128 * col, 128), 128)

    def group(i):
        return lax.rem(col + i + 1, 8)

    def gain_copy(i):
        return remote(gain_tile, gmine.at[:, tile_at], gs.at[i], gr.at[i], (at.s, 2 * group(i) + c))

    def push_gain(i, carry):
        gain_copy(i).start()
        return carry

    lax.fori_loop(0, 7, push_gain, 0)
    gmine[:, tile_at] = gain_tile[...]
    half = pl.ds(pl.multiple_of(32 * yh, 32), 32)
    down_rows = w_down.at[pl.ds(pl.multiple_of(64 * z + 32 * yh, 32), 32)]
    sources = (sq.at[half], w_out.at[half], su.at[half], down_rows)
    fulls = (wq, wo, wu, wd)
    own.start(0, sources[0], wq)

    def wait_gain(i, carry):
        q = lax.rem(col + 7 - i, 8)
        dst = gmine.at[:, pl.ds(pl.multiple_of(128 * q, 128), 128)]
        remote(dst, dst, gs.at[i], gr.at[i], (at.s, 2 * q + c)).wait_recv()
        return carry

    lax.fori_loop(0, 7, wait_gain, 0)
    gain_core = remote(gmine, gother, gs.at[7], gr.at[7], at.other)
    gain_core.start()
    gain_core.wait_recv()
    vectors = gmine[...].astype(jnp.float32) + gother[...].astype(jnp.float32)
    gains[...] = vectors[0:8]
    n1[block(z), :] = (xhat * gains[0:1, :] + gains[2:3, :]).astype(jnp.bfloat16)
    line.spread(0, n1)
    own.step_x(0, wq)
    low = lax.broadcasted_iota(jnp.int32, (64, 128), 1) < 64
    odd = lax.rem(z, 2) == 1
    for n in range(8):
        first = 512 * n + 128 * lax.div(z, 2)
        a = w_up[:, pl.ds(pl.multiple_of(first, 128), 128)].astype(jnp.float32)
        b = w_up[:, pl.ds(pl.multiple_of(first + 256, 128), 128)].astype(jnp.float32)
        kept = jnp.where(low, a, pltpu.roll(b, 64, 1))
        moved = jnp.where(low, pltpu.roll(a, 64, 1), b)
        su[:, 128 * n : 128 * n + 128] = jnp.where(odd, moved, kept).astype(jnp.bfloat16)
    for phase in (1, 2, 3):
        own.start(phase, sources[phase], fulls[phase])
    left, right = placings(route[0:1, :])
    sendc[...] = to_pieces(left, right, cot[...])
    own.step_core(0, wq)
    plane.start(0, piece(sendc), piece(arrc))
    keep_piece(at, sendc, arrc)
    for phase in (1, 2, 3):
        own.step_x(phase, fulls[phase])
    own.wait(0, wq)

    def kv_copy(i, j):
        return remote(kvb.at[block(j)], kvo.at[block(j)], kvs.at[i], kvr.at[i], at.mate)

    def project_qkv(i, carry):
        d = order(i)
        j = line.index(d)

        @pl.when(i > 0)
        def _():
            line.arrived(0, d, n1)

        values = n1[block(j), :]
        kvb[block(j), 0:256] = nn(values, wide_tile(wq, slice(256, 512))).astype(jnp.bfloat16)
        kvb[block(j), 256:512] = nn(values, wide_tile(wq, slice(512, 768))).astype(jnp.bfloat16)
        kv_copy(i, j).start()
        qb[block(j), :] = nn(values, wide_tile(wq, slice(0, 256))).astype(jnp.bfloat16)
        return carry

    lax.fori_loop(0, 4, project_qkv, 0)
    plane.wait(0, piece(arrc))
    cz[block(z), :] = rows_of(arrc[...]).astype(jnp.bfloat16)
    line.spread(4, cz)
    own.step_core(1, wo)
    for i in range(4):
        kv_copy(i, line.index(order(i))).wait_recv()
    swaps = [
        remote(exp_in.at[0], o_in0, ss.at[0], sr.at[0], at.swap_mate),
        remote(exp_out.at[0], o_out0, ss.at[1], sr.at[1], at.swap_mate),
        remote(exp_in.at[1], o_in1, ss.at[2], sr.at[2], at.swap_mate),
    ]

    @pl.when(c != yh)
    def _():
        for swap in swaps:
            swap.start()

    for j in range(4):
        seen = masks(j, yh, docs)
        wide = slice(0, 128 * (j + 1))
        for p in range(2):
            lanes = slice(128 * p, 128 * p + 128)
            value_lanes = slice(256 + 128 * p, 384 + 128 * p)
            q = qb[128 * j : 128 * j + 128, lanes]
            keys = [kvb[wide, lanes], kvo[wide, lanes]]
            values = [kvb[wide, value_lanes], kvo[wide, value_lanes]]
            outs = []
            for h in range(2):
                probs = probabilities(only(head_lanes(h), q), keys, seen)
                outs.append(
                    nn(probs[0].astype(jnp.bfloat16), values[0]) + nn(probs[1].astype(jnp.bfloat16), values[1])
                )
            mixs[128 * j : 128 * j + 128, lanes] = jnp.where(head_lanes(0), outs[0], outs[1]).astype(jnp.bfloat16)
    my_lanes = pl.ds(pl.multiple_of(256 * z, 256), 256)

    def mix_copy(d):
        return line.copy(1, d, mixs.at[block(line.index(d))], mixed.at[:, my_lanes])

    for d in (1, 3, 2):
        mix_copy(d).start()
    mixed[:, my_lanes] = mixs[block(z), :]
    own.step_core(2, wu)
    own.step_core(3, wd)
    own.wait(1, wo)
    for d in (1, 3, 2):
        line.got(1, d, mixed.at[:, pl.ds(pl.multiple_of(256 * line.index(d), 256), 256)])
    for n in range(4):
        tile = slice(256 * n, 256 * n + 256)
        after[:, tile] = x[:, tile].astype(jnp.float32) + nn(mixed[...], wide_tile(wo, tile))
    xhat = norm_parts(after[...])[0]
    n2[block(z), :] = (xhat * gains[1:2, :] + gains[3:4, :]).astype(jnp.bfloat16)
    line.spread(2, n2)
    own.wait(2, wu)
    own.wait(3, wd)
    stores = [
        pltpu.make_async_copy(src, dst, osem.at[k])
        for k, (src, dst) in enumerate(
            [(n1, o_n1), (qb, o_q), (kvb, o_kv), (kvo, o_kvo), (wq, o_wq), (wo, o_wo), (wu, o_wu), (wd, o_wd)]
        )
    ]
    for store in stores:
        store.start()

    def feed(i, carry):
        d = order(i)
        j = line.index(d)

        @pl.when(i > 0)
        def _():
            line.arrived(2, d, n2)

        values = n2[block(j), :]
        for n in range(4):
            tile = slice(n * 256, (n + 1) * 256)
            acted, slope = gelu_parts(nn(values, wide_tile(wu, tile)))
            act[block(j), tile] = acted.astype(jnp.bfloat16)
            dg[block(j), tile] = slope
        values = act[block(j), :]
        for n in range(4):
            tile = slice(n * 256, (n + 1) * 256)
            ps[block(j), tile] = nn(values, wide_tile(wd, tile)).astype(jnp.bfloat16)

        @pl.when(i > 0)
        def _():
            line.give(3, d, ps, pr)

        return carry

    lax.fori_loop(0, 4, feed, 0)
    for d in (1, 3, 2):
        line.arrived(4, d, cz)
    late = [
        pltpu.make_async_copy(src, dst, osem.at[8 + k])
        for k, (src, dst) in enumerate([(n2, o_n2), (act, o_act), (dg, o_dg), (cz, o_cz)])
    ]
    for store in late:
        store.start()
    gain_core.wait_send()

    def sent_gain(i, carry):
        gain_copy(i).wait_send()
        return carry

    lax.fori_loop(0, 7, sent_gain, 0)
    for phase in range(4):
        own.sent(phase, sources[phase], fulls[phase])
    for i in range(4):
        kv_copy(i, line.index(order(i))).wait_send()
    line.sent(0, n1)
    for d in (1, 3, 2):
        mix_copy(d).wait_send()
    line.sent(2, n2)
    line.sent(4, cz)
    plane.sent(0, piece(sendc), piece(arrc))
    hid[...] = (after[...] + line.total(3, ps, pr)).astype(jnp.bfloat16)
    line.sent(3, ps)

    @pl.when(c != yh)
    def _():
        for swap in swaps:
            swap.wait()

    for store in stores + late:
        store.wait()


def dense_forward_call(x, gain_tile, docs, route, cot, w_qkv, w_out, w_up, w_down, exp_in, exp_out):
    bf, f32 = jnp.bfloat16, jnp.float32
    vmem, anywhere = pl.BlockSpec(memory_space=pltpu.VMEM), pl.BlockSpec(memory_space=pl.ANY)
    smem = pl.BlockSpec(memory_space=pltpu.SMEM)
    shape, V, dma = jax.ShapeDtypeStruct, pltpu.VMEM, pltpu.SemaphoreType.DMA
    line = [V((512, 1024), bf)]
    weight = [(2, 4, 2, 2, 32, 768)] + [(2, 4, 2, 2, 32, 1024)] * 3
    saved = [
        shape((512, 1024), bf), shape((512, 1024), bf), shape((512, 1024), bf), shape((512, 1024), f32),
        shape((512, 256), bf), shape((512, 512), bf), shape((512, 512), bf),
    ] + [shape(w, bf) for w in weight] + [
        shape((512, 1024), bf), shape((1024, 512), bf), shape((512, 1024), bf), shape((1024, 512), bf),
    ]
    return pl.pallas_call(
        dense_forward_kernel,
        out_shape=[shape((128, 1024), bf), shape((128, 1024), bf), shape((128, 1024), f32), shape((8, 1024), f32)]
        + saved,
        in_specs=[vmem, vmem, smem] + [vmem] * 6 + [anywhere, anywhere],
        out_specs=[vmem] * 4 + [anywhere] * len(saved),
        scratch_shapes=[
            V((64, 768), bf), V((64, 1024), bf), *[V(w, bf) for w in weight], V((16, 1024), bf), V((16, 1024), bf),
            *(line * 3), V((512, 256), bf), V((512, 512), bf), V((512, 512), bf), V((512, 256), bf),
            *line, V((512, 1024), f32), *(line * 2), V((256, 512), bf), V((256, 512), bf),
            dma((5, 3)), dma((5, 3)), dma((4, 3)), dma((4, 3)), dma((4, 3)), dma((4, 3)), dma((4,)), dma((4,)),
            dma((4,)), dma((4,)), dma((8,)), dma((8,)), dma((1, 15)), dma((1, 15)), dma((3,)), dma((3,)), dma((12,)),
        ],
        compiler_params=pltpu.CompilerParams(collective_id=2, has_side_effects=True, vmem_limit_bytes=60 << 20),
        name="dense_forward",
    )(x, gain_tile, docs, route, cot, w_qkv, w_out, w_up, w_down, exp_in, exp_out)


def expert_kernel(
    hid, route, vec, cz_h, exp_in, exp_out, in0, out0, in1,
    gh, vecg, mid, gate_out, o_ps, gin1, gout1, gin0, gout0,
    w_in, w_out, sendh, sendg, arrh, arrg, cz,
    e0, e1, g0, g1, ps0, ps1, pr0, pb0, pb1,
    act0, act1, dg0, dg1, gp0, gp1,
    arrived, base, xh0, xh1, sc, gates, dots, dots_in,
    ga_in, ga_out, sb_in, sb_out, rb_in, rb_out, vmine, vcore, vline, vsum, vswap,
    wsem, zs, zr, cs, cr, ks, kr, osem, bs, br, ss, sr, vs, vr,
):
    at = Place()
    z, yh, c, same = at.z, at.yh, at.c, at.same
    line, plane = Ring(at, "z", zs, zr), Plane(at, cs, cr)
    bar = pltpu.get_barrier_semaphore()
    plane.greet(bar)
    for d in (1, 2, 3):
        greet(bar, line.device(line.index(d)))
    greet(bar, at.other)
    greet(bar, at.swap_mate)
    low, high = slice(0, 512), slice(512, 1024)

    def slot(k, i, half):
        return w_in.at[k, :, half] if i == 0 else w_out.at[k, half, :]

    def load(k, i):
        return pltpu.make_async_copy((exp_in, exp_out)[i].at[k], slot(k, i, low), wsem.at[k, i])

    def swapped(k, i):
        return pltpu.make_async_copy((in0, out0)[i] if k == 0 else in1, slot(k, i, low), wsem.at[k, i])

    swap_out = remote(exp_out.at[1], slot(1, 1, low), ss.at[0], sr.at[0], at.swap_mate)

    def share(k, i):
        return remote(slot(k, i, low), slot(k, i, high), bs.at[k, i], br.at[k, i], at.other)

    def on_either(when_same, when_swapped):
        pl.when(same)(when_same)
        pl.when(jnp.logical_not(same))(when_swapped)

    load_c = pltpu.make_async_copy(cz_h, cz, wsem.at[2, 0])

    def begin_same():
        for k, i in ((0, 0), (0, 1), (1, 0), (1, 1)):
            load(k, i).start()

    def begin_swapped():
        for k, i in ((0, 0), (0, 1), (1, 0)):
            swapped(k, i).start()

    on_either(begin_same, begin_swapped)
    load_c.start()
    left, right = placings(route[0:1, :])
    sendh[...] = to_pieces(left, right, hid[...])
    pl.semaphore_wait(bar, 20)
    plane.start(0, piece(sendh), piece(arrh))
    keep_piece(at, sendh, arrh)

    def wait_loads(k, i):
        on_either(lambda: load(k, i).wait(), lambda: swapped(k, i).wait())
        share(k, i).start()

    pl.when(jnp.logical_not(same))(lambda: swap_out.start())
    wait_loads(0, 0)
    wait_loads(0, 1)
    wait_loads(1, 0)
    plane.wait(0, piece(arrh))
    gain = [vec[0:1, :], vec[1:2, :]]
    bias = [vec[2:3, :], vec[3:4, :]]
    rows = rows_of(arrh[...])
    arrived[...] = rows
    xhat, scale = norm_parts(rows)
    xh0[...] = xhat
    sc[0] = jnp.broadcast_to(scale, (128, 128))
    e0[block(z), :] = (xhat * gain[0] + bias[0]).astype(jnp.bfloat16)
    line.spread(0, e0)
    gating = jax.nn.sigmoid(split_sum(rows * vec[4:5, :]))
    gates[z] = jnp.broadcast_to(gating, (128, 128))

    def gate_copy(d):
        return line.copy(3, d, gates.at[z], gates.at[z])

    for d in (1, 3, 2):
        gate_copy(d).start()
    share(0, 0).wait_recv()
    share(0, 1).wait_recv()
    load_c.wait()

    def forward(k, j, rows_in, act, dg):
        values = rows_in[block(j), :]
        for n in range(4):
            tile = slice(n * 256, (n + 1) * 256)
            pre = nn(values, w_in[k, :, tile])
            acted, slope = gelu_parts(pre)
            act[block(j), tile] = acted.astype(jnp.bfloat16)
            dg[block(j), tile] = slope

    def project(k, j, act, part):
        values = act[block(j), :]
        for n in range(4):
            tile = slice(n * 256, (n + 1) * 256)
            part[block(j), tile] = nn(values, w_out[k, :, tile]).astype(jnp.bfloat16)

    def backward(k, j, grad, dg, gp, part):
        values = grad[block(j), :]
        for n in range(4):
            tile = slice(n * 256, (n + 1) * 256)
            slope = dg[block(j), tile] * nt(values, w_out[k, tile, :])
            gp[block(j), tile] = slope.astype(jnp.bfloat16)
        pres = gp[block(j), :]
        for n in range(4):
            tile = slice(n * 256, (n + 1) * 256)
            part[block(j), tile] = nt(pres, w_in[k, tile, :]).astype(jnp.bfloat16)

    def sub0(i, carry):
        d = order(i)
        j = line.index(d)

        @pl.when(i > 0)
        def _():
            line.arrived(0, d, e0)

        forward(0, j, e0, act0, dg0)
        project(0, j, act0, ps0)

        @pl.when(i > 0)
        def _():
            line.give(1, d, ps0, pr0)

        return carry

    lax.fori_loop(0, 4, sub0, 0)
    on_either(lambda: load(1, 1).wait(), lambda: swap_out.wait())
    share(1, 1).start()
    stream = arrived[...] + line.total(1, ps0, pr0)
    base[...] = stream
    xhat, scale = norm_parts(stream)
    xh1[...] = xhat
    sc[1] = jnp.broadcast_to(scale, (128, 128))
    e1[block(z), :] = (xhat * gain[1] + bias[1]).astype(jnp.bfloat16)
    line.spread(2, e1)
    gate = gates[z][:, 0:1]
    mid[...] = arrived[...] + gate * (base[...] - arrived[...])
    gate_out[...] = gates[z]
    line.sent(1, ps0)
    share(1, 0).wait_recv()
    share(1, 1).wait_recv()

    def sub1(i, carry):
        d = order(i)
        j = line.index(d)

        @pl.when(i > 0)
        def _():
            line.got(3, d, gates.at[j])

        g1[block(j), :] = (gates[j][:, 0:1] * cz[block(j), :].astype(jnp.float32)).astype(jnp.bfloat16)

        @pl.when(i > 0)
        def _():
            line.arrived(2, d, e1)

        forward(1, j, e1, act1, dg1)
        backward(1, j, g1, dg1, gp1, ps0)

        @pl.when(i > 0)
        def _():
            line.give(4, d, ps0, pb1)

        return carry

    lax.fori_loop(0, 4, sub1, 0)

    def second_part(i, carry):
        d = order(3 - i)
        j = line.index(d)
        project(1, j, act1, ps1)
        products = cz[block(j), :].astype(jnp.float32) * ps1[block(j), :].astype(jnp.float32)
        dots[j] = jnp.broadcast_to(split_sum(products), (128, 128))

        @pl.when(i < 3)
        def _():
            line.copy(5, d, dots.at[j], dots_in.at[z]).start()

        return carry

    lax.fori_loop(0, 4, second_part, 0)
    keep_ps = pltpu.make_async_copy(ps1, o_ps, wsem.at[2, 1])
    keep_ps.start()

    def weight_grads(k, rows_in, gp, act, grad):
        def one(n, carry):
            tile = pl.ds(pl.multiple_of(n * 256, 256), 256)
            tile_b = pl.ds(pl.multiple_of(n * 256 + 512, 256), 256)
            ga_out[k, tile, :] = tn(act[:, tile], grad[...])
            sb_out[k, tile, :] = tn(act[:, tile_b], grad[...]).astype(jnp.bfloat16)
            return carry

        lax.fori_loop(0, 2, one, 0)

        def two(n, carry):
            tile = pl.ds(pl.multiple_of(n * 256, 256), 256)
            ga_in[k, tile, :] = tn(rows_in[:, tile], gp[:, 0:512])
            sb_in[k, tile, :] = tn(rows_in[:, tile], gp[:, 512:1024]).astype(jnp.bfloat16)
            return carry

        lax.fori_loop(0, 4, two, 0)

    def swap(k, i):
        src, dst = ((sb_in, rb_in), (sb_out, rb_out))[i]
        return remote(src.at[k], dst.at[k], ks.at[k, i], kr.at[k, i], at.other)

    def join_cores(k):
        for i in range(2):
            swap(k, i).wait()
        sb_in[k] = (ga_in[k] + rb_in[k].astype(jnp.float32)).astype(jnp.bfloat16)
        sb_out[k] = (ga_out[k] + rb_out[k].astype(jnp.float32)).astype(jnp.bfloat16)

    weight_grads(1, e1, gp1, act1, g1)
    swap(1, 0).start()
    swap(1, 1).start()
    grad_normed = line.total(4, ps0, pb1)
    cot = cz[block(z), :].astype(jnp.float32)
    grad_stream = gates[z][:, 0:1] * cot
    grad_stream += norm_back(grad_normed, gain[1], xh1[...], sc[1][:, 0:1])
    g0[block(z), :] = grad_stream.astype(jnp.bfloat16)
    line.spread(6, g0)
    vmine[1:2, :] = jnp.sum(grad_normed * xh1[...], axis=0, keepdims=True)
    vmine[3:4, :] = jnp.sum(grad_normed, axis=0, keepdims=True)
    line.sent(4, ps0)
    grad_gating = split_sum(cot * (base[...] - arrived[...])) + dots[z][:, 0:1]
    for d in (1, 3, 2):
        line.got(5, d, dots_in.at[line.index(d)])
        grad_gating += dots_in[line.index(d)][:, 0:1]
    gate = gates[z][:, 0:1]
    grad_logit = gate * (1.0 - gate) * grad_gating
    vmine[4:5, :] = jnp.sum(grad_logit * arrived[...], axis=0, keepdims=True)
    base[...] = grad_stream + (1.0 - gate) * cot + grad_logit * vec[4:5, :]
    join_cores(1)
    kept = [
        pltpu.make_async_copy(sb_in.at[1], gin1, osem.at[1, 0]),
        pltpu.make_async_copy(sb_out.at[1], gout1, osem.at[1, 1]),
    ]
    given = [
        remote(sb_in.at[1], gin1, ss.at[1], sr.at[1], at.swap_mate),
        remote(sb_out.at[1], gout1, ss.at[2], sr.at[2], at.swap_mate),
    ]

    def begin(copies):
        for copy in copies:
            copy.start()

    def finish(copies):
        for copy in copies:
            copy.wait()

    on_either(lambda: begin(kept), lambda: begin(given))

    def sub0_back(i, carry):
        d = order(i)
        j = line.index(d)

        @pl.when(i > 0)
        def _():
            line.arrived(6, d, g0)

        backward(0, j, g0, dg0, gp0, ps0)

        @pl.when(i > 0)
        def _():
            line.give(7, d, ps0, pb0)

        return carry

    lax.fori_loop(0, 4, sub0_back, 0)
    weight_grads(0, e0, gp0, act0, g0)
    swap(0, 0).start()
    swap(0, 1).start()
    grad_normed = line.total(7, ps0, pb0)
    grad_stream = base[...] + norm_back(grad_normed, gain[0], xh0[...], sc[0][:, 0:1])
    sendg[...] = pieces_of(grad_stream)
    plane.start(1, piece(sendg), piece(arrg))
    keep_piece(at, sendg, arrg)
    vmine[0:1, :] = jnp.sum(grad_normed * xh0[...], axis=0, keepdims=True)
    vmine[2:3, :] = jnp.sum(grad_normed, axis=0, keepdims=True)
    vmine[5:8, :] = jnp.zeros((3, 1024), jnp.float32)
    give_core = remote(vmine, vcore, vs.at[0], vr.at[0], at.other)
    give_core.start()
    give_core.wait_recv()
    vline[z] = vmine[...] + vcore[...]

    def give_line(d):
        return line.copy(8, d, vline.at[z], vline.at[z])

    for d in (1, 3, 2):
        give_line(d).start()
    join_cores(0)
    stores = [
        pltpu.make_async_copy(sb_in.at[0], gin0, osem.at[0, 0]),
        pltpu.make_async_copy(sb_out.at[0], gout0, osem.at[0, 1]),
    ]
    begin(stores)
    plane.wait(1, piece(arrg))
    left, right = placings(route[0:1, :])
    gh[...] = from_pieces(left, right, arrg[...])
    for d in (1, 3, 2):
        line.got(8, d, vline.at[line.index(d)])
    vsum[...] = vline[0] + vline[1] + vline[2] + vline[3]
    give_mate = remote(vsum, vswap, vs.at[1], vr.at[1], at.swap_mate)
    pl.when(jnp.logical_not(same))(lambda: give_mate.start())
    give_core.wait_send()
    for d in (1, 3, 2):
        give_line(d).wait_send()
        gate_copy(d).wait_send()
        line.copy(5, d, dots.at[line.index(d)], dots_in.at[z]).wait_send()
    for k in (0, 1):
        for i in range(2):
            share(k, i).wait_send()
    line.sent(0, e0)
    line.sent(2, e1)
    line.sent(6, g0)
    line.sent(7, ps0)
    plane.sent(0, piece(sendh), piece(arrh))
    plane.sent(1, piece(sendg), piece(arrg))
    keep_ps.wait()
    finish(stores)
    on_either(lambda: finish(kept), lambda: finish(given))

    @pl.when(same)
    def _():
        vecg[...] = vsum[...]

    @pl.when(jnp.logical_not(same))
    def _():
        give_mate.wait()
        vecg[...] = vswap[...]


def expert_call(hid, route, vec, cz, exp_in, exp_out, in0, out0, in1):
    bf, f32 = jnp.bfloat16, jnp.float32
    vmem, anywhere = pl.BlockSpec(memory_space=pltpu.VMEM), pl.BlockSpec(memory_space=pl.ANY)
    shape, V, dma = jax.ShapeDtypeStruct, pltpu.VMEM, pltpu.SemaphoreType.DMA
    line, rows, pieces = [V((512, 1024), bf)], [V((128, 1024), f32)], [V((256, 512), bf)]
    wide, small = [V((512, 1024), f32)], [V((4, 128, 128), f32)]
    vectors = [V((8, 1024), f32)]
    return pl.pallas_call(
        expert_kernel,
        out_shape=(
            shape((128, 1024), bf), shape((8, 1024), f32), shape((128, 1024), f32), shape((128, 128), f32),
            shape((512, 1024), bf), shape((1024, 512), bf), shape((512, 1024), bf), shape((1024, 512), bf),
            shape((512, 1024), bf),
        ),
        in_specs=[vmem] * 3 + [anywhere] * 6,
        out_specs=tuple([vmem] * 4 + [anywhere] * 5),
        scratch_shapes=[
            V((2, 1024, 1024), bf), V((2, 1024, 1024), bf), *(pieces * 4), *line,
            *(line * 9), *(line * 2), *(wide * 2), *(line * 2),
            *(rows * 4), *(small * 4),
            V((2, 1024, 512), f32), V((2, 512, 1024), f32),
            V((2, 1024, 512), bf), V((2, 512, 1024), bf), V((2, 1024, 512), bf), V((2, 512, 1024), bf),
            *(vectors * 2), V((4, 8, 1024), f32), *(vectors * 2),
            dma((3, 2)), dma((9, 3)), dma((9, 3)), dma((2, 15)), dma((2, 15)), dma((2, 2)), dma((2, 2)), dma((2, 2)),
            dma((2, 2)), dma((2, 2)), dma((3,)), dma((3,)), dma((2,)), dma((2,)),
        ],
        compiler_params=pltpu.CompilerParams(collective_id=1, has_side_effects=True, vmem_limit_bytes=60 << 20),
        name="experts",
    )(hid, route, vec, cz, exp_in, exp_out, in0, out0, in1)


class Everyone:
    def __init__(self, at, send, recv):
        self.at, self.send, self.recv = at, send, recv

    def copy(self, phase, i, buf):
        own = buf.at[self.at.s]
        to = (lax.rem(self.at.s + i + 1, 8), self.at.f)
        return remote(own, own, self.send.at[phase, i], self.recv.at[phase, i], to)

    def start(self, phase, buf):
        for i in range(7):
            self.copy(phase, i, buf).start()

    def wait(self, phase, buf):
        for i in range(7):
            q = lax.rem(self.at.s + 7 - i, 8)
            dst = buf.at[q]
            remote(dst, dst, self.send.at[phase, i], self.recv.at[phase, i], (q, self.at.f)).wait_recv()

    def sent(self, phase, buf):
        for i in range(7):
            self.copy(phase, i, buf).wait_send()


def dense_backward_kernel(
    gh, x, after, docs, gains, mixed, route, mid, gate, n1_h, n2_h, act_h, dg_h, q_h, kv_h, kvo_h, wq_h, wo_h, wu_h,
    wd_h, ps_h, gin0, gout0,
    gx, gq, go, gu, gd, gvec, res, fin0, fout0,
    ghs, n1, n2, act, dg, gp, qb, kvb, kvo, wq, wo, wu, wd,
    ps, pr, ps2, pr2, ps3, pr3, gms, gm, dp, dkv, dkvo, kvs, kvr,
    md, mu, mo, mq, td, tu, to, tq, rd, ru, ro, rq, xd, xu, xo, sd, su, so, yd, yu, yo, rp, sendr, arrr,
    vmine, vcore, vplane, vline, outz, bd, bu, bo, bq,
    lsem, zs, zr, xs, xr, ys, yr, kvss, kvsr, ks, kr, cs, cr, qs, qr, ss, sr, vs, vr,
):
    at = Place()
    z, yh, c, col = at.z, at.yh, at.c, at.col
    line, ring_x, ring_y = Ring(at, "z", zs, zr), Ring(at, "x", xs, xr), Ring(at, "y", ys, yr)
    plane, everyone = Plane(at, cs, cr), Everyone(at, qs, qr)
    bar = pltpu.get_barrier_semaphore()
    plane.greet(bar)
    for d in (1, 2, 3):
        greet(bar, line.device(line.index(d)))
        greet(bar, (2 * line.index(d) + 1 - yh, at.f))
    greet(bar, at.other)
    greet(bar, at.swap_mate)
    loads = [
        pltpu.make_async_copy(src, dst, lsem.at[k])
        for k, (src, dst) in enumerate(
            [
                (wd_h, wd), (dg_h, dg), (wu_h, wu), (act_h, act), (n2_h, n2), (wo_h, wo), (ps_h, ps3), (q_h, qb),
                (kv_h, kvb), (kvo_h, kvo), (wq_h, wq), (n1_h, n1),
            ]
        )
    ]
    for load in loads:
        load.start()
    ghs[block(z), :] = gh[...]
    pl.semaphore_wait(bar, 23)
    line.spread(0, ghs)
    swaps = [
        remote(gin0, fin0, ss.at[0], sr.at[0], at.swap_mate),
        remote(gout0, fout0, ss.at[1], sr.at[1], at.swap_mate),
    ]
    keeps = [
        pltpu.make_async_copy(gin0, fin0, lsem.at[12]),
        pltpu.make_async_copy(gout0, fout0, lsem.at[13]),
    ]

    @pl.when(at.same)
    def _():
        for keep in keeps:
            keep.start()

    @pl.when(jnp.logical_not(at.same))
    def _():
        for swap in swaps:
            swap.start()

    for load in loads[:3]:
        load.wait()

    def feed(i, carry):
        d = order(i)
        j = line.index(d)

        @pl.when(i > 0)
        def _():
            line.arrived(0, d, ghs)

        values = ghs[block(j), :]
        for n in range(4):
            tile = slice(n * 256, (n + 1) * 256)
            gp[block(j), tile] = (dg[block(j), tile] * nt(values, tall_tile(wd, n))).astype(jnp.bfloat16)
        pres = gp[block(j), :]
        for n in range(4):
            tile = slice(n * 256, (n + 1) * 256)
            ps[block(j), tile] = nt(pres, tall_tile(wu, n)).astype(jnp.bfloat16)

        @pl.when(i > 0)
        def _():
            line.give(1, d, ps, pr)

        return carry

    lax.fori_loop(0, 4, feed, 0)
    for load in loads[3:7]:
        load.wait()

    def weight_grad(lhs, rhs, mine, theirs):
        def one(n, carry):
            rows = lhs[:, pl.ds(pl.multiple_of(n * 256, 256), 256)]
            grad = tn(rows, rhs[...])
            for half in range(2):
                first = grad[128 * half : 128 * half + 64].astype(jnp.bfloat16)
                second = grad[128 * half + 64 : 128 * half + 128].astype(jnp.bfloat16)
                here = lax.div(n, 2), 2 * lax.rem(n, 2) + half
                mine[here] = jnp.where(c == 0, first, second)
                theirs[here] = jnp.where(c == 0, second, first)
            return carry

        lax.fori_loop(0, 4, one, 0)

    def core_copy(phase, src, dst):
        return remote(src, dst, ks.at[phase], kr.at[phase], at.other)

    def join_cores(phase, mine, theirs, got):
        core_copy(phase, theirs, got).wait()

        def one(n, carry):
            here = lax.div(n, 4), lax.rem(n, 4)
            mine[here] = (mine[here].astype(jnp.float32) + got[here].astype(jnp.float32)).astype(jnp.bfloat16)
            return carry

        lax.fori_loop(0, 8, one, 0)

    def x_copy(phase, d, mine, dst):
        return ring_x.copy(phase, d, mine.at[:, ring_x.index(d)], dst.at[at.x])

    def y_copy(phase, d, part, dst):
        j = ring_y.index(d)
        src = part.at[lax.rem(j, 2), pl.ds(pl.multiple_of(32 * lax.div(j, 2), 32), 32)]
        return ring_y.copy(phase, d, src, dst.at[ring_y.pos])

    def to_x(phase, mine, dst):
        for d in (1, 3, 2):
            x_copy(phase, d, mine, dst).start()

    def to_y(phase, mine, got, part, dst):
        acc = mine[:, at.x].astype(jnp.float32)
        for d in (1, 3, 2):
            j = ring_x.index(d)
            ring_x.got(phase, d, got.at[j])
            acc += got[j].astype(jnp.float32)
        part[...] = acc.astype(jnp.bfloat16)
        for d in (1, 3, 2):
            y_copy(phase, d, part, dst).start()

    def y_total(phase, part, got):
        acc = part[at.yl, pl.ds(pl.multiple_of(32 * yh, 32), 32), :].astype(jnp.float32)
        for d in (1, 3, 2):
            j = ring_y.index(d)
            ring_y.got(phase, d, got.at[j])
            acc += got[j].astype(jnp.float32)
        return acc

    weight_grad(act, ghs, md, td)
    core_copy(0, td, rd).start()
    weight_grad(n2, gp, mu, tu)
    core_copy(1, tu, ru).start()
    join_cores(0, md, td, rd)
    to_x(0, md, xd)
    join_cores(1, mu, tu, ru)
    to_x(1, mu, xu)
    grad_normed = line.total(1, ps, pr)
    xhat, scale = norm_parts(after[...])
    vmine[1:2, :] = jnp.sum(grad_normed * xhat, axis=0, keepdims=True)
    vmine[3:4, :] = jnp.sum(grad_normed, axis=0, keepdims=True)
    grad_after = gh[...].astype(jnp.float32) + norm_back(grad_normed, gains[1:2, :], xhat, scale)
    gx[...] = grad_after
    grad_attn = grad_after.astype(jnp.bfloat16)
    for n in range(4):
        gms[:, 256 * n : 256 * n + 256] = nt(grad_attn, tall_tile(wo, n)).astype(jnp.bfloat16)

    def gm_copy(d):
        lanes = pl.ds(pl.multiple_of(256 * line.index(d), 256), 256)
        return line.copy(2, d, gms.at[:, lanes], gm.at[block(z)])

    for d in (1, 3, 2):
        gm_copy(d).start()
    gm[block(z), :] = gms[:, pl.ds(pl.multiple_of(256 * z, 256), 256)]
    for d in (1, 3, 2):
        line.give(6, d, ps3, pr3)
    gp[block(0), :] = grad_attn
    weight_grad(mixed, gp.at[block(0)], mo, to)
    core_copy(2, to, ro).start()
    to_y(0, md, xd, sd, yd)
    join_cores(2, mo, to, ro)
    to_x(2, mo, xo)
    for load in loads[7:]:
        load.wait()
    for d in (1, 3, 2):
        line.arrived(2, d, gm)
    dkv[...] = jnp.zeros_like(dkv)
    dkvo[...] = jnp.zeros_like(dkvo)

    def kv_copy(j):
        return remote(kvs.at[block(j)], kvr.at[block(j)], kvss.at[j], kvsr.at[j], at.mate)

    def attend_back(j):
        seen = masks(j, yh, docs)
        wide = slice(0, 128 * (j + 1))
        rows = slice(128 * j, 128 * j + 128)
        for p in range(2):
            lanes = slice(128 * p, 128 * p + 128)
            value_lanes = slice(256 + 128 * p, 384 + 128 * p)
            q, grad = qb[rows, lanes], gm[rows, lanes]
            keys = [kvb[wide, lanes], kvo[wide, lanes]]
            values = [kvb[wide, value_lanes], kvo[wide, value_lanes]]
            outs = []
            for h in range(2):
                q_h, grad_h = only(head_lanes(h), q), only(head_lanes(h), grad)
                probs = probabilities(q_h, keys, seen)
                back = [nt(grad_h, v) for v in values]
                dot = split_sum(probs[0] * back[0]) + split_sum(probs[1] * back[1])
                slopes = [(prob * (b - dot)).astype(jnp.bfloat16) for prob, b in zip(probs, back)]
                outs.append(nn(slopes[0], keys[0]) + nn(slopes[1], keys[1]))
                for k, acc in enumerate((dkv, dkvo)):
                    acc[wide, lanes] += tn(slopes[k], q_h) * 0.125
                    acc[wide, value_lanes] += tn(probs[k].astype(jnp.bfloat16), grad_h)
            dp[rows, lanes] = (jnp.where(head_lanes(0), outs[0], outs[1]) * 0.125).astype(jnp.bfloat16)
        kvs[rows, :] = dkvo[rows, :].astype(jnp.bfloat16)
        kv_copy(j).start()

    attend_back(3)
    attend_back(2)
    to_y(1, mu, xu, su, yu)
    attend_back(1)
    attend_back(0)
    sendr[...] = pieces_of(mid[...] + gate[:, 0:1] * line.total(6, ps3, pr3))
    plane.start(2, piece(sendr), piece(arrr))
    keep_piece(at, sendr, arrr)
    to_y(2, mo, xo, so, yo)
    for j in (3, 2, 1, 0):
        rows = slice(128 * j, 128 * j + 128)
        kv_copy(j).wait_recv()
        dp[rows, 256:768] = (dkv[rows, :] + kvr[rows, :].astype(jnp.float32)).astype(jnp.bfloat16)

    def last(i, carry):
        d = order(3 - i)
        j = line.index(d)
        values = dp[block(j), :]
        for n in range(4):
            tile = slice(n * 256, (n + 1) * 256)
            ps2[block(j), tile] = nt(values, tall_tile(wq, n)).astype(jnp.bfloat16)

        @pl.when(i < 3)
        def _():
            line.give(3, d, ps2, pr2)

        return carry

    lax.fori_loop(0, 4, last, 0)
    weight_grad(n1, dp, mq, tq)
    core_copy(3, tq, rq).start()
    bd[at.s] = y_total(0, sd, yd).astype(jnp.bfloat16)
    everyone.start(0, bd)
    join_cores(3, mq, tq, rq)

    def piece_q(q):
        return mq.at[lax.div(q, 8), lax.rem(lax.div(q, 2), 4), pl.ds(pl.multiple_of(32 * lax.rem(q, 2), 32), 32)]

    def slot_q(q):
        return rp.at[q]

    plane.start(0, piece_q, slot_q)
    rp[at.m] = mq[at.yl, at.x, pl.ds(pl.multiple_of(32 * yh, 32), 32), :]
    bu[at.s] = y_total(1, su, yu).astype(jnp.bfloat16)
    everyone.start(1, bu)
    total_out = y_total(2, so, yo)
    for n in range(4):
        outz[4 + n] = total_out[:, 256 * n : 256 * n + 256].astype(jnp.bfloat16)

    def out_copy(d):
        return line.copy(4, d, outz.at[4 + line.index(d)], outz.at[z])

    for d in (1, 3, 2):
        out_copy(d).start()
    grad_normed = line.total(3, ps2, pr2)
    xhat, scale = norm_parts(x[...].astype(jnp.float32))
    vmine[0:1, :] = jnp.sum(grad_normed * xhat, axis=0, keepdims=True)
    vmine[2:3, :] = jnp.sum(grad_normed, axis=0, keepdims=True)
    vmine[4:8, :] = jnp.zeros((4, 1024), jnp.float32)
    give_core = remote(vmine, vcore, vs.at[0], vr.at[0], at.other)
    give_core.start()
    gx[...] += norm_back(grad_normed, gains[0:1, :], xhat, scale)
    give_core.wait()
    vmine[...] += vcore[...]

    def tile_of(q):
        return vmine.at[:, pl.ds(pl.multiple_of(128 * lax.div(q, 2), 128), 128)]

    def slot_v(q):
        return vplane.at[q]

    plane.start(1, tile_of, slot_v)
    vplane[at.m] = vmine[:, pl.ds(pl.multiple_of(128 * col, 128), 128)]
    acc = outz[4 + z].astype(jnp.float32)
    for d in (1, 3, 2):
        line.got(4, d, outz.at[line.index(d)])
        acc += outz[line.index(d)].astype(jnp.float32)
    bo[at.s] = acc.astype(jnp.bfloat16)
    everyone.start(2, bo)
    plane.wait(0, slot_q)
    acc = rp[0].astype(jnp.float32)
    for q in range(1, 16):
        acc += rp[q].astype(jnp.float32)
    bq[at.s] = acc.astype(jnp.bfloat16)
    everyone.start(3, bq)
    plane.wait(1, slot_v)
    vline[z] = jnp.sum(vplane[...], axis=0)

    def vec_copy(d):
        return line.copy(5, d, vline.at[z], vline.at[z])

    for d in (1, 3, 2):
        vec_copy(d).start()
    plane.wait(2, piece(arrr))
    left, right = placings(route[0:1, :])
    res[...] = from_pieces(left, right, arrr[...])
    everyone.wait(0, bd)
    everyone.wait(1, bu)
    for zz in range(4):
        for half in range(2):
            gd[64 * zz + 32 * half : 64 * zz + 32 * half + 32, :] = bd[2 * zz + half].astype(jnp.float32)
    for half in range(2):
        rows = slice(32 * half, 32 * half + 32)
        lane = lax.broadcasted_iota(jnp.int32, (32, 128), 1) < 64
        for n in range(8):
            tile = slice(128 * n, 128 * n + 128)
            quarter = [bu[2 * zz + half, :, tile].astype(jnp.float32) for zz in range(4)]
            turned = [pltpu.roll(v, 64, 1) for v in quarter]
            first = 512 * n
            gu[rows, first : first + 128] = jnp.where(lane, quarter[0], turned[1])
            gu[rows, first + 128 : first + 256] = jnp.where(lane, quarter[2], turned[3])
            gu[rows, first + 256 : first + 384] = jnp.where(lane, turned[0], quarter[1])
            gu[rows, first + 384 : first + 512] = jnp.where(lane, turned[2], quarter[3])
    everyone.wait(2, bo)
    for zz in range(4):
        for half in range(2):
            go[32 * half : 32 * half + 32, 256 * zz : 256 * zz + 256] = bo[2 * zz + half].astype(jnp.float32)
    everyone.wait(3, bq)
    for zz in range(4):
        for half in range(2):
            for part in range(3):
                gq[32 * half : 32 * half + 32, 1024 * part + 256 * zz : 1024 * part + 256 * zz + 256] = bq[
                    2 * zz + half, :, 256 * part : 256 * part + 256
                ].astype(jnp.float32)
    for d in (1, 3, 2):
        line.got(5, d, vline.at[line.index(d)])
    gvec[...] = jnp.sum(vline[...], axis=0)
    line.sent(0, ghs)
    line.sent(1, ps)
    line.sent(3, ps2)
    line.sent(6, ps3)
    for d in (1, 3, 2):
        gm_copy(d).wait_send()
        out_copy(d).wait_send()
        vec_copy(d).wait_send()
        for phase, (mine, x_got, part, y_got) in enumerate(((md, xd, sd, yd), (mu, xu, su, yu), (mo, xo, so, yo))):
            x_copy(phase, d, mine, x_got).wait_send()
            y_copy(phase, d, part, y_got).wait_send()
    for j in range(4):
        kv_copy(j).wait_send()
    plane.sent(0, piece_q, slot_q)
    plane.sent(1, tile_of, slot_v)
    plane.sent(2, piece(sendr), piece(arrr))
    for phase, buf in enumerate((bd, bu, bo, bq)):
        everyone.sent(phase, buf)

    @pl.when(at.same)
    def _():
        for keep in keeps:
            keep.wait()

    @pl.when(jnp.logical_not(at.same))
    def _():
        for swap in swaps:
            swap.wait()


def dense_backward_call(gh, x, after, docs, gains, mixed, route, mid, gate, saved, ps, gin0, gout0):
    bf, f32 = jnp.bfloat16, jnp.float32
    vmem, anywhere = pl.BlockSpec(memory_space=pltpu.VMEM), pl.BlockSpec(memory_space=pl.ANY)
    smem = pl.BlockSpec(memory_space=pltpu.SMEM)
    shape, V, dma = jax.ShapeDtypeStruct, pltpu.VMEM, pltpu.SemaphoreType.DMA
    line, pieces = [V((512, 1024), bf)], [V((256, 512), bf)]
    wide, narrow = [V((2, 4, 64, 1024), bf)], [V((2, 4, 64, 768), bf)]
    return pl.pallas_call(
        dense_backward_kernel,
        out_shape=[
            shape((128, 1024), f32), shape((64, 3072), f32), shape((64, 1024), f32), shape((64, 4096), f32),
            shape((256, 1024), f32), shape((8, 128), f32), shape((128, 1024), bf), shape((1024, 512), bf),
            shape((512, 1024), bf),
        ],
        in_specs=[vmem, vmem, vmem, smem] + [vmem] * 5 + [anywhere] * 14,
        out_specs=[vmem] * 7 + [anywhere] * 2,
        scratch_shapes=[
            *(line * 4), V((512, 1024), f32), *line,
            V((512, 256), bf), V((512, 512), bf), V((512, 512), bf),
            V((2, 4, 2, 2, 32, 768), bf), *([V((2, 4, 2, 2, 32, 1024), bf)] * 3),
            *(line * 6),
            V((128, 1024), bf), V((512, 256), bf), V((512, 768), bf), V((512, 512), f32), V((512, 512), f32),
            V((512, 512), bf), V((512, 512), bf),
            *(wide * 3), *narrow, *(wide * 3), *narrow, *(wide * 3), *narrow,
            *([V((4, 2, 64, 1024), bf)] * 3), *([V((2, 64, 1024), bf)] * 3), *([V((4, 32, 1024), bf)] * 3),
            V((16, 32, 768), bf), *(pieces * 2),
            V((8, 1024), f32), V((8, 1024), f32), V((16, 8, 128), f32), V((4, 8, 128), f32),
            V((8, 32, 256), bf),
            V((8, 32, 1024), bf), V((8, 32, 1024), bf), V((8, 32, 256), bf), V((8, 32, 768), bf),
            dma((14,)), dma((7, 3)), dma((7, 3)), dma((3, 3)), dma((3, 3)), dma((3, 3)), dma((3, 3)), dma((4,)),
            dma((4,)), dma((4,)), dma((4,)), dma((3, 15)), dma((3, 15)), dma((4, 7)), dma((4, 7)), dma((2,)),
            dma((2,)), dma((1,)), dma((1,)),
        ],
        compiler_params=pltpu.CompilerParams(collective_id=3, has_side_effects=True, vmem_limit_bytes=62 << 20),
        name="dense_backward",
    )(gh, x, after, docs, gains, mixed, route, mid, gate, *saved, ps, gin0, gout0)


def on_device(
    inputs,
    doc_starts,
    route,
    norm_gain,
    norm_bias,
    w_qkv,
    w_out,
    w_up,
    w_down,
    exp_gain,
    exp_bias,
    exp_in,
    exp_out,
    centroid,
    cotangent,
):
    tok_rows, width = 128, 1024
    x = inputs.reshape(tok_rows, width)
    cot = cotangent.reshape(tok_rows, width)
    slots = route.reshape(1, tok_rows)
    core = lax.rem(lax.axis_index("fsdp"), 2)
    mine = lax.rem(lax.axis_index("seq"), 2) == core
    share = jnp.pad(jnp.concatenate([norm_gain, norm_bias]), ((0, 12), (0, 0)))
    none = jnp.zeros_like(share)
    gain_tile = jnp.where(core == 0, jnp.concatenate([share, none], 1), jnp.concatenate([none, share], 1))
    core_pairs = [(i, i + 1 - 2 * (i % 2)) for i in range(128)]
    vec = jnp.concatenate([exp_gain[0], exp_bias[0], centroid], axis=0)
    vec = jnp.where(mine, vec, lax.ppermute(vec, ("seq", "fsdp"), core_pairs)).astype(jnp.float32)
    vec = jnp.pad(vec, ((0, 3), (0, 0)))
    hidden, mixed, after, gains, *saved, cz, in0, out0, in1 = dense_forward_call(
        x, gain_tile, doc_starts, slots, cot, w_qkv, w_out, w_up, w_down, exp_in[0], exp_out[0]
    )
    grad_hidden, vec_grads, mid, gate, part, grad_in1, grad_out1, grad_in0, grad_out0 = expert_call(
        hidden, slots, vec, cz, exp_in[0], exp_out[0], in0, out0, in1
    )
    grad_x, grad_qkv, grad_wo, grad_up, grad_down, norm_grads, result, grad_in0, grad_out0 = dense_backward_call(
        grad_hidden, x, after, doc_starts, gains, mixed, slots, mid, gate, saved, part, grad_in0, grad_out0
    )
    norm_grads = jnp.where(core == 0, norm_grads[:4, :64], norm_grads[:4, 64:])
    return (
        result[None],
        grad_x[None],
        norm_grads[0:2],
        norm_grads[2:4],
        grad_qkv,
        grad_wo,
        grad_up,
        grad_down,
        vec_grads[None, 0:2],
        vec_grads[None, 2:4],
        jnp.stack([grad_in0, grad_in1]).astype(jnp.float32)[None],
        jnp.stack([grad_out0, grad_out1]).astype(jnp.float32)[None],
        vec_grads[4:5],
    )


def solution(mesh):
    in_specs = (
        P("fsdp", "seq", None),
        P("fsdp", None),
        P("fsdp", "seq", None),
        P(None, "fsdp"),
        P(None, "fsdp"),
        P("fsdp", None),
        P("fsdp", None),
        P("fsdp", None),
        P("fsdp", None),
        P("fsdp", None, None),
        P("fsdp", None, None),
        P("fsdp", None, None, "seq"),
        P("fsdp", None, "seq", None),
        P("fsdp", None),
        P("fsdp", "seq", None),
    )
    out_specs = (
        P("fsdp", "seq", None),
        P("fsdp", "seq", None),
        P(None, "fsdp"),
        P(None, "fsdp"),
        P("fsdp", None),
        P("fsdp", None),
        P("fsdp", None),
        P("fsdp", None),
        P("fsdp", None, None),
        P("fsdp", None, None),
        P("fsdp", None, None, "seq"),
        P("fsdp", None, "seq", None),
        P("fsdp", None),
    )
    return jax.shard_map(
        on_device, mesh=mesh, in_specs=in_specs, out_specs=out_specs, check_vma=False
    )
```

time: 1180 us -> 331 us (0.28)
  waiting for transfers between devices: 674 us -> 0.01 us
  Pallas kernels: 123 us -> 310 us
  starting transfers between devices: 97.1 us -> 0.09 us
  matrix products: 86.5 us -> 0 us
  blocking collectives: 76.2 us -> 0 us
  local copies, waits for them, and re-layouts: 54 us -> 8.43 us
  other arithmetic: 41.4 us -> 9.53 us
  between operations: 14.9 us -> 0.75 us
    unnamed x19 -> x0, waiting for transfers between devices: 232 us -> none
    reduce_scatter x4 -> x0, waiting for transfers between devices: 202 us -> none  [the longest x1 75.4 us: on_device(): lax.psum_scatter(dense_terms[4].astype(jnp.bfloat16), 'fsdp', scatter_dim...]
    pallas_call x1 -> x3, Pallas kernels: 123 us -> 310 us  [the longest x1 111 us: expert_call(): pl.pallas_call(expert_kernel, out_shape=(shape((128, 1024), bf), shape((8...]
    all_gather x6 -> x0, waiting for transfers between devices: 180 us -> none  [the longest x1 51.9 us: on_device(): lax.all_gather(w_up, 'fsdp', axis=0, tiled=True)]
    ppermute x8 -> x1, starting transfers between devices: 96.3 us -> 0.09 us  [on_device(): lax.ppermute(vec, ('seq', 'fsdp'), core_pairs)]
    dot_general x18 -> x0, matrix products: 86.5 us -> none  [the longest x1 7.05 us: on_device(): jnp.einsum('rd,fd->rf', grad_hidden, down_weight, preferred_element_type=...]
    psum x1 -> x0, waiting for transfers between devices: 59.9 us -> none  [on_device(): lax.psum(shard_qkv.astype(jnp.bfloat16), 'seq').astype(jnp.float32)]
    unnamed x59 -> x30, local copies, waits for them, and re-layouts: 49.2 us -> 5.06 us
  transfers between devices with their start and end apart: 23 -> 1, of which waited for: 14 -> 0; matrix products, arithmetic and copies ran while one was open for 11% -> 0% of each run, Pallas kernels for 0% -> 28%
where the time goes in v3:
time: 331 us; the launch traced here: 329 us
  Pallas kernels  310 us (94%)
  other arithmetic  9.53 us (3%)
  local copies, waits for them, and re-layouts  8.43 us (3%)
    pallas_call x1, Pallas kernels, expert_call(): pl.pallas_call(expert_kernel, out_shape=(shape((128, 1024), bf), shape((8...  111 us
    pallas_call x1, Pallas kernels, dense_backward_call(): pl.pallas_call(dense_backward_kernel, out_shape=[shape((128, 1024), f32),...  107 us
    pallas_call x1, Pallas kernels, dense_forward_call(): pl.pallas_call(dense_forward_kernel, out_shape=[shape((128, 1024), bf), s...  91.8 us
  transfers between devices with their start and end apart: 1, of which 0 were waited for; matrix products, arithmetic and copies ran while one was open for 0% of the time, Pallas kernels for 28%

profile of v3, /device:TPU:4, one launch (start us, length us, event | category | flops | bytes accessed | tf_op | source)
XLA Modules:
  0.0 329.3 jit_solution(1691925733008945574)
XLA Ops:
  0.6 0.7 pad_maximum_fusion
  1.4 0.1 collective-permute-start
  1.5 0.7 fusion.2
  2.2 0.7 pad_select_fusion.gain_tile
  2.8 91.8 %dense_forward.1 = (bf16[128,1024]{1,0:T(8,128)(2,1)}, bf16[128,1024]{1,0:T(8,128)(2,1)}, f32[128,1024]{1,0:T(8,128)}, f32[8,1024]{1,0:T(8,128)}, bf16[512,1024]...) custom-call(bf16[128,1024]{1,0:T(8,128)(2,1)} %bitcast.21, ...), custom_call_target="tpu_custom_call" | custom-call | tf_op jit(solution)/shard_map/dense_forward/pallas_call | solution.py:543
  94.7 0.0 collective-permute-done
  94.7 0.0 copy-done.9
  94.7 0.0 copy-done.10
  94.7 0.0 copy-done.11
  94.7 0.6 pad_convert_fusion.vec
  95.4 111.4 %experts.1 = (bf16[128,1024]{1,0:T(8,128)(2,1)}, f32[8,1024]{1,0:T(8,128)}, f32[128,1024]{1,0:T(8,128)}, f32[128,128]{1,0:T(8,128)}, bf16[512,1024]{1,0:T(8,128)...) custom-call(bf16[128,1024]{1,0:T(8,128)(2,1)} %get-tuple-element.50., ...), custom_call_target="tpu_custom_call" | custom-call | tf_op jit(solution)/shard_map/experts/pallas_call | solution.py:905
  206.8 1.4 slice.27
  208.2 1.4 slice_bitcast_fusion
  209.6 107.2 %dense_backward.1 = (f32[128,1024]{1,0:T(8,128)}, f32[64,3072]{1,0:T(8,128)}, f32[64,1024]{1,0:T(8,128)}, f32[64,4096]{1,0:T(8,128)}, f32[256,1024]{1,0:T(8,128)...) custom-call(bf16[128,1024]{1,0:T(8,128)(2,1)} %get-tuple-element.55.gh, ...), custom_call_target="tpu_custom_call" | custom-call | tf_op jit(solution)/shard_map/dense_backward/pallas_call | solution.py:1326
  316.8 0.8 slice_select_fusion
  317.7 0.6 fusion.3
  318.2 0.0 copy-done.3
  318.3 3.7 %maximum_convert_fusion = f32[1,2,1024,512]{3,2,1,0:T(8,128)} fusion(bf16[1,1,1024,512]{3,2,1,0:T(8,128)(2,1)S(1)} %bitcast.24, bf16[1,1,1024,512]{3,2,1,0:T(8,128)(2,1)} %bitcast.26), kind=kLoop, calls=%fused_computation | loop fusion | flops 2097152 | bytes 6291456 | tf_op jit(solution)/shard_map/convert_element_type | solution.py:1408
  321.9 0.0 copy-done.2
  321.9 0.0 copy-done.4
  321.9 0.0 copy-start.5
  321.9 2.3 maximum_convert_fusion.1
  324.2 0.0 copy-done.8
  324.2 0.7 copy.34
  324.9 0.0 copy-done.6
  324.9 0.8 copy.35
  325.7 0.0 copy-done.5
  325.7 0.9 copy.36
  326.6 0.0 copy-done.7
  326.6 0.7 copy.37
  327.3 1.0 copy.38
  328.3 1.0 copy.39
  (14 shorter events, 0.0 us)
Async XLA Ops:
  1.4 93.3 %collective-permute-start = (bf16[5,1024]{1,0:T(8,128)(2,1)S(1)}, bf16[5,1024]{1,0:T(8,128)(2,1)S(1)}, u32[]{:S(2)}, u32[]{:S(2)}) collective-permute-start(bf16[5,1024]{1,0:T(8,128)(2,1)S(1)} %pad_maximum_fusion), channel_id=1, source_target_pairs={{0,1},{1,0},{2,3},{3,2},{4,5},{5,4},{6,7},{7,6},{8,9},{9,8},{10,11... | collective-permute-start | bytes 30728 | tf_op jit(solution)/shard_map/ppermute | solution.py:1385
  2.8 91.8 %copy-start.9 = (bf16[1,1024]{1,0:T(2,128)(2,1)S(1)}, bf16[1,1024]{1,0:T(2,128)(2,1)}, u32[]{:S(2)}) copy-start(bf16[1,1024]{1,0:T(2,128)(2,1)} %param.28) | copy-start | bytes 6148
  2.8 91.8 %copy-start.10 = (bf16[1,2,1024]{2,1,0:T(2,128)(2,1)S(1)}, bf16[1,2,1024]{2,1,0:T(2,128)(2,1)}, u32[]{:S(2)}) copy-start(bf16[1,2,1024]{2,1,0:T(2,128)(2,1)} %param.25) | copy-start | bytes 12292
  2.8 91.8 %copy-start.11 = (bf16[1,2,1024]{2,1,0:T(2,128)(2,1)S(1)}, bf16[1,2,1024]{2,1,0:T(2,128)(2,1)}, u32[]{:S(2)}) copy-start(bf16[1,2,1024]{2,1,0:T(2,128)(2,1)} %param.24) | copy-start | bytes 12292
  209.6 108.6 %copy-start.3 = (bf16[1024,512]{1,0:T(8,128)(2,1)S(1)}, bf16[1024,512]{1,0:T(8,128)(2,1)}, u32[]{:S(2)}) copy-start(bf16[1024,512]{1,0:T(8,128)(2,1)} %get-tuple-element.84) | copy-start | bytes 3145732
  318.2 3.7 %copy-start.2 = (bf16[512,1024]{1,0:T(8,128)(2,1)S(1)}, bf16[512,1024]{1,0:T(8,128)(2,1)}, u32[]{:S(2)}) copy-start(bf16[512,1024]{1,0:T(8,128)(2,1)} %get-tuple-element.86) | copy-start | bytes 3145732
  318.2 3.7 %copy-start.4 = (bf16[512,1024]{1,0:T(8,128)(2,1)S(1)}, bf16[512,1024]{1,0:T(8,128)(2,1)}, u32[]{:S(2)}) copy-start(bf16[512,1024]{1,0:T(8,128)(2,1)} %get-tuple-element.85) | copy-start | bytes 3145732
  321.9 2.3 copy-start.8
  321.9 3.0 copy-start.6
  321.9 3.8 %copy-start.5 = (f32[64,3072]{1,0:T(8,128)S(1)}, f32[64,3072]{1,0:T(8,128)}, u32[]{:S(2)}) copy-start(f32[64,3072]{1,0:T(8,128)} %get-tuple-element.108) | copy-start | bytes 2359300
  324.2 2.4 copy-start.7
  324.2 3.1 copy-start.1
  325.7 2.6 copy-start

commit v4 on v3

--- a/solution.py
+++ b/solution.py
@@ -110,6 +110,46 @@
         for d in (1, 3, 2):
             self.copy(phase, d, own, own).start()
 
+    def near(self, phase, d, buf):
+        own = buf.at[block(self.pos)]
+        return self.copy(phase, d, own, own)
+
+    def half(self, buf, d, upper):
+        return buf.at[pl.ds(pl.multiple_of(128 * self.index(d) + 64 * upper, 64), 64)]
+
+    def onward(self, phase, buf, upper):
+        rows = self.half(buf, 3 if upper else 1, upper)
+        slot = 3 if upper else 1
+        to = self.device(self.index(1 if upper else 3))
+        return remote(rows, rows, self.send.at[phase, slot], self.recv.at[phase, slot], to)
+
+    def begin(self, phase, buf):
+        for d in (1, 3):
+            self.near(phase, d, buf).start()
+
+    def relay(self, phase, buf):
+        for d in (1, 3):
+            self.arrived(phase, d, buf)
+        for upper in (0, 1):
+            self.onward(phase, buf, upper).start()
+
+    def far(self, phase, buf):
+        for upper in (0, 1):
+            slot = 3 if upper else 1
+            rows = self.half(buf, 2, upper)
+            to = self.device(self.index(1 if upper else 3))
+            remote(rows, rows, self.send.at[phase, slot], self.recv.at[phase, slot], to).wait_recv()
+
+    def ready(self, phase, i, buf):
+        pl.when(i == 1)(lambda: self.relay(phase, buf))
+        pl.when(i == 3)(lambda: self.far(phase, buf))
+
+    def sent_all(self, phase, buf):
+        for d in (1, 3):
+            self.near(phase, d, buf).wait_send()
+        for upper in (0, 1):
+            self.onward(phase, buf, upper).wait_send()
+
     def arrived(self, phase, d, buf):
         self.got(phase, d, buf.at[block(self.index(d))])
 
@@ -211,51 +251,59 @@
     return jnp.concatenate([left, right], axis=1).reshape(256, 512).astype(jnp.bfloat16)
 
 
-class Owners:
-    def __init__(self, at, xs, xr, ys, yr, ks, kr):
-        self.at = at
-        self.ring_x, self.ring_y = Ring(at, "x", xs, xr), Ring(at, "y", ys, yr)
+class Gather:
+    def __init__(self, at, phase, first, src, full, xs, xr, ys, yr, ks, kr):
+        self.at, self.phase, self.src, self.full = at, phase, src, full
+        self.x_first = first == "x"
+        self.rings = [Ring(at, "y", ys, yr), Ring(at, "x", xs, xr)]
+        if self.x_first:
+            self.rings.reverse()
         self.ks, self.kr = ks, kr
 
-    def along_y(self, phase, d, src, full):
+    def pushed(self, d):
         at = self.at
-        return self.ring_y.copy(phase, d, src, full.at[at.yl, at.x, at.c, at.yh])
-
-    def along_x(self, phase, d, full):
-        own = full.at[:, self.at.x, self.at.c]
-        return self.ring_x.copy(phase, d, own, own)
-
-    def core(self, phase, full, c):
-        half = full.at[:, :, c]
-        return remote(half, half, self.ks.at[phase], self.kr.at[phase], self.at.other)
-
-    def start(self, phase, src, full):
+        return self.rings[0].copy(self.phase, d, self.src, self.full.at[at.yl, at.x, at.c, at.yh])
+
+    def passed(self, d):
+        at = self.at
+        own = self.full.at[at.yl, :, at.c, at.yh] if self.x_first else self.full.at[:, at.x, at.c]
+        return self.rings[1].copy(self.phase, d, own, own)
+
+    def core(self, c):
+        half = self.full.at[:, :, c]
+        return remote(half, half, self.ks.at[self.phase], self.kr.at[self.phase], self.at.other)
+
+    def start(self):
         at = self.at
         for d in (1, 3, 2):
-            self.along_y(phase, d, src, full).start()
-        full[at.yl, at.x, at.c, at.yh] = src[...]
-
-    def step_x(self, phase, full):
-        at = self.at
+            self.pushed(d).start()
+        self.full[at.yl, at.x, at.c, at.yh] = self.src[...]
+
+    def turn(self):
+        at, full = self.at, self.full
         for d in (1, 3, 2):
-            j = self.ring_y.index(d)
-            self.ring_y.got(phase, d, full.at[lax.rem(j, 2), at.x, at.c, lax.div(j, 2)])
+            j = self.rings[0].index(d)
+            dst = full.at[at.yl, j, at.c, at.yh] if self.x_first else full.at[lax.rem(j, 2), at.x, at.c, lax.div(j, 2)]
+            self.rings[0].got(self.phase, d, dst)
         for d in (1, 3, 2):
-            self.along_x(phase, d, full).start()
-
-    def step_core(self, phase, full):
+            self.passed(d).start()
+
+    def share(self):
+        at, full = self.at, self.full
         for d in (1, 3, 2):
-            self.ring_x.got(phase, d, full.at[:, self.ring_x.index(d), self.at.c])
-        self.core(phase, full, self.at.c).start()
-
-    def wait(self, phase, full):
-        self.core(phase, full, 1 - self.at.c).wait_recv()
-
-    def sent(self, phase, src, full):
+            j = self.rings[1].index(d)
+            dst = full.at[lax.rem(j, 2), :, at.c, lax.div(j, 2)] if self.x_first else full.at[:, j, at.c]
+            self.rings[1].got(self.phase, d, dst)
+        self.core(at.c).start()
+
+    def wait(self):
+        self.core(1 - self.at.c).wait_recv()
+
+    def sent(self):
         for d in (1, 3, 2):
-            self.along_y(phase, d, src, full).wait_send()
-            self.along_x(phase, d, full).wait_send()
-        self.core(phase, full, self.at.c).wait_send()
+            self.pushed(d).wait_send()
+            self.passed(d).wait_send()
+        self.core(self.at.c).wait_send()
 
 
 def labels(position, first, second):
@@ -306,62 +354,56 @@
 
 
 def dense_forward_kernel(
-    x, gain_tile, docs, route, cot, w_qkv, w_out, w_up, w_down, exp_in, exp_out,
+    x, gain, bias, docs, route, cot, w_qkv, w_out, w_up, w_down, exp_in, exp_out,
     hid, mixed, after, gains,
-    o_n1, o_n2, o_act, o_dg, o_q, o_kv, o_kvo, o_wq, o_wo, o_wu, o_wd, o_cz, o_in0, o_out0, o_in1,
-    sq, su, wq, wo, wu, wd, gmine, gother,
-    n1, n2, cz, qb, kvb, kvo, mixs, act, dg, ps, pr, sendc, arrc,
+    o_x, o_n1, o_n2, o_act, o_dg, o_q, o_kv, o_kvo, o_wq, o_wo, o_wu, o_wd, o_cz, o_in0, o_out0, o_in1,
+    sq, su, wq, wo, wu, wd, gtile, gmine, gother,
+    xa, n1, n2, cz, qb, kvb, kvo, mixs, act, dg, ps, pr, sendc, arrc,
     zs, zr, xs, xr, ys, yr, kvs, kvr, ks, kr, gs, gr, cs, cr, ss, sr, osem,
 ):
     at = Place()
     z, yh, c, col = at.z, at.yh, at.c, at.col
     line, plane = Ring(at, "z", zs, zr), Plane(at, cs, cr)
-    own = Owners(at, xs, xr, ys, yr, ks, kr)
     bar = pltpu.get_barrier_semaphore()
     for d in (1, 2, 3):
         greet(bar, line.device(line.index(d)))
     greet(bar, at.other)
     greet(bar, at.swap_mate)
     plane.greet(bar)
+    xa[block(z), :] = x[...]
     for part in range(3):
         sq[:, 256 * part : 256 * part + 256] = w_qkv[:, pl.ds(pl.multiple_of(1024 * part + 256 * z, 256), 256)]
-    xhat = norm_parts(x[...].astype(jnp.float32))[0]
+    gtile[...] = jnp.zeros_like(gtile)
+    for k, ref in enumerate((gain, bias)):
+        values = ref[...].astype(jnp.float32)
+        none = jnp.zeros_like(values)
+        here = jnp.where(c == 0, jnp.concatenate([values, none], 1), jnp.concatenate([none, values], 1))
+        gtile[2 * k : 2 * k + 2, :] = here
+    half = pl.ds(pl.multiple_of(32 * yh, 32), 32)
+    down_rows = w_down.at[pl.ds(pl.multiple_of(64 * z + 32 * yh, 32), 32)]
+    sems = (xs, xr, ys, yr, ks, kr)
+    left_q, right_q = (wq.at[:, :, :, :, :, 0:384], wq.at[:, :, :, :, :, 384:768])
+    qkv_a = Gather(at, 0, "y", sq.at[half, 0:384], left_q, *sems)
+    qkv_b = Gather(at, 1, "x", sq.at[half, 384:768], right_q, *sems)
+    out = Gather(at, 2, "y", w_out.at[half], wo, *sems)
+    up = Gather(at, 3, "y", su.at[half], wu, *sems)
+    down = Gather(at, 4, "x", down_rows, wd, *sems)
     pl.semaphore_wait(bar, 20)
+    line.begin(0, xa)
     tile_at = pl.ds(pl.multiple_of(128 * col, 128), 128)
 
-    def group(i):
-        return lax.rem(col + i + 1, 8)
-
     def gain_copy(i):
-        return remote(gain_tile, gmine.at[:, tile_at], gs.at[i], gr.at[i], (at.s, 2 * group(i) + c))
+        to = (at.s, 2 * lax.rem(col + i + 1, 8) + c)
+        return remote(gtile, gmine.at[:, tile_at], gs.at[i], gr.at[i], to)
 
     def push_gain(i, carry):
         gain_copy(i).start()
         return carry
 
     lax.fori_loop(0, 7, push_gain, 0)
-    gmine[:, tile_at] = gain_tile[...]
-    half = pl.ds(pl.multiple_of(32 * yh, 32), 32)
-    down_rows = w_down.at[pl.ds(pl.multiple_of(64 * z + 32 * yh, 32), 32)]
-    sources = (sq.at[half], w_out.at[half], su.at[half], down_rows)
-    fulls = (wq, wo, wu, wd)
-    own.start(0, sources[0], wq)
-
-    def wait_gain(i, carry):
-        q = lax.rem(col + 7 - i, 8)
-        dst = gmine.at[:, pl.ds(pl.multiple_of(128 * q, 128), 128)]
-        remote(dst, dst, gs.at[i], gr.at[i], (at.s, 2 * q + c)).wait_recv()
-        return carry
-
-    lax.fori_loop(0, 7, wait_gain, 0)
-    gain_core = remote(gmine, gother, gs.at[7], gr.at[7], at.other)
-    gain_core.start()
-    gain_core.wait_recv()
-    vectors = gmine[...].astype(jnp.float32) + gother[...].astype(jnp.float32)
-    gains[...] = vectors[0:8]
-    n1[block(z), :] = (xhat * gains[0:1, :] + gains[2:3, :]).astype(jnp.bfloat16)
-    line.spread(0, n1)
-    own.step_x(0, wq)
+    gmine[:, tile_at] = gtile[...]
+    qkv_a.start()
+    qkv_b.start()
     low = lax.broadcasted_iota(jnp.int32, (64, 128), 1) < 64
     odd = lax.rem(z, 2) == 1
     for n in range(8):
@@ -371,27 +413,47 @@
         kept = jnp.where(low, a, pltpu.roll(b, 64, 1))
         moved = jnp.where(low, pltpu.roll(a, 64, 1), b)
         su[:, 128 * n : 128 * n + 128] = jnp.where(odd, moved, kept).astype(jnp.bfloat16)
-    for phase in (1, 2, 3):
-        own.start(phase, sources[phase], fulls[phase])
+    out.start()
+    qkv_a.turn()
+    qkv_b.turn()
+    down.start()
+    up.start()
+
+    def wait_gain(i, carry):
+        q = lax.rem(col + 7 - i, 8)
+        dst = gmine.at[:, pl.ds(pl.multiple_of(128 * q, 128), 128)]
+        remote(dst, dst, gs.at[i], gr.at[i], (at.s, 2 * q + c)).wait_recv()
+        return carry
+
+    lax.fori_loop(0, 7, wait_gain, 0)
+    gain_core = remote(gmine, gother, gs.at[7], gr.at[7], at.other)
+    gain_core.start()
     left, right = placings(route[0:1, :])
     sendc[...] = to_pieces(left, right, cot[...])
-    own.step_core(0, wq)
+    line.relay(0, xa)
+    out.turn()
+    down.turn()
+    up.turn()
     plane.start(0, piece(sendc), piece(arrc))
     keep_piece(at, sendc, arrc)
-    for phase in (1, 2, 3):
-        own.step_x(phase, fulls[phase])
-    own.wait(0, wq)
+    gain_core.wait_recv()
+    gains[...] = gmine[...] + gother[...]
+    qkv_a.share()
+    qkv_b.share()
 
     def kv_copy(i, j):
         return remote(kvb.at[block(j)], kvo.at[block(j)], kvs.at[i], kvr.at[i], at.mate)
 
     def project_qkv(i, carry):
-        d = order(i)
-        j = line.index(d)
-
-        @pl.when(i > 0)
+        j = line.index(order(i))
+        pl.when(i == 3)(lambda: line.far(0, xa))
+        xhat = norm_parts(xa[block(j), :].astype(jnp.float32))[0]
+        n1[block(j), :] = (xhat * gains[0:1, :] + gains[2:3, :]).astype(jnp.bfloat16)
+
+        @pl.when(i == 0)
         def _():
-            line.arrived(0, d, n1)
+            qkv_a.wait()
+            qkv_b.wait()
 
         values = n1[block(j), :]
         kvb[block(j), 0:256] = nn(values, wide_tile(wq, slice(256, 512))).astype(jnp.bfloat16)
@@ -404,7 +466,6 @@
     plane.wait(0, piece(arrc))
     cz[block(z), :] = rows_of(arrc[...]).astype(jnp.bfloat16)
     line.spread(4, cz)
-    own.step_core(1, wo)
     for i in range(4):
         kv_copy(i, line.index(order(i))).wait_recv()
     swaps = [
@@ -417,6 +478,11 @@
     def _():
         for swap in swaps:
             swap.start()
+
+    my_lanes = pl.ds(pl.multiple_of(256 * z, 256), 256)
+
+    def mix_copy(d):
+        return line.copy(1, d, mixs.at[block(line.index(d))], mixed.at[:, my_lanes])
 
     for j in range(4):
         seen = masks(j, yh, docs)
@@ -434,17 +500,10 @@
                     nn(probs[0].astype(jnp.bfloat16), values[0]) + nn(probs[1].astype(jnp.bfloat16), values[1])
                 )
             mixs[128 * j : 128 * j + 128, lanes] = jnp.where(head_lanes(0), outs[0], outs[1]).astype(jnp.bfloat16)
-    my_lanes = pl.ds(pl.multiple_of(256 * z, 256), 256)
-
-    def mix_copy(d):
-        return line.copy(1, d, mixs.at[block(line.index(d))], mixed.at[:, my_lanes])
-
-    for d in (1, 3, 2):
-        mix_copy(d).start()
+        pl.when(z != j)(lambda: mix_copy(lax.rem(j + 4 - z, 4)).start())
     mixed[:, my_lanes] = mixs[block(z), :]
-    own.step_core(2, wu)
-    own.step_core(3, wd)
-    own.wait(1, wo)
+    out.share()
+    out.wait()
     for d in (1, 3, 2):
         line.got(1, d, mixed.at[:, pl.ds(pl.multiple_of(256 * line.index(d), 256), 256)])
     for n in range(4):
@@ -452,13 +511,15 @@
         after[:, tile] = x[:, tile].astype(jnp.float32) + nn(mixed[...], wide_tile(wo, tile))
     xhat = norm_parts(after[...])[0]
     n2[block(z), :] = (xhat * gains[1:2, :] + gains[3:4, :]).astype(jnp.bfloat16)
-    line.spread(2, n2)
-    own.wait(2, wu)
-    own.wait(3, wd)
+    line.begin(2, n2)
+    up.share()
+    down.share()
+    up.wait()
+    down.wait()
     stores = [
         pltpu.make_async_copy(src, dst, osem.at[k])
         for k, (src, dst) in enumerate(
-            [(n1, o_n1), (qb, o_q), (kvb, o_kv), (kvo, o_kvo), (wq, o_wq), (wo, o_wo), (wu, o_wu), (wd, o_wd)]
+            [(xa, o_x), (n1, o_n1), (qb, o_q), (kvb, o_kv), (kvo, o_kvo), (wq, o_wq), (wo, o_wo), (wu, o_wu), (wd, o_wd)]
         )
     ]
     for store in stores:
@@ -467,11 +528,7 @@
     def feed(i, carry):
         d = order(i)
         j = line.index(d)
-
-        @pl.when(i > 0)
-        def _():
-            line.arrived(2, d, n2)
-
+        line.ready(2, i, n2)
         values = n2[block(j), :]
         for n in range(4):
             tile = slice(n * 256, (n + 1) * 256)
@@ -493,7 +550,7 @@
     for d in (1, 3, 2):
         line.arrived(4, d, cz)
     late = [
-        pltpu.make_async_copy(src, dst, osem.at[8 + k])
+        pltpu.make_async_copy(src, dst, osem.at[9 + k])
         for k, (src, dst) in enumerate([(n2, o_n2), (act, o_act), (dg, o_dg), (cz, o_cz)])
     ]
     for store in late:
@@ -505,14 +562,14 @@
         return carry
 
     lax.fori_loop(0, 7, sent_gain, 0)
-    for phase in range(4):
-        own.sent(phase, sources[phase], fulls[phase])
+    for weight in (qkv_a, qkv_b, out, up, down):
+        weight.sent()
     for i in range(4):
         kv_copy(i, line.index(order(i))).wait_send()
-    line.sent(0, n1)
+    line.sent_all(0, xa)
     for d in (1, 3, 2):
         mix_copy(d).wait_send()
-    line.sent(2, n2)
+    line.sent_all(2, n2)
     line.sent(4, cz)
     plane.sent(0, piece(sendc), piece(arrc))
     hid[...] = (after[...] + line.total(3, ps, pr)).astype(jnp.bfloat16)
@@ -527,7 +584,7 @@
         store.wait()
 
 
-def dense_forward_call(x, gain_tile, docs, route, cot, w_qkv, w_out, w_up, w_down, exp_in, exp_out):
+def dense_forward_call(x, gain, bias, docs, route, cot, w_qkv, w_out, w_up, w_down, exp_in, exp_out):
     bf, f32 = jnp.bfloat16, jnp.float32
     vmem, anywhere = pl.BlockSpec(memory_space=pltpu.VMEM), pl.BlockSpec(memory_space=pl.ANY)
     smem = pl.BlockSpec(memory_space=pltpu.SMEM)
@@ -535,8 +592,8 @@
     line = [V((512, 1024), bf)]
     weight = [(2, 4, 2, 2, 32, 768)] + [(2, 4, 2, 2, 32, 1024)] * 3
     saved = [
-        shape((512, 1024), bf), shape((512, 1024), bf), shape((512, 1024), bf), shape((512, 1024), f32),
-        shape((512, 256), bf), shape((512, 512), bf), shape((512, 512), bf),
+        shape((512, 1024), bf), shape((512, 1024), bf), shape((512, 1024), bf), shape((512, 1024), bf),
+        shape((512, 1024), f32), shape((512, 256), bf), shape((512, 512), bf), shape((512, 512), bf),
     ] + [shape(w, bf) for w in weight] + [
         shape((512, 1024), bf), shape((1024, 512), bf), shape((512, 1024), bf), shape((1024, 512), bf),
     ]
@@ -544,28 +601,29 @@
         dense_forward_kernel,
         out_shape=[shape((128, 1024), bf), shape((128, 1024), bf), shape((128, 1024), f32), shape((8, 1024), f32)]
         + saved,
-        in_specs=[vmem, vmem, smem] + [vmem] * 6 + [anywhere, anywhere],
+        in_specs=[vmem] * 3 + [smem] + [vmem] * 6 + [anywhere, anywhere],
         out_specs=[vmem] * 4 + [anywhere] * len(saved),
         scratch_shapes=[
-            V((64, 768), bf), V((64, 1024), bf), *[V(w, bf) for w in weight], V((16, 1024), bf), V((16, 1024), bf),
-            *(line * 3), V((512, 256), bf), V((512, 512), bf), V((512, 512), bf), V((512, 256), bf),
+            V((64, 768), bf), V((64, 1024), bf), *[V(w, bf) for w in weight], V((8, 128), f32), V((8, 1024), f32),
+            V((8, 1024), f32),
+            *(line * 4), V((512, 256), bf), V((512, 512), bf), V((512, 512), bf), V((512, 256), bf),
             *line, V((512, 1024), f32), *(line * 2), V((256, 512), bf), V((256, 512), bf),
-            dma((5, 3)), dma((5, 3)), dma((4, 3)), dma((4, 3)), dma((4, 3)), dma((4, 3)), dma((4,)), dma((4,)),
-            dma((4,)), dma((4,)), dma((8,)), dma((8,)), dma((1, 15)), dma((1, 15)), dma((3,)), dma((3,)), dma((12,)),
+            dma((5, 4)), dma((5, 4)), dma((5, 3)), dma((5, 3)), dma((5, 3)), dma((5, 3)), dma((4,)), dma((4,)),
+            dma((5,)), dma((5,)), dma((8,)), dma((8,)), dma((1, 15)), dma((1, 15)), dma((3,)), dma((3,)), dma((13,)),
         ],
         compiler_params=pltpu.CompilerParams(collective_id=2, has_side_effects=True, vmem_limit_bytes=60 << 20),
         name="dense_forward",
-    )(x, gain_tile, docs, route, cot, w_qkv, w_out, w_up, w_down, exp_in, exp_out)
+    )(x, gain, bias, docs, route, cot, w_qkv, w_out, w_up, w_down, exp_in, exp_out)
 
 
 def expert_kernel(
-    hid, route, vec, cz_h, exp_in, exp_out, in0, out0, in1,
+    hid, route, exp_gain, exp_bias, centroid, cz_h, exp_in, exp_out, in0, out0, in1,
     gh, vecg, mid, gate_out, o_ps, gin1, gout1, gin0, gout0,
     w_in, w_out, sendh, sendg, arrh, arrg, cz,
     e0, e1, g0, g1, ps0, ps1, pr0, pb0, pb1,
     act0, act1, dg0, dg1, gp0, gp1,
     arrived, base, xh0, xh1, sc, gates, dots, dots_in,
-    ga_in, ga_out, sb_in, sb_out, rb_in, rb_out, vmine, vcore, vline, vsum, vswap,
+    ga_in, ga_out, sb_in, sb_out, rb_in, rb_out, vec, vec_own, vec_other, vmine, vcore, vline, vsum, vswap,
     wsem, zs, zr, cs, cr, ks, kr, osem, bs, br, ss, sr, vs, vr,
 ):
     at = Place()
@@ -611,18 +669,24 @@
     load_c.start()
     left, right = placings(route[0:1, :])
     sendh[...] = to_pieces(left, right, hid[...])
+    vec_own[0:2, :] = exp_gain[...].astype(jnp.float32)
+    vec_own[2:4, :] = exp_bias[...].astype(jnp.float32)
+    vec_own[4:5, :] = centroid[...].astype(jnp.float32)
+    vec_own[5:8, :] = jnp.zeros((3, 1024), jnp.float32)
     pl.semaphore_wait(bar, 20)
     plane.start(0, piece(sendh), piece(arrh))
     keep_piece(at, sendh, arrh)
+    trade = remote(vec_own, vec_other, vs.at[2], vr.at[2], at.other)
+    trade.start()
 
     def wait_loads(k, i):
         on_either(lambda: load(k, i).wait(), lambda: swapped(k, i).wait())
         share(k, i).start()
 
-    pl.when(jnp.logical_not(same))(lambda: swap_out.start())
     wait_loads(0, 0)
     wait_loads(0, 1)
-    wait_loads(1, 0)
+    trade.wait()
+    vec[...] = jnp.where(same, vec_own[...], vec_other[...])
     plane.wait(0, piece(arrh))
     gain = [vec[0:1, :], vec[1:2, :]]
     bias = [vec[2:3, :], vec[3:4, :]]
@@ -632,7 +696,9 @@
     xh0[...] = xhat
     sc[0] = jnp.broadcast_to(scale, (128, 128))
     e0[block(z), :] = (xhat * gain[0] + bias[0]).astype(jnp.bfloat16)
-    line.spread(0, e0)
+    line.begin(0, e0)
+    pl.when(jnp.logical_not(same))(lambda: swap_out.start())
+    wait_loads(1, 0)
     gating = jax.nn.sigmoid(split_sum(rows * vec[4:5, :]))
     gates[z] = jnp.broadcast_to(gating, (128, 128))
 
@@ -675,10 +741,7 @@
         d = order(i)
         j = line.index(d)
 
-        @pl.when(i > 0)
-        def _():
-            line.arrived(0, d, e0)
-
+        line.ready(0, i, e0)
         forward(0, j, e0, act0, dg0)
         project(0, j, act0, ps0)
 
@@ -697,7 +760,7 @@
     xh1[...] = xhat
     sc[1] = jnp.broadcast_to(scale, (128, 128))
     e1[block(z), :] = (xhat * gain[1] + bias[1]).astype(jnp.bfloat16)
-    line.spread(2, e1)
+    line.begin(2, e1)
     gate = gates[z][:, 0:1]
     mid[...] = arrived[...] + gate * (base[...] - arrived[...])
     gate_out[...] = gates[z]
@@ -715,10 +778,7 @@
 
         g1[block(j), :] = (gates[j][:, 0:1] * cz[block(j), :].astype(jnp.float32)).astype(jnp.bfloat16)
 
-        @pl.when(i > 0)
-        def _():
-            line.arrived(2, d, e1)
-
+        line.ready(2, i, e1)
         forward(1, j, e1, act1, dg1)
         backward(1, j, g1, dg1, gp1, ps0)
 
@@ -783,7 +843,7 @@
     grad_stream = gates[z][:, 0:1] * cot
     grad_stream += norm_back(grad_normed, gain[1], xh1[...], sc[1][:, 0:1])
     g0[block(z), :] = grad_stream.astype(jnp.bfloat16)
-    line.spread(6, g0)
+    line.begin(6, g0)
     vmine[1:2, :] = jnp.sum(grad_normed * xh1[...], axis=0, keepdims=True)
     vmine[3:4, :] = jnp.sum(grad_normed, axis=0, keepdims=True)
     line.sent(4, ps0)
@@ -819,10 +879,7 @@
         d = order(i)
         j = line.index(d)
 
-        @pl.when(i > 0)
-        def _():
-            line.arrived(6, d, g0)
-
+        line.ready(6, i, g0)
         backward(0, j, g0, dg0, gp0, ps0)
 
         @pl.when(i > 0)
@@ -875,9 +932,9 @@
     for k in (0, 1):
         for i in range(2):
             share(k, i).wait_send()
-    line.sent(0, e0)
-    line.sent(2, e1)
-    line.sent(6, g0)
+    line.sent_all(0, e0)
+    line.sent_all(2, e1)
+    line.sent_all(6, g0)
     line.sent(7, ps0)
     plane.sent(0, piece(sendh), piece(arrh))
     plane.sent(1, piece(sendg), piece(arrg))
@@ -895,7 +952,7 @@
         vecg[...] = vswap[...]
 
 
-def expert_call(hid, route, vec, cz, exp_in, exp_out, in0, out0, in1):
+def expert_call(hid, route, exp_gain, exp_bias, centroid, cz, exp_in, exp_out, in0, out0, in1):
     bf, f32 = jnp.bfloat16, jnp.float32
     vmem, anywhere = pl.BlockSpec(memory_space=pltpu.VMEM), pl.BlockSpec(memory_space=pl.ANY)
     shape, V, dma = jax.ShapeDtypeStruct, pltpu.VMEM, pltpu.SemaphoreType.DMA
@@ -909,7 +966,7 @@
             shape((512, 1024), bf), shape((1024, 512), bf), shape((512, 1024), bf), shape((1024, 512), bf),
             shape((512, 1024), bf),
         ),
-        in_specs=[vmem] * 3 + [anywhere] * 6,
+        in_specs=[vmem] * 5 + [anywhere] * 6,
         out_specs=tuple([vmem] * 4 + [anywhere] * 5),
         scratch_shapes=[
             V((2, 1024, 1024), bf), V((2, 1024, 1024), bf), *(pieces * 4), *line,
@@ -917,13 +974,13 @@
             *(rows * 4), *(small * 4),
             V((2, 1024, 512), f32), V((2, 512, 1024), f32),
             V((2, 1024, 512), bf), V((2, 512, 1024), bf), V((2, 1024, 512), bf), V((2, 512, 1024), bf),
-            *(vectors * 2), V((4, 8, 1024), f32), *(vectors * 2),
-            dma((3, 2)), dma((9, 3)), dma((9, 3)), dma((2, 15)), dma((2, 15)), dma((2, 2)), dma((2, 2)), dma((2, 2)),
-            dma((2, 2)), dma((2, 2)), dma((3,)), dma((3,)), dma((2,)), dma((2,)),
+            *(vectors * 5), V((4, 8, 1024), f32), *(vectors * 2),
+            dma((3, 2)), dma((9, 4)), dma((9, 4)), dma((2, 15)), dma((2, 15)), dma((2, 2)), dma((2, 2)), dma((2, 2)),
+            dma((2, 2)), dma((2, 2)), dma((3,)), dma((3,)), dma((3,)), dma((3,)),
         ],
         compiler_params=pltpu.CompilerParams(collective_id=1, has_side_effects=True, vmem_limit_bytes=60 << 20),
         name="experts",
-    )(hid, route, vec, cz, exp_in, exp_out, in0, out0, in1)
+    )(hid, route, exp_gain, exp_bias, centroid, cz, exp_in, exp_out, in0, out0, in1)
 
 
 class Everyone:
@@ -951,13 +1008,13 @@
 
 
 def dense_backward_kernel(
-    gh, x, after, docs, gains, mixed, route, mid, gate, n1_h, n2_h, act_h, dg_h, q_h, kv_h, kvo_h, wq_h, wo_h, wu_h,
+    gh, after, docs, gains, mixed, route, mid, gate, x_h, n1_h, n2_h, act_h, dg_h, q_h, kv_h, kvo_h, wq_h, wo_h, wu_h,
     wd_h, ps_h, gin0, gout0,
-    gx, gq, go, gu, gd, gvec, res, fin0, fout0,
-    ghs, n1, n2, act, dg, gp, qb, kvb, kvo, wq, wo, wu, wd,
+    gx, bd, bu, bo, bq, gvec, res, fin0, fout0,
+    ghs, xa, xh, n1, n2, act, dg, gp, qb, kvb, kvo, wq, wo, wu, wd,
     ps, pr, ps2, pr2, ps3, pr3, gms, gm, dp, dkv, dkvo, kvs, kvr,
     md, mu, mo, mq, td, tu, to, tq, rd, ru, ro, rq, xd, xu, xo, sd, su, so, yd, yu, yo, rp, sendr, arrr,
-    vmine, vcore, vplane, vline, outz, bd, bu, bo, bq,
+    vmine, vcore, vplane, vline, outz,
     lsem, zs, zr, xs, xr, ys, yr, kvss, kvsr, ks, kr, cs, cr, qs, qr, ss, sr, vs, vr,
 ):
     at = Place()
@@ -976,7 +1033,7 @@
         for k, (src, dst) in enumerate(
             [
                 (wd_h, wd), (dg_h, dg), (wu_h, wu), (act_h, act), (n2_h, n2), (wo_h, wo), (ps_h, ps3), (q_h, qb),
-                (kv_h, kvb), (kvo_h, kvo), (wq_h, wq), (n1_h, n1),
+                (kv_h, kvb), (kvo_h, kvo), (wq_h, wq), (n1_h, n1), (x_h, xa),
             ]
         )
     ]
@@ -984,14 +1041,14 @@
         load.start()
     ghs[block(z), :] = gh[...]
     pl.semaphore_wait(bar, 23)
-    line.spread(0, ghs)
+    line.begin(0, ghs)
     swaps = [
         remote(gin0, fin0, ss.at[0], sr.at[0], at.swap_mate),
         remote(gout0, fout0, ss.at[1], sr.at[1], at.swap_mate),
     ]
     keeps = [
-        pltpu.make_async_copy(gin0, fin0, lsem.at[12]),
-        pltpu.make_async_copy(gout0, fout0, lsem.at[13]),
+        pltpu.make_async_copy(gin0, fin0, lsem.at[13]),
+        pltpu.make_async_copy(gout0, fout0, lsem.at[14]),
     ]
 
     @pl.when(at.same)
@@ -1011,10 +1068,7 @@
         d = order(i)
         j = line.index(d)
 
-        @pl.when(i > 0)
-        def _():
-            line.arrived(0, d, ghs)
-
+        line.ready(0, i, ghs)
         values = ghs[block(j), :]
         for n in range(4):
             tile = slice(n * 256, (n + 1) * 256)
@@ -1159,15 +1213,14 @@
         kvs[rows, :] = dkvo[rows, :].astype(jnp.bfloat16)
         kv_copy(j).start()
 
-    attend_back(3)
-    attend_back(2)
+    for j in (3, 2, 1, 0):
+        attend_back(j)
+    bd[at.s] = y_total(0, sd, yd).astype(jnp.bfloat16)
+    everyone.start(0, bd)
     to_y(1, mu, xu, su, yu)
-    attend_back(1)
-    attend_back(0)
-    sendr[...] = pieces_of(mid[...] + gate[:, 0:1] * line.total(6, ps3, pr3))
-    plane.start(2, piece(sendr), piece(arrr))
-    keep_piece(at, sendr, arrr)
-    to_y(2, mo, xo, so, yo)
+    vmine[0:1, :] = jnp.zeros((1, 1024), jnp.float32)
+    vmine[2:3, :] = jnp.zeros((1, 1024), jnp.float32)
+    vmine[4:8, :] = jnp.zeros((4, 1024), jnp.float32)
     for j in (3, 2, 1, 0):
         rows = slice(128 * j, 128 * j + 128)
         kv_copy(j).wait_recv()
@@ -1177,9 +1230,13 @@
         d = order(3 - i)
         j = line.index(d)
         values = dp[block(j), :]
+        xh[...] = norm_parts(xa[block(j), :].astype(jnp.float32))[0]
         for n in range(4):
             tile = slice(n * 256, (n + 1) * 256)
-            ps2[block(j), tile] = nt(values, tall_tile(wq, n)).astype(jnp.bfloat16)
+            part = nt(values, tall_tile(wq, n))
+            ps2[block(j), tile] = part.astype(jnp.bfloat16)
+            vmine[0:1, tile] += jnp.sum(part * xh[:, tile], axis=0, keepdims=True)
+            vmine[2:3, tile] += jnp.sum(part, axis=0, keepdims=True)
 
         @pl.when(i < 3)
         def _():
@@ -1188,10 +1245,19 @@
         return carry
 
     lax.fori_loop(0, 4, last, 0)
+    give_core = remote(vmine, vcore, vs.at[0], vr.at[0], at.other)
+    give_core.start()
     weight_grad(n1, dp, mq, tq)
     core_copy(3, tq, rq).start()
-    bd[at.s] = y_total(0, sd, yd).astype(jnp.bfloat16)
-    everyone.start(0, bd)
+
+    def tile_of(q):
+        return vmine.at[:, pl.ds(pl.multiple_of(128 * lax.div(q, 2), 128), 128)]
+
+    def slot_v(q):
+        return vplane.at[q]
+
+    give_core.wait()
+    vmine[...] += vcore[...]
     join_cores(3, mq, tq, rq)
 
     def piece_q(q):
@@ -1202,8 +1268,14 @@
 
     plane.start(0, piece_q, slot_q)
     rp[at.m] = mq[at.yl, at.x, pl.ds(pl.multiple_of(32 * yh, 32), 32), :]
+    plane.start(1, tile_of, slot_v)
+    vplane[at.m] = vmine[:, pl.ds(pl.multiple_of(128 * col, 128), 128)]
+    to_y(2, mo, xo, so, yo)
     bu[at.s] = y_total(1, su, yu).astype(jnp.bfloat16)
     everyone.start(1, bu)
+    sendr[...] = pieces_of(mid[...] + gate[:, 0:1] * line.total(6, ps3, pr3))
+    plane.start(2, piece(sendr), piece(arrr))
+    keep_piece(at, sendr, arrr)
     total_out = y_total(2, so, yo)
     for n in range(4):
         outz[4 + n] = total_out[:, 256 * n : 256 * n + 256].astype(jnp.bfloat16)
@@ -1214,36 +1286,20 @@
     for d in (1, 3, 2):
         out_copy(d).start()
     grad_normed = line.total(3, ps2, pr2)
-    xhat, scale = norm_parts(x[...].astype(jnp.float32))
-    vmine[0:1, :] = jnp.sum(grad_normed * xhat, axis=0, keepdims=True)
-    vmine[2:3, :] = jnp.sum(grad_normed, axis=0, keepdims=True)
-    vmine[4:8, :] = jnp.zeros((4, 1024), jnp.float32)
-    give_core = remote(vmine, vcore, vs.at[0], vr.at[0], at.other)
-    give_core.start()
+    xhat, scale = norm_parts(xa[block(z), :].astype(jnp.float32))
     gx[...] += norm_back(grad_normed, gains[0:1, :], xhat, scale)
-    give_core.wait()
-    vmine[...] += vcore[...]
-
-    def tile_of(q):
-        return vmine.at[:, pl.ds(pl.multiple_of(128 * lax.div(q, 2), 128), 128)]
-
-    def slot_v(q):
-        return vplane.at[q]
-
-    plane.start(1, tile_of, slot_v)
-    vplane[at.m] = vmine[:, pl.ds(pl.multiple_of(128 * col, 128), 128)]
+    plane.wait(0, slot_q)
+    acc = rp[0].astype(jnp.float32)
+    for q in range(1, 16):
+        acc += rp[q].astype(jnp.float32)
+    bq[at.s] = acc.astype(jnp.bfloat16)
+    everyone.start(3, bq)
     acc = outz[4 + z].astype(jnp.float32)
     for d in (1, 3, 2):
         line.got(4, d, outz.at[line.index(d)])
         acc += outz[line.index(d)].astype(jnp.float32)
     bo[at.s] = acc.astype(jnp.bfloat16)
     everyone.start(2, bo)
-    plane.wait(0, slot_q)
-    acc = rp[0].astype(jnp.float32)
-    for q in range(1, 16):
-        acc += rp[q].astype(jnp.float32)
-    bq[at.s] = acc.astype(jnp.bfloat16)
-    everyone.start(3, bq)
     plane.wait(1, slot_v)
     vline[z] = jnp.sum(vplane[...], axis=0)
 
@@ -1257,36 +1313,12 @@
     res[...] = from_pieces(left, right, arrr[...])
     everyone.wait(0, bd)
     everyone.wait(1, bu)
-    for zz in range(4):
-        for half in range(2):
-            gd[64 * zz + 32 * half : 64 * zz + 32 * half + 32, :] = bd[2 * zz + half].astype(jnp.float32)
-    for half in range(2):
-        rows = slice(32 * half, 32 * half + 32)
-        lane = lax.broadcasted_iota(jnp.int32, (32, 128), 1) < 64
-        for n in range(8):
-            tile = slice(128 * n, 128 * n + 128)
-            quarter = [bu[2 * zz + half, :, tile].astype(jnp.float32) for zz in range(4)]
-            turned = [pltpu.roll(v, 64, 1) for v in quarter]
-            first = 512 * n
-            gu[rows, first : first + 128] = jnp.where(lane, quarter[0], turned[1])
-            gu[rows, first + 128 : first + 256] = jnp.where(lane, quarter[2], turned[3])
-            gu[rows, first + 256 : first + 384] = jnp.where(lane, turned[0], quarter[1])
-            gu[rows, first + 384 : first + 512] = jnp.where(lane, turned[2], quarter[3])
     everyone.wait(2, bo)
-    for zz in range(4):
-        for half in range(2):
-            go[32 * half : 32 * half + 32, 256 * zz : 256 * zz + 256] = bo[2 * zz + half].astype(jnp.float32)
-    everyone.wait(3, bq)
-    for zz in range(4):
-        for half in range(2):
-            for part in range(3):
-                gq[32 * half : 32 * half + 32, 1024 * part + 256 * zz : 1024 * part + 256 * zz + 256] = bq[
-                    2 * zz + half, :, 256 * part : 256 * part + 256
-                ].astype(jnp.float32)
     for d in (1, 3, 2):
         line.got(5, d, vline.at[line.index(d)])
     gvec[...] = jnp.sum(vline[...], axis=0)
-    line.sent(0, ghs)
+    everyone.wait(3, bq)
+    line.sent_all(0, ghs)
     line.sent(1, ps)
     line.sent(3, ps2)
     line.sent(6, ps3)
@@ -1316,7 +1348,7 @@
             swap.wait()
 
 
-def dense_backward_call(gh, x, after, docs, gains, mixed, route, mid, gate, saved, ps, gin0, gout0):
+def dense_backward_call(gh, after, docs, gains, mixed, route, mid, gate, saved, ps, gin0, gout0):
     bf, f32 = jnp.bfloat16, jnp.float32
     vmem, anywhere = pl.BlockSpec(memory_space=pltpu.VMEM), pl.BlockSpec(memory_space=pl.ANY)
     smem = pl.BlockSpec(memory_space=pltpu.SMEM)
@@ -1326,14 +1358,14 @@
     return pl.pallas_call(
         dense_backward_kernel,
         out_shape=[
-            shape((128, 1024), f32), shape((64, 3072), f32), shape((64, 1024), f32), shape((64, 4096), f32),
-            shape((256, 1024), f32), shape((8, 128), f32), shape((128, 1024), bf), shape((1024, 512), bf),
+            shape((128, 1024), f32), shape((8, 32, 1024), bf), shape((8, 32, 1024), bf), shape((8, 32, 256), bf),
+            shape((8, 32, 768), bf), shape((8, 128), f32), shape((128, 1024), bf), shape((1024, 512), bf),
             shape((512, 1024), bf),
         ],
-        in_specs=[vmem, vmem, vmem, smem] + [vmem] * 5 + [anywhere] * 14,
+        in_specs=[vmem, vmem, smem] + [vmem] * 5 + [anywhere] * 15,
         out_specs=[vmem] * 7 + [anywhere] * 2,
         scratch_shapes=[
-            *(line * 4), V((512, 1024), f32), *line,
+            *(line * 2), V((128, 1024), f32), *(line * 3), V((512, 1024), f32), *line,
             V((512, 256), bf), V((512, 512), bf), V((512, 512), bf),
             V((2, 4, 2, 2, 32, 768), bf), *([V((2, 4, 2, 2, 32, 1024), bf)] * 3),
             *(line * 6),
@@ -1344,14 +1376,96 @@
             V((16, 32, 768), bf), *(pieces * 2),
             V((8, 1024), f32), V((8, 1024), f32), V((16, 8, 128), f32), V((4, 8, 128), f32),
             V((8, 32, 256), bf),
-            V((8, 32, 1024), bf), V((8, 32, 1024), bf), V((8, 32, 256), bf), V((8, 32, 768), bf),
-            dma((14,)), dma((7, 3)), dma((7, 3)), dma((3, 3)), dma((3, 3)), dma((3, 3)), dma((3, 3)), dma((4,)),
+            dma((15,)), dma((7, 4)), dma((7, 4)), dma((3, 3)), dma((3, 3)), dma((3, 3)), dma((3, 3)), dma((4,)),
             dma((4,)), dma((4,)), dma((4,)), dma((3, 15)), dma((3, 15)), dma((4, 7)), dma((4, 7)), dma((2,)),
             dma((2,)), dma((1,)), dma((1,)),
         ],
         compiler_params=pltpu.CompilerParams(collective_id=3, has_side_effects=True, vmem_limit_bytes=62 << 20),
         name="dense_backward",
-    )(gh, x, after, docs, gains, mixed, route, mid, gate, *saved, ps, gin0, gout0)
+    )(gh, after, docs, gains, mixed, route, mid, gate, *saved, ps, gin0, gout0)
+
+
+def finish_kernel(
+    gvec, vecg, res, gx, bd, bu, bo, bq, in0, in1, out0, out1,
+    ng, nb, eg, eb, cen, o_res, o_gx, o_gq, o_go, o_gu, o_gd, o_in, o_out,
+    b_in, b_out, f_in, f_out, vd, vu, vo, vq, gq, go, gu, gd, isem, osem,
+):
+    whole = [pltpu.make_async_copy(res, o_res, osem.at[0]), pltpu.make_async_copy(gx, o_gx, osem.at[1])]
+    pairs = [
+        (in0, b_in.at[0]), (in1, b_in.at[1]), (out0, b_out.at[0]), (out1, b_out.at[1]), (bd, vd), (bu, vu), (bo, vo),
+        (bq, vq),
+    ]
+    loads = [pltpu.make_async_copy(src, dst, isem.at[k]) for k, (src, dst) in enumerate(pairs)]
+    for copy in loads + whole:
+        copy.start()
+    c = lax.rem(lax.axis_index("fsdp"), 2)
+    mine = jnp.where(c == 0, gvec[0:4, 0:64], gvec[0:4, 64:128])
+    ng[...] = mine[0:2]
+    nb[...] = mine[2:4]
+    eg[...] = vecg[0:2, :]
+    eb[...] = vecg[2:4, :]
+    cen[...] = vecg[4:5, :]
+    stores = []
+
+    def store(src, dst):
+        stores.append(pltpu.make_async_copy(src, dst, osem.at[2 + len(stores)]))
+        stores[-1].start()
+
+    for k in range(4):
+        loads[k].wait()
+        low, wide, out = ((b_in, f_in, o_in), (b_out, f_out, o_out))[k // 2]
+        wide[k % 2] = low[k % 2].astype(jnp.float32)
+        store(wide.at[k % 2], out.at[k % 2])
+    for k in range(4, 8):
+        loads[k].wait()
+    lane = lax.broadcasted_iota(jnp.int32, (32, 128), 1) < 64
+    for half in range(2):
+        rows = slice(32 * half, 32 * half + 32)
+        for z in range(4):
+            gd[64 * z + 32 * half : 64 * z + 32 * half + 32, :] = vd[2 * z + half].astype(jnp.float32)
+            go[rows, 256 * z : 256 * z + 256] = vo[2 * z + half].astype(jnp.float32)
+            for part in range(3):
+                gq[rows, 1024 * part + 256 * z : 1024 * part + 256 * z + 256] = vq[
+                    2 * z + half, :, 256 * part : 256 * part + 256
+                ].astype(jnp.float32)
+        for n in range(8):
+            tile = slice(128 * n, 128 * n + 128)
+            quarter = [vu[2 * z + half, :, tile].astype(jnp.float32) for z in range(4)]
+            turned = [pltpu.roll(v, 64, 1) for v in quarter]
+            first = 512 * n
+            gu[rows, first : first + 128] = jnp.where(lane, quarter[0], turned[1])
+            gu[rows, first + 128 : first + 256] = jnp.where(lane, quarter[2], turned[3])
+            gu[rows, first + 256 : first + 384] = jnp.where(lane, turned[0], quarter[1])
+            gu[rows, first + 384 : first + 512] = jnp.where(lane, turned[2], quarter[3])
+    for src, dst in ((gq, o_gq), (go, o_go), (gu, o_gu), (gd, o_gd)):
+        store(src, dst)
+    for copy in whole + stores:
+        copy.wait()
+
+
+def finish_call(gvec, vecg, res, gx, bd, bu, bo, bq, in0, in1, out0, out1):
+    bf, f32 = jnp.bfloat16, jnp.float32
+    vmem, anywhere = pl.BlockSpec(memory_space=pltpu.VMEM), pl.BlockSpec(memory_space=pl.ANY)
+    shape, V, dma = jax.ShapeDtypeStruct, pltpu.VMEM, pltpu.SemaphoreType.DMA
+    return pl.pallas_call(
+        finish_kernel,
+        out_shape=[
+            shape((2, 64), f32), shape((2, 64), f32), shape((2, 1024), f32), shape((2, 1024), f32),
+            shape((1, 1024), f32), shape((128, 1024), bf), shape((128, 1024), f32), shape((64, 3072), f32),
+            shape((64, 1024), f32), shape((64, 4096), f32), shape((256, 1024), f32), shape((2, 1024, 512), f32),
+            shape((2, 512, 1024), f32),
+        ],
+        in_specs=[vmem] * 2 + [anywhere] * 10,
+        out_specs=[vmem] * 5 + [anywhere] * 8,
+        scratch_shapes=[
+            V((2, 1024, 512), bf), V((2, 512, 1024), bf), V((2, 1024, 512), f32), V((2, 512, 1024), f32),
+            V((8, 32, 1024), bf), V((8, 32, 1024), bf), V((8, 32, 256), bf), V((8, 32, 768), bf),
+            V((64, 3072), f32), V((64, 1024), f32), V((64, 4096), f32), V((256, 1024), f32),
+            dma((8,)), dma((10,)),
+        ],
+        compiler_params=pltpu.CompilerParams(vmem_limit_bytes=62 << 20),
+        name="finish",
+    )(gvec, vecg, res, gx, bd, bu, bo, bq, in0, in1, out0, out1)
 
 
 def on_device(
@@ -1375,39 +1489,32 @@
     x = inputs.reshape(tok_rows, width)
     cot = cotangent.reshape(tok_rows, width)
     slots = route.reshape(1, tok_rows)
-    core = lax.rem(lax.axis_index("fsdp"), 2)
-    mine = lax.rem(lax.axis_index("seq"), 2) == core
-    share = jnp.pad(jnp.concatenate([norm_gain, norm_bias]), ((0, 12), (0, 0)))
-    none = jnp.zeros_like(share)
-    gain_tile = jnp.where(core == 0, jnp.concatenate([share, none], 1), jnp.concatenate([none, share], 1))
-    core_pairs = [(i, i + 1 - 2 * (i % 2)) for i in range(128)]
-    vec = jnp.concatenate([exp_gain[0], exp_bias[0], centroid], axis=0)
-    vec = jnp.where(mine, vec, lax.ppermute(vec, ("seq", "fsdp"), core_pairs)).astype(jnp.float32)
-    vec = jnp.pad(vec, ((0, 3), (0, 0)))
     hidden, mixed, after, gains, *saved, cz, in0, out0, in1 = dense_forward_call(
-        x, gain_tile, doc_starts, slots, cot, w_qkv, w_out, w_up, w_down, exp_in[0], exp_out[0]
+        x, norm_gain, norm_bias, doc_starts, slots, cot, w_qkv, w_out, w_up, w_down, exp_in[0], exp_out[0]
     )
     grad_hidden, vec_grads, mid, gate, part, grad_in1, grad_out1, grad_in0, grad_out0 = expert_call(
-        hidden, slots, vec, cz, exp_in[0], exp_out[0], in0, out0, in1
+        hidden, slots, exp_gain[0], exp_bias[0], centroid, cz, exp_in[0], exp_out[0], in0, out0, in1
     )
-    grad_x, grad_qkv, grad_wo, grad_up, grad_down, norm_grads, result, grad_in0, grad_out0 = dense_backward_call(
-        grad_hidden, x, after, doc_starts, gains, mixed, slots, mid, gate, saved, part, grad_in0, grad_out0
+    grad_x, down, up, out, qkv, norm_grads, result, grad_in0, grad_out0 = dense_backward_call(
+        grad_hidden, after, doc_starts, gains, mixed, slots, mid, gate, saved, part, grad_in0, grad_out0
     )
-    norm_grads = jnp.where(core == 0, norm_grads[:4, :64], norm_grads[:4, 64:])
+    gain, bias, e_gain, e_bias, center, result, grad_x, g_qkv, g_out, g_up, g_down, e_in, e_out = finish_call(
+        norm_grads, vec_grads, result, grad_x, down, up, out, qkv, grad_in0, grad_in1, grad_out0, grad_out1
+    )
     return (
         result[None],
         grad_x[None],
-        norm_grads[0:2],
-        norm_grads[2:4],
-        grad_qkv,
-        grad_wo,
-        grad_up,
-        grad_down,
-        vec_grads[None, 0:2],
-        vec_grads[None, 2:4],
-        jnp.stack([grad_in0, grad_in1]).astype(jnp.float32)[None],
-        jnp.stack([grad_out0, grad_out1]).astype(jnp.float32)[None],
-        vec_grads[4:5],
+        gain,
+        bias,
+        g_qkv,
+        g_out,
+        g_up,
+        g_down,
+        e_gain[None],
+        e_bias[None],
+        e_in[None],
+        e_out[None],
+        center,
     )
 
 

time: 331 us -> 314 us (0.949)
  other arithmetic: 9.53 us -> 0 us
  local copies, waits for them, and re-layouts: 8.43 us -> 0 us
    pallas_call x0 -> x1, Pallas kernels: none -> 26.5 us  [finish_call(): pl.pallas_call(finish_kernel, out_shape=[shape((2, 64), f32), shape((2, 6...]
    pallas_call x1, Pallas kernels: 111 us -> 96.8 us  [expert_call(): pl.pallas_call(expert_kernel, out_shape=(shape((128, 1024), bf), shape((8...]
    pallas_call x1, Pallas kernels: 107 us -> 99.8 us  [dense_backward_call(): pl.pallas_call(dense_backward_kernel, out_shape=[shape((128, 1024), f32),...]
    convert_element_type x2 -> x0, other arithmetic: 5.95 us -> none  [the longest x1 3.66 us: on_device(): jnp.stack([grad_in0, grad_in1]).astype(jnp.float32)[None]]
    unnamed x30 -> x0, local copies, waits for them, and re-layouts: 5.06 us -> none
    pallas_call x1, Pallas kernels: 91.8 us -> 87.1 us  [dense_forward_call(): pl.pallas_call(dense_forward_kernel, out_shape=[shape((128, 1024), bf), s...]
  transfers between devices with their start and end apart: 1 -> 0, of which waited for: 0 -> 0; matrix products, arithmetic and copies ran while one was open for 0% -> 0% of each run, Pallas kernels for 28% -> 0%
where the time goes in v4:
time: 314 us; the launch traced here: 311 us
  Pallas kernels  310 us (99%)
    pallas_call x1, Pallas kernels, dense_backward_call(): pl.pallas_call(dense_backward_kernel, out_shape=[shape((128, 1024), f32),...  99.8 us
    pallas_call x1, Pallas kernels, expert_call(): pl.pallas_call(expert_kernel, out_shape=(shape((128, 1024), bf), shape((8...  96.8 us
    pallas_call x1, Pallas kernels, dense_forward_call(): pl.pallas_call(dense_forward_kernel, out_shape=[shape((128, 1024), bf), s...  87.1 us
    pallas_call x1, Pallas kernels, finish_call(): pl.pallas_call(finish_kernel, out_shape=[shape((2, 64), f32), shape((2, 6...  26.5 us

profile of v4, /device:TPU:4, one launch (start us, length us, event | category | flops | bytes accessed | tf_op | source)
XLA Modules:
  0.0 311.0 jit_solution(10974991464783869331)
XLA Ops:
  0.6 87.1 %dense_forward.1 = (bf16[128,1024]{1,0:T(8,128)(2,1)}, bf16[128,1024]{1,0:T(8,128)(2,1)}, f32[128,1024]{1,0:T(8,128)}, f32[8,1024]{1,0:T(8,128)}, bf16[512,1024]...) custom-call(bf16[128,1024]{1,0:T(8,128)(2,1)} %bitcast.17, ...), custom_call_target="tpu_custom_call" | custom-call | tf_op jit(solution)/shard_map/dense_forward/pallas_call | solution.py:600
  87.7 96.8 %experts.1 = (bf16[128,1024]{1,0:T(8,128)(2,1)}, f32[8,1024]{1,0:T(8,128)}, f32[128,1024]{1,0:T(8,128)}, f32[128,128]{1,0:T(8,128)}, bf16[512,1024]{1,0:T(8,128)...) custom-call(bf16[128,1024]{1,0:T(8,128)(2,1)} %get-tuple-element.64., ...), custom_call_target="tpu_custom_call" | custom-call | tf_op jit(solution)/shard_map/experts/pallas_call | solution.py:962
  184.6 99.8 %dense_backward.1 = (f32[128,1024]{1,0:T(8,128)}, bf16[8,32,1024]{2,1,0:T(8,128)(2,1)}, bf16[8,32,1024]{2,1,0:T(8,128)(2,1)}, bf16[8,32,256]{2,1,0:T(8,128)(2,1)...) custom-call(bf16[128,1024]{1,0:T(8,128)(2,1)} %get-tuple-element.69., ...), custom_call_target="tpu_custom_call" | custom-call | tf_op jit(solution)/shard_map/dense_backward/pallas_call | solution.py:1358
  284.4 26.5 %finish.1 = (f32[2,64]{1,0:T(2,128)}, f32[2,64]{1,0:T(2,128)}, f32[2,1024]{1,0:T(2,128)}, f32[2,1024]{1,0:T(2,128)}, f32[1,1024]{1,0:T(1,128)}, /*index=5*/bf16[...) custom-call(f32[8,128]{1,0:T(8,128)} %get-tuple-element.90.gvec, ...), custom_call_target="tpu_custom_call" | custom-call | tf_op jit(solution)/shard_map/finish/pallas_call | solution.py:1450

commit v5 on v4

--- a/solution.py
+++ b/solution.py
@@ -310,22 +310,21 @@
     return jnp.where(position >= first, 1, 0) + jnp.where(position >= second, 1, 0)
 
 
-def masks(j, yh, docs):
+def mask(j, yh, parity, docs):
     first, second = docs[0, 0], docs[0, 1]
     wide = 128 * (j + 1)
     row = lax.broadcasted_iota(jnp.int32, (128, wide), 0) + 128 * (2 * j + yh)
     lane = lax.broadcasted_iota(jnp.int32, (128, wide), 1)
-    start = (lane >> 7) * 256 + (lane & 127)
-    row_label = labels(row, first, second)
-    found = []
-    for parity in (yh, 1 - yh):
-        key = start + 128 * parity
-        found.append((key <= row) & (labels(key, first, second) == row_label))
-    return found
+    key = (lane >> 7) * 256 + (lane & 127) + 128 * parity
+    return (key <= row) & (labels(key, first, second) == labels(row, first, second))
+
+
+def masked_scores(q, keys, seen):
+    return jnp.where(seen, nt(q, keys) * 0.125, masked_score)
 
 
 def probabilities(q, keys, seen):
-    scores = [jnp.where(ok, nt(q, k) * 0.125, masked_score) for k, ok in zip(keys, seen)]
+    scores = [masked_scores(q, k, ok) for k, ok in zip(keys, seen)]
     top = jnp.maximum(
         jnp.max(scores[0], axis=-1, keepdims=True), jnp.max(scores[1], axis=-1, keepdims=True)
     )
@@ -356,9 +355,9 @@
 def dense_forward_kernel(
     x, gain, bias, docs, route, cot, w_qkv, w_out, w_up, w_down, exp_in, exp_out,
     hid, mixed, after, gains,
-    o_x, o_n1, o_n2, o_act, o_dg, o_q, o_kv, o_kvo, o_wq, o_wo, o_wu, o_wd, o_cz, o_in0, o_out0, o_in1,
+    o_x, o_n1, o_n2, o_act, o_dg, o_q, o_kv, o_kvo, o_wq, o_wo, o_wu, o_wd, o_cz, o_in0, o_out0,
     sq, su, wq, wo, wu, wd, gtile, gmine, gother,
-    xa, n1, n2, cz, qb, kvb, kvo, mixs, act, dg, ps, pr, sendc, arrc,
+    xa, n1, n2, cz, qb, kvb, kvo, mixs, act, dg, ps, pr, sendc, arrc, stats, own_sum,
     zs, zr, xs, xr, ys, yr, kvs, kvr, ks, kr, gs, gr, cs, cr, ss, sr, osem,
 ):
     at = Place()
@@ -388,22 +387,6 @@
     out = Gather(at, 2, "y", w_out.at[half], wo, *sems)
     up = Gather(at, 3, "y", su.at[half], wu, *sems)
     down = Gather(at, 4, "x", down_rows, wd, *sems)
-    pl.semaphore_wait(bar, 20)
-    line.begin(0, xa)
-    tile_at = pl.ds(pl.multiple_of(128 * col, 128), 128)
-
-    def gain_copy(i):
-        to = (at.s, 2 * lax.rem(col + i + 1, 8) + c)
-        return remote(gtile, gmine.at[:, tile_at], gs.at[i], gr.at[i], to)
-
-    def push_gain(i, carry):
-        gain_copy(i).start()
-        return carry
-
-    lax.fori_loop(0, 7, push_gain, 0)
-    gmine[:, tile_at] = gtile[...]
-    qkv_a.start()
-    qkv_b.start()
     low = lax.broadcasted_iota(jnp.int32, (64, 128), 1) < 64
     odd = lax.rem(z, 2) == 1
     for n in range(8):
@@ -413,11 +396,31 @@
         kept = jnp.where(low, a, pltpu.roll(b, 64, 1))
         moved = jnp.where(low, pltpu.roll(a, 64, 1), b)
         su[:, 128 * n : 128 * n + 128] = jnp.where(odd, moved, kept).astype(jnp.bfloat16)
-    out.start()
+    left, right = placings(route[0:1, :])
+    sendc[...] = to_pieces(left, right, cot[...])
+    pl.semaphore_wait(bar, 20)
+    line.begin(0, xa)
+    tile_at = pl.ds(pl.multiple_of(128 * col, 128), 128)
+
+    def gain_copy(i):
+        to = (at.s, 2 * lax.rem(col + i + 1, 8) + c)
+        return remote(gtile, gmine.at[:, tile_at], gs.at[i], gr.at[i], to)
+
+    def push_gain(i, carry):
+        gain_copy(i).start()
+        return carry
+
+    lax.fori_loop(0, 7, push_gain, 0)
+    gmine[:, tile_at] = gtile[...]
+    qkv_a.start()
+    qkv_b.start()
+    plane.start(0, piece(sendc), piece(arrc))
+    keep_piece(at, sendc, arrc)
+    for weight in (out, up, down):
+        weight.start()
     qkv_a.turn()
     qkv_b.turn()
-    down.start()
-    up.start()
+    line.relay(0, xa)
 
     def wait_gain(i, carry):
         q = lax.rem(col + 7 - i, 8)
@@ -428,18 +431,12 @@
     lax.fori_loop(0, 7, wait_gain, 0)
     gain_core = remote(gmine, gother, gs.at[7], gr.at[7], at.other)
     gain_core.start()
-    left, right = placings(route[0:1, :])
-    sendc[...] = to_pieces(left, right, cot[...])
-    line.relay(0, xa)
-    out.turn()
-    down.turn()
-    up.turn()
-    plane.start(0, piece(sendc), piece(arrc))
-    keep_piece(at, sendc, arrc)
     gain_core.wait_recv()
     gains[...] = gmine[...] + gother[...]
     qkv_a.share()
     qkv_b.share()
+    out.turn()
+    up.turn()
 
     def kv_copy(i, j):
         return remote(kvb.at[block(j)], kvo.at[block(j)], kvs.at[i], kvr.at[i], at.mate)
@@ -463,21 +460,42 @@
         return carry
 
     lax.fori_loop(0, 4, project_qkv, 0)
+    down.turn()
     plane.wait(0, piece(arrc))
     cz[block(z), :] = rows_of(arrc[...]).astype(jnp.bfloat16)
     line.spread(4, cz)
+
+    def heads(j, keys, parity):
+        seen = mask(j, yh, parity, docs)
+        wide = slice(0, 128 * (j + 1))
+        for p in range(2):
+            lanes = slice(128 * p, 128 * p + 128)
+            q = qb[128 * j : 128 * j + 128, lanes]
+            for h in range(2):
+                scores = masked_scores(only(head_lanes(h), q), keys[wide, lanes], seen)
+                yield 4 * j + 2 * p + h, h, lanes, scores, keys[wide, 256 + 128 * p : 384 + 128 * p]
+
+    first = None
+    for j in range(4):
+        for k, h, lanes, scores, values in heads(j, kvb, yh):
+            top = jnp.max(scores, axis=-1, keepdims=True)
+            weights = jnp.exp(scores - top)
+            stats[k] = jnp.where(head_lanes(0), top, split_sum(weights))
+            summed = nn(weights.astype(jnp.bfloat16), values)
+            if h == 0:
+                first = summed
+            else:
+                own_sum[128 * j : 128 * j + 128, lanes] = jnp.where(head_lanes(0), first, summed)
     for i in range(4):
         kv_copy(i, line.index(order(i))).wait_recv()
     swaps = [
         remote(exp_in.at[0], o_in0, ss.at[0], sr.at[0], at.swap_mate),
         remote(exp_out.at[0], o_out0, ss.at[1], sr.at[1], at.swap_mate),
-        remote(exp_in.at[1], o_in1, ss.at[2], sr.at[2], at.swap_mate),
     ]
 
     @pl.when(c != yh)
     def _():
-        for swap in swaps:
-            swap.start()
+        swaps[0].start()
 
     my_lanes = pl.ds(pl.multiple_of(256 * z, 256), 256)
 
@@ -485,21 +503,18 @@
         return line.copy(1, d, mixs.at[block(line.index(d))], mixed.at[:, my_lanes])
 
     for j in range(4):
-        seen = masks(j, yh, docs)
-        wide = slice(0, 128 * (j + 1))
-        for p in range(2):
-            lanes = slice(128 * p, 128 * p + 128)
-            value_lanes = slice(256 + 128 * p, 384 + 128 * p)
-            q = qb[128 * j : 128 * j + 128, lanes]
-            keys = [kvb[wide, lanes], kvo[wide, lanes]]
-            values = [kvb[wide, value_lanes], kvo[wide, value_lanes]]
-            outs = []
-            for h in range(2):
-                probs = probabilities(only(head_lanes(h), q), keys, seen)
-                outs.append(
-                    nn(probs[0].astype(jnp.bfloat16), values[0]) + nn(probs[1].astype(jnp.bfloat16), values[1])
-                )
-            mixs[128 * j : 128 * j + 128, lanes] = jnp.where(head_lanes(0), outs[0], outs[1]).astype(jnp.bfloat16)
+        rows = slice(128 * j, 128 * j + 128)
+        for k, h, lanes, scores, values in heads(j, kvo, 1 - yh):
+            top, total = stats[k][:, 0:1], stats[k][:, 64:65]
+            new_top = jnp.maximum(top, jnp.max(scores, axis=-1, keepdims=True))
+            kept = jnp.exp(top - new_top)
+            weights = jnp.exp(scores - new_top)
+            inverse = 1.0 / (total * kept + split_sum(weights))
+            summed = (own_sum[rows, lanes] * kept + nn(weights.astype(jnp.bfloat16), values)) * inverse
+            if h == 0:
+                first = summed
+            else:
+                mixs[rows, lanes] = jnp.where(head_lanes(0), first, summed).astype(jnp.bfloat16)
         pl.when(z != j)(lambda: mix_copy(lax.rem(j + 4 - z, 4)).start())
     mixed[:, my_lanes] = mixs[block(z), :]
     out.share()
@@ -514,6 +529,10 @@
     line.begin(2, n2)
     up.share()
     down.share()
+    @pl.when(c != yh)
+    def _():
+        swaps[1].start()
+
     up.wait()
     down.wait()
     stores = [
@@ -595,7 +614,7 @@
         shape((512, 1024), bf), shape((512, 1024), bf), shape((512, 1024), bf), shape((512, 1024), bf),
         shape((512, 1024), f32), shape((512, 256), bf), shape((512, 512), bf), shape((512, 512), bf),
     ] + [shape(w, bf) for w in weight] + [
-        shape((512, 1024), bf), shape((1024, 512), bf), shape((512, 1024), bf), shape((1024, 512), bf),
+        shape((512, 1024), bf), shape((1024, 512), bf), shape((512, 1024), bf),
     ]
     return pl.pallas_call(
         dense_forward_kernel,
@@ -608,7 +627,7 @@
             V((8, 1024), f32),
             *(line * 4), V((512, 256), bf), V((512, 512), bf), V((512, 512), bf), V((512, 256), bf),
             *line, V((512, 1024), f32), *(line * 2), V((256, 512), bf), V((256, 512), bf),
-            dma((5, 4)), dma((5, 4)), dma((5, 3)), dma((5, 3)), dma((5, 3)), dma((5, 3)), dma((4,)), dma((4,)),
+            V((16, 128, 128), f32), V((512, 256), f32), dma((5, 4)), dma((5, 4)), dma((5, 3)), dma((5, 3)), dma((5, 3)), dma((5, 3)), dma((4,)), dma((4,)),
             dma((5,)), dma((5,)), dma((8,)), dma((8,)), dma((1, 15)), dma((1, 15)), dma((3,)), dma((3,)), dma((13,)),
         ],
         compiler_params=pltpu.CompilerParams(collective_id=2, has_side_effects=True, vmem_limit_bytes=60 << 20),
@@ -617,7 +636,7 @@
 
 
 def expert_kernel(
-    hid, route, exp_gain, exp_bias, centroid, cz_h, exp_in, exp_out, in0, out0, in1,
+    hid, route, exp_gain, exp_bias, centroid, cz_h, exp_in, exp_out, in0, out0,
     gh, vecg, mid, gate_out, o_ps, gin1, gout1, gin0, gout0,
     w_in, w_out, sendh, sendg, arrh, arrg, cz,
     e0, e1, g0, g1, ps0, ps1, pr0, pb0, pb1,
@@ -644,9 +663,10 @@
         return pltpu.make_async_copy((exp_in, exp_out)[i].at[k], slot(k, i, low), wsem.at[k, i])
 
     def swapped(k, i):
-        return pltpu.make_async_copy((in0, out0)[i] if k == 0 else in1, slot(k, i, low), wsem.at[k, i])
+        return pltpu.make_async_copy((in0, out0)[i], slot(k, i, low), wsem.at[k, i])
 
     swap_out = remote(exp_out.at[1], slot(1, 1, low), ss.at[0], sr.at[0], at.swap_mate)
+    swap_in = remote(exp_in.at[1], slot(1, 0, low), ss.at[3], sr.at[3], at.swap_mate)
 
     def share(k, i):
         return remote(slot(k, i, low), slot(k, i, high), bs.at[k, i], br.at[k, i], at.other)
@@ -662,7 +682,7 @@
             load(k, i).start()
 
     def begin_swapped():
-        for k, i in ((0, 0), (0, 1), (1, 0)):
+        for k, i in ((0, 0), (0, 1)):
             swapped(k, i).start()
 
     on_either(begin_same, begin_swapped)
@@ -697,8 +717,12 @@
     sc[0] = jnp.broadcast_to(scale, (128, 128))
     e0[block(z), :] = (xhat * gain[0] + bias[0]).astype(jnp.bfloat16)
     line.begin(0, e0)
-    pl.when(jnp.logical_not(same))(lambda: swap_out.start())
-    wait_loads(1, 0)
+
+    @pl.when(jnp.logical_not(same))
+    def _():
+        swap_in.start()
+        swap_out.start()
+
     gating = jax.nn.sigmoid(split_sum(rows * vec[4:5, :]))
     gates[z] = jnp.broadcast_to(gating, (128, 128))
 
@@ -752,6 +776,8 @@
         return carry
 
     lax.fori_loop(0, 4, sub0, 0)
+    on_either(lambda: load(1, 0).wait(), lambda: swap_in.wait())
+    share(1, 0).start()
     on_either(lambda: load(1, 1).wait(), lambda: swap_out.wait())
     share(1, 1).start()
     stream = arrived[...] + line.total(1, ps0, pr0)
@@ -952,7 +978,7 @@
         vecg[...] = vswap[...]
 
 
-def expert_call(hid, route, exp_gain, exp_bias, centroid, cz, exp_in, exp_out, in0, out0, in1):
+def expert_call(hid, route, exp_gain, exp_bias, centroid, cz, exp_in, exp_out, in0, out0):
     bf, f32 = jnp.bfloat16, jnp.float32
     vmem, anywhere = pl.BlockSpec(memory_space=pltpu.VMEM), pl.BlockSpec(memory_space=pl.ANY)
     shape, V, dma = jax.ShapeDtypeStruct, pltpu.VMEM, pltpu.SemaphoreType.DMA
@@ -966,7 +992,7 @@
             shape((512, 1024), bf), shape((1024, 512), bf), shape((512, 1024), bf), shape((1024, 512), bf),
             shape((512, 1024), bf),
         ),
-        in_specs=[vmem] * 5 + [anywhere] * 6,
+        in_specs=[vmem] * 5 + [anywhere] * 5,
         out_specs=tuple([vmem] * 4 + [anywhere] * 5),
         scratch_shapes=[
             V((2, 1024, 1024), bf), V((2, 1024, 1024), bf), *(pieces * 4), *line,
@@ -976,11 +1002,11 @@
             V((2, 1024, 512), bf), V((2, 512, 1024), bf), V((2, 1024, 512), bf), V((2, 512, 1024), bf),
             *(vectors * 5), V((4, 8, 1024), f32), *(vectors * 2),
             dma((3, 2)), dma((9, 4)), dma((9, 4)), dma((2, 15)), dma((2, 15)), dma((2, 2)), dma((2, 2)), dma((2, 2)),
-            dma((2, 2)), dma((2, 2)), dma((3,)), dma((3,)), dma((3,)), dma((3,)),
+            dma((2, 2)), dma((2, 2)), dma((4,)), dma((4,)), dma((3,)), dma((3,)),
         ],
         compiler_params=pltpu.CompilerParams(collective_id=1, has_side_effects=True, vmem_limit_bytes=60 << 20),
         name="experts",
-    )(hid, route, exp_gain, exp_bias, centroid, cz, exp_in, exp_out, in0, out0, in1)
+    )(hid, route, exp_gain, exp_bias, centroid, cz, exp_in, exp_out, in0, out0)
 
 
 class Everyone:
@@ -1012,8 +1038,8 @@
     wd_h, ps_h, gin0, gout0,
     gx, bd, bu, bo, bq, gvec, res, fin0, fout0,
     ghs, xa, xh, n1, n2, act, dg, gp, qb, kvb, kvo, wq, wo, wu, wd,
-    ps, pr, ps2, pr2, ps3, pr3, gms, gm, dp, dkv, dkvo, kvs, kvr,
-    md, mu, mo, mq, td, tu, to, tq, rd, ru, ro, rq, xd, xu, xo, sd, su, so, yd, yu, yo, rp, sendr, arrr,
+    ps, pr, ps2, pr2, ps3, pr3, prob, gms, gm, dp, dkv, dkvo, kvs, kvr,
+    md, mu, mo, mq, mkv, td, tu, to, tq, tkv, rd, ru, ro, rq, rkv, xd, xu, xo, sd, su, so, yd, yu, yo, rp, rpkv, sendr, arrr,
     vmine, vcore, vplane, vline, outz,
     lsem, zs, zr, xs, xr, ys, yr, kvss, kvsr, ks, kr, cs, cr, qs, qr, ss, sr, vs, vr,
 ):
@@ -1032,8 +1058,8 @@
         pltpu.make_async_copy(src, dst, lsem.at[k])
         for k, (src, dst) in enumerate(
             [
-                (wd_h, wd), (dg_h, dg), (wu_h, wu), (act_h, act), (n2_h, n2), (wo_h, wo), (ps_h, ps3), (q_h, qb),
-                (kv_h, kvb), (kvo_h, kvo), (wq_h, wq), (n1_h, n1), (x_h, xa),
+                (q_h, qb), (kv_h, kvb), (kvo_h, kvo), (wd_h, wd), (dg_h, dg), (wu_h, wu), (act_h, act), (n2_h, n2),
+                (wo_h, wo), (ps_h, ps3), (wq_h, wq), (n1_h, n1), (x_h, xa),
             ]
         )
     ]
@@ -1046,22 +1072,25 @@
         remote(gin0, fin0, ss.at[0], sr.at[0], at.swap_mate),
         remote(gout0, fout0, ss.at[1], sr.at[1], at.swap_mate),
     ]
-    keeps = [
-        pltpu.make_async_copy(gin0, fin0, lsem.at[13]),
-        pltpu.make_async_copy(gout0, fout0, lsem.at[14]),
-    ]
-
-    @pl.when(at.same)
-    def _():
-        for keep in keeps:
-            keep.start()
-
     @pl.when(jnp.logical_not(at.same))
     def _():
         for swap in swaps:
             swap.start()
 
     for load in loads[:3]:
+        load.wait()
+    for j in range(4):
+        seen = [mask(j, yh, parity, docs) for parity in (yh, 1 - yh)]
+        wide = slice(0, 128 * (j + 1))
+        for p in range(2):
+            lanes = slice(128 * p, 128 * p + 128)
+            keys = [kvb[wide, lanes], kvo[wide, lanes]]
+            q = qb[128 * j : 128 * j + 128, lanes]
+            for h in range(2):
+                found = probabilities(only(head_lanes(h), q), keys, seen)
+                for k in range(2):
+                    prob[k, 4 * j + 2 * p + h, :, wide] = found[k].astype(jnp.bfloat16)
+    for load in loads[3:6]:
         load.wait()
 
     def feed(i, carry):
@@ -1085,7 +1114,7 @@
         return carry
 
     lax.fori_loop(0, 4, feed, 0)
-    for load in loads[3:7]:
+    for load in loads[6:10]:
         load.wait()
 
     def weight_grad(lhs, rhs, mine, theirs):
@@ -1175,11 +1204,12 @@
     gp[block(0), :] = grad_attn
     weight_grad(mixed, gp.at[block(0)], mo, to)
     core_copy(2, to, ro).start()
-    to_y(0, md, xd, sd, yd)
+    for load in loads[10:]:
+        load.wait()
+    for j in range(4):
+        xh[block(j), :] = norm_parts(xa[block(j), :].astype(jnp.float32))[0]
     join_cores(2, mo, to, ro)
     to_x(2, mo, xo)
-    for load in loads[7:]:
-        load.wait()
     for d in (1, 3, 2):
         line.arrived(2, d, gm)
     dkv[...] = jnp.zeros_like(dkv)
@@ -1189,7 +1219,6 @@
         return remote(kvs.at[block(j)], kvr.at[block(j)], kvss.at[j], kvsr.at[j], at.mate)
 
     def attend_back(j):
-        seen = masks(j, yh, docs)
         wide = slice(0, 128 * (j + 1))
         rows = slice(128 * j, 128 * j + 128)
         for p in range(2):
@@ -1201,23 +1230,23 @@
             outs = []
             for h in range(2):
                 q_h, grad_h = only(head_lanes(h), q), only(head_lanes(h), grad)
-                probs = probabilities(q_h, keys, seen)
+                probs = [prob[k, 4 * j + 2 * p + h, :, wide].astype(jnp.float32) for k in range(2)]
                 back = [nt(grad_h, v) for v in values]
                 dot = split_sum(probs[0] * back[0]) + split_sum(probs[1] * back[1])
-                slopes = [(prob * (b - dot)).astype(jnp.bfloat16) for prob, b in zip(probs, back)]
+                slopes = [(share * (b - dot)).astype(jnp.bfloat16) for share, b in zip(probs, back)]
                 outs.append(nn(slopes[0], keys[0]) + nn(slopes[1], keys[1]))
                 for k, acc in enumerate((dkv, dkvo)):
                     acc[wide, lanes] += tn(slopes[k], q_h) * 0.125
-                    acc[wide, value_lanes] += tn(probs[k].astype(jnp.bfloat16), grad_h)
+                    acc[wide, value_lanes] += tn(prob[k, 4 * j + 2 * p + h, :, wide], grad_h)
             dp[rows, lanes] = (jnp.where(head_lanes(0), outs[0], outs[1]) * 0.125).astype(jnp.bfloat16)
         kvs[rows, :] = dkvo[rows, :].astype(jnp.bfloat16)
         kv_copy(j).start()
 
     for j in (3, 2, 1, 0):
         attend_back(j)
-    bd[at.s] = y_total(0, sd, yd).astype(jnp.bfloat16)
-    everyone.start(0, bd)
-    to_y(1, mu, xu, su, yu)
+    to_y(0, md, xd, sd, yd)
+    weight_grad(n1, dp.at[:, 0:256], mq, tq)
+    core_copy(3, tq, rq).start()
     vmine[0:1, :] = jnp.zeros((1, 1024), jnp.float32)
     vmine[2:3, :] = jnp.zeros((1, 1024), jnp.float32)
     vmine[4:8, :] = jnp.zeros((4, 1024), jnp.float32)
@@ -1225,17 +1254,45 @@
         rows = slice(128 * j, 128 * j + 128)
         kv_copy(j).wait_recv()
         dp[rows, 256:768] = (dkv[rows, :] + kvr[rows, :].astype(jnp.float32)).astype(jnp.bfloat16)
+    weight_grad(n1, dp.at[:, 256:768], mkv, tkv)
+    core_copy(4, tkv, rkv).start()
+
+    def piece_of(mine):
+        def at_piece(q):
+            return mine.at[lax.div(q, 8), lax.rem(lax.div(q, 2), 4), pl.ds(pl.multiple_of(32 * lax.rem(q, 2), 32), 32)]
+
+        return at_piece
+
+    def slot_of(got):
+        return lambda q: got.at[q]
+
+    def to_plane(phase, mine, got):
+        plane.start(phase, piece_of(mine), slot_of(got))
+        got[at.m] = mine[at.yl, at.x, pl.ds(pl.multiple_of(32 * yh, 32), 32), :]
+
+    def plane_total(phase, got):
+        plane.wait(phase, slot_of(got))
+        acc = got[0].astype(jnp.float32)
+        for q in range(1, 16):
+            acc += got[q].astype(jnp.float32)
+        return acc.astype(jnp.bfloat16)
+
+    join_cores(3, mq, tq, rq)
+    to_plane(0, mq, rp)
+    bd[at.s] = y_total(0, sd, yd).astype(jnp.bfloat16)
+    everyone.start(0, bd)
+    join_cores(4, mkv, tkv, rkv)
+    to_plane(3, mkv, rpkv)
 
     def last(i, carry):
         d = order(3 - i)
         j = line.index(d)
         values = dp[block(j), :]
-        xh[...] = norm_parts(xa[block(j), :].astype(jnp.float32))[0]
         for n in range(4):
             tile = slice(n * 256, (n + 1) * 256)
             part = nt(values, tall_tile(wq, n))
             ps2[block(j), tile] = part.astype(jnp.bfloat16)
-            vmine[0:1, tile] += jnp.sum(part * xh[:, tile], axis=0, keepdims=True)
+            vmine[0:1, tile] += jnp.sum(part * xh[block(j), tile], axis=0, keepdims=True)
             vmine[2:3, tile] += jnp.sum(part, axis=0, keepdims=True)
 
         @pl.when(i < 3)
@@ -1247,28 +1304,14 @@
     lax.fori_loop(0, 4, last, 0)
     give_core = remote(vmine, vcore, vs.at[0], vr.at[0], at.other)
     give_core.start()
-    weight_grad(n1, dp, mq, tq)
-    core_copy(3, tq, rq).start()
+    to_y(1, mu, xu, su, yu)
 
     def tile_of(q):
         return vmine.at[:, pl.ds(pl.multiple_of(128 * lax.div(q, 2), 128), 128)]
 
-    def slot_v(q):
-        return vplane.at[q]
-
     give_core.wait()
     vmine[...] += vcore[...]
-    join_cores(3, mq, tq, rq)
-
-    def piece_q(q):
-        return mq.at[lax.div(q, 8), lax.rem(lax.div(q, 2), 4), pl.ds(pl.multiple_of(32 * lax.rem(q, 2), 32), 32)]
-
-    def slot_q(q):
-        return rp.at[q]
-
-    plane.start(0, piece_q, slot_q)
-    rp[at.m] = mq[at.yl, at.x, pl.ds(pl.multiple_of(32 * yh, 32), 32), :]
-    plane.start(1, tile_of, slot_v)
+    plane.start(1, tile_of, slot_of(vplane))
     vplane[at.m] = vmine[:, pl.ds(pl.multiple_of(128 * col, 128), 128)]
     to_y(2, mo, xo, so, yo)
     bu[at.s] = y_total(1, su, yu).astype(jnp.bfloat16)
@@ -1286,13 +1329,10 @@
     for d in (1, 3, 2):
         out_copy(d).start()
     grad_normed = line.total(3, ps2, pr2)
-    xhat, scale = norm_parts(xa[block(z), :].astype(jnp.float32))
-    gx[...] += norm_back(grad_normed, gains[0:1, :], xhat, scale)
-    plane.wait(0, slot_q)
-    acc = rp[0].astype(jnp.float32)
-    for q in range(1, 16):
-        acc += rp[q].astype(jnp.float32)
-    bq[at.s] = acc.astype(jnp.bfloat16)
+    scale = norm_parts(xa[block(z), :].astype(jnp.float32))[1]
+    gx[...] += norm_back(grad_normed, gains[0:1, :], xh[block(z), :], scale)
+    bq[at.s, :, 0:256] = plane_total(0, rp)
+    bq[at.s, :, 256:768] = plane_total(3, rpkv)
     everyone.start(3, bq)
     acc = outz[4 + z].astype(jnp.float32)
     for d in (1, 3, 2):
@@ -1300,7 +1340,7 @@
         acc += outz[line.index(d)].astype(jnp.float32)
     bo[at.s] = acc.astype(jnp.bfloat16)
     everyone.start(2, bo)
-    plane.wait(1, slot_v)
+    plane.wait(1, slot_of(vplane))
     vline[z] = jnp.sum(vplane[...], axis=0)
 
     def vec_copy(d):
@@ -1331,16 +1371,12 @@
             y_copy(phase, d, part, y_got).wait_send()
     for j in range(4):
         kv_copy(j).wait_send()
-    plane.sent(0, piece_q, slot_q)
-    plane.sent(1, tile_of, slot_v)
+    plane.sent(0, piece_of(mq), slot_of(rp))
+    plane.sent(3, piece_of(mkv), slot_of(rpkv))
+    plane.sent(1, tile_of, slot_of(vplane))
     plane.sent(2, piece(sendr), piece(arrr))
     for phase, buf in enumerate((bd, bu, bo, bq)):
         everyone.sent(phase, buf)
-
-    @pl.when(at.same)
-    def _():
-        for keep in keeps:
-            keep.wait()
 
     @pl.when(jnp.logical_not(at.same))
     def _():
@@ -1354,7 +1390,7 @@
     smem = pl.BlockSpec(memory_space=pltpu.SMEM)
     shape, V, dma = jax.ShapeDtypeStruct, pltpu.VMEM, pltpu.SemaphoreType.DMA
     line, pieces = [V((512, 1024), bf)], [V((256, 512), bf)]
-    wide, narrow = [V((2, 4, 64, 1024), bf)], [V((2, 4, 64, 768), bf)]
+    wide, narrow = [V((2, 4, 64, 1024), bf)], [V((2, 4, 64, 256), bf), V((2, 4, 64, 512), bf)]
     return pl.pallas_call(
         dense_backward_kernel,
         out_shape=[
@@ -1365,19 +1401,19 @@
         in_specs=[vmem, vmem, smem] + [vmem] * 5 + [anywhere] * 15,
         out_specs=[vmem] * 7 + [anywhere] * 2,
         scratch_shapes=[
-            *(line * 2), V((128, 1024), f32), *(line * 3), V((512, 1024), f32), *line,
+            *(line * 2), V((512, 1024), f32), *(line * 3), V((512, 1024), f32), *line,
             V((512, 256), bf), V((512, 512), bf), V((512, 512), bf),
             V((2, 4, 2, 2, 32, 768), bf), *([V((2, 4, 2, 2, 32, 1024), bf)] * 3),
-            *(line * 6),
+            *(line * 6), V((2, 16, 128, 512), bf),
             V((128, 1024), bf), V((512, 256), bf), V((512, 768), bf), V((512, 512), f32), V((512, 512), f32),
             V((512, 512), bf), V((512, 512), bf),
             *(wide * 3), *narrow, *(wide * 3), *narrow, *(wide * 3), *narrow,
             *([V((4, 2, 64, 1024), bf)] * 3), *([V((2, 64, 1024), bf)] * 3), *([V((4, 32, 1024), bf)] * 3),
-            V((16, 32, 768), bf), *(pieces * 2),
+            V((16, 32, 256), bf), V((16, 32, 512), bf), *(pieces * 2),
             V((8, 1024), f32), V((8, 1024), f32), V((16, 8, 128), f32), V((4, 8, 128), f32),
             V((8, 32, 256), bf),
-            dma((15,)), dma((7, 4)), dma((7, 4)), dma((3, 3)), dma((3, 3)), dma((3, 3)), dma((3, 3)), dma((4,)),
-            dma((4,)), dma((4,)), dma((4,)), dma((3, 15)), dma((3, 15)), dma((4, 7)), dma((4, 7)), dma((2,)),
+            dma((13,)), dma((7, 4)), dma((7, 4)), dma((3, 3)), dma((3, 3)), dma((3, 3)), dma((3, 3)), dma((4,)),
+            dma((4,)), dma((5,)), dma((5,)), dma((4, 15)), dma((4, 15)), dma((4, 7)), dma((4, 7)), dma((2,)),
             dma((2,)), dma((1,)), dma((1,)),
         ],
         compiler_params=pltpu.CompilerParams(collective_id=3, has_side_effects=True, vmem_limit_bytes=62 << 20),
@@ -1386,19 +1422,34 @@
 
 
 def finish_kernel(
-    gvec, vecg, res, gx, bd, bu, bo, bq, in0, in1, out0, out1,
+    gvec, vecg, res, gx, bd, bu, bo, bq, in0, in1, out0, out1, swapped_in, swapped_out,
     ng, nb, eg, eb, cen, o_res, o_gx, o_gq, o_go, o_gu, o_gd, o_in, o_out,
-    b_in, b_out, f_in, f_out, vd, vu, vo, vq, gq, go, gu, gd, isem, osem,
+    b_in, b_out, f_in, f_out, vd, vu, vo, vq, gq, go, gu, gd, vres, vgx, isem, osem,
 ):
-    whole = [pltpu.make_async_copy(res, o_res, osem.at[0]), pltpu.make_async_copy(gx, o_gx, osem.at[1])]
+    at = Place()
+    swapped = [
+        pltpu.make_async_copy(swapped_in, b_in.at[0], isem.at[0]),
+        pltpu.make_async_copy(swapped_out, b_out.at[0], isem.at[2]),
+    ]
     pairs = [
         (in0, b_in.at[0]), (in1, b_in.at[1]), (out0, b_out.at[0]), (out1, b_out.at[1]), (bd, vd), (bu, vu), (bo, vo),
-        (bq, vq),
+        (bq, vq), (res, vres), (gx, vgx),
     ]
     loads = [pltpu.make_async_copy(src, dst, isem.at[k]) for k, (src, dst) in enumerate(pairs)]
-    for copy in loads + whole:
-        copy.start()
-    c = lax.rem(lax.axis_index("fsdp"), 2)
+
+    @pl.when(at.same)
+    def _():
+        loads[0].start()
+        loads[2].start()
+
+    @pl.when(jnp.logical_not(at.same))
+    def _():
+        for copy in swapped:
+            copy.start()
+
+    for k in (1, 3, 4, 5, 6, 7, 8, 9):
+        loads[k].start()
+    c = at.c
     mine = jnp.where(c == 0, gvec[0:4, 0:64], gvec[0:4, 64:128])
     ng[...] = mine[0:2]
     nb[...] = mine[2:4]
@@ -1408,7 +1459,7 @@
     stores = []
 
     def store(src, dst):
-        stores.append(pltpu.make_async_copy(src, dst, osem.at[2 + len(stores)]))
+        stores.append(pltpu.make_async_copy(src, dst, osem.at[len(stores)]))
         stores[-1].start()
 
     for k in range(4):
@@ -1416,8 +1467,10 @@
         low, wide, out = ((b_in, f_in, o_in), (b_out, f_out, o_out))[k // 2]
         wide[k % 2] = low[k % 2].astype(jnp.float32)
         store(wide.at[k % 2], out.at[k % 2])
-    for k in range(4, 8):
+    for k in range(4, 10):
         loads[k].wait()
+    store(vres, o_res)
+    store(vgx, o_gx)
     lane = lax.broadcasted_iota(jnp.int32, (32, 128), 1) < 64
     for half in range(2):
         rows = slice(32 * half, 32 * half + 32)
@@ -1439,11 +1492,11 @@
             gu[rows, first + 384 : first + 512] = jnp.where(lane, turned[2], quarter[3])
     for src, dst in ((gq, o_gq), (go, o_go), (gu, o_gu), (gd, o_gd)):
         store(src, dst)
-    for copy in whole + stores:
+    for copy in stores:
         copy.wait()
 
 
-def finish_call(gvec, vecg, res, gx, bd, bu, bo, bq, in0, in1, out0, out1):
+def finish_call(gvec, vecg, res, gx, bd, bu, bo, bq, in0, in1, out0, out1, swapped_in, swapped_out):
     bf, f32 = jnp.bfloat16, jnp.float32
     vmem, anywhere = pl.BlockSpec(memory_space=pltpu.VMEM), pl.BlockSpec(memory_space=pl.ANY)
     shape, V, dma = jax.ShapeDtypeStruct, pltpu.VMEM, pltpu.SemaphoreType.DMA
@@ -1455,17 +1508,17 @@
             shape((64, 1024), f32), shape((64, 4096), f32), shape((256, 1024), f32), shape((2, 1024, 512), f32),
             shape((2, 512, 1024), f32),
         ],
-        in_specs=[vmem] * 2 + [anywhere] * 10,
+        in_specs=[vmem] * 2 + [anywhere] * 12,
         out_specs=[vmem] * 5 + [anywhere] * 8,
         scratch_shapes=[
             V((2, 1024, 512), bf), V((2, 512, 1024), bf), V((2, 1024, 512), f32), V((2, 512, 1024), f32),
             V((8, 32, 1024), bf), V((8, 32, 1024), bf), V((8, 32, 256), bf), V((8, 32, 768), bf),
             V((64, 3072), f32), V((64, 1024), f32), V((64, 4096), f32), V((256, 1024), f32),
-            dma((8,)), dma((10,)),
+            V((128, 1024), bf), V((128, 1024), f32), dma((10,)), dma((10,)),
         ],
         compiler_params=pltpu.CompilerParams(vmem_limit_bytes=62 << 20),
         name="finish",
-    )(gvec, vecg, res, gx, bd, bu, bo, bq, in0, in1, out0, out1)
+    )(gvec, vecg, res, gx, bd, bu, bo, bq, in0, in1, out0, out1, swapped_in, swapped_out)
 
 
 def on_device(
@@ -1489,17 +1542,30 @@
     x = inputs.reshape(tok_rows, width)
     cot = cotangent.reshape(tok_rows, width)
     slots = route.reshape(1, tok_rows)
-    hidden, mixed, after, gains, *saved, cz, in0, out0, in1 = dense_forward_call(
+    hidden, mixed, after, gains, *saved, cz, in0, out0 = dense_forward_call(
         x, norm_gain, norm_bias, doc_starts, slots, cot, w_qkv, w_out, w_up, w_down, exp_in[0], exp_out[0]
     )
     grad_hidden, vec_grads, mid, gate, part, grad_in1, grad_out1, grad_in0, grad_out0 = expert_call(
-        hidden, slots, exp_gain[0], exp_bias[0], centroid, cz, exp_in[0], exp_out[0], in0, out0, in1
+        hidden, slots, exp_gain[0], exp_bias[0], centroid, cz, exp_in[0], exp_out[0], in0, out0
     )
-    grad_x, down, up, out, qkv, norm_grads, result, grad_in0, grad_out0 = dense_backward_call(
+    grad_x, down, up, out, qkv, norm_grads, result, swapped_in, swapped_out = dense_backward_call(
         grad_hidden, after, doc_starts, gains, mixed, slots, mid, gate, saved, part, grad_in0, grad_out0
     )
     gain, bias, e_gain, e_bias, center, result, grad_x, g_qkv, g_out, g_up, g_down, e_in, e_out = finish_call(
-        norm_grads, vec_grads, result, grad_x, down, up, out, qkv, grad_in0, grad_in1, grad_out0, grad_out1
+        norm_grads,
+        vec_grads,
+        result,
+        grad_x,
+        down,
+        up,
+        out,
+        qkv,
+        grad_in0,
+        grad_in1,
+        grad_out0,
+        grad_out1,
+        swapped_in,
+        swapped_out,
     )
     return (
         result[None],

time: 314 us -> 282 us (0.90)
  Pallas kernels: 310 us -> 278 us
    pallas_call x1, Pallas kernels: 26.5 us -> 7.7 us  [finish_call(): pl.pallas_call(finish_kernel, out_shape=[shape((2, 64), f32), shape((2, 6...]
    pallas_call x1, Pallas kernels: 87.1 us -> 76 us  [dense_forward_call(): pl.pallas_call(dense_forward_kernel, out_shape=[shape((128, 1024), bf), s...]
where the time goes in v5:
time: 282 us; the launch traced here: 279 us
  Pallas kernels  278 us (99%)
    pallas_call x1, Pallas kernels, dense_backward_call(): pl.pallas_call(dense_backward_kernel, out_shape=[shape((128, 1024), f32),...  99.9 us
    pallas_call x1, Pallas kernels, expert_call(): pl.pallas_call(expert_kernel, out_shape=(shape((128, 1024), bf), shape((8...  94.4 us
    pallas_call x1, Pallas kernels, dense_forward_call(): pl.pallas_call(dense_forward_kernel, out_shape=[shape((128, 1024), bf), s...  76 us
    pallas_call x1, Pallas kernels, finish_call(): pl.pallas_call(finish_kernel, out_shape=[shape((2, 64), f32), shape((2, 6...  7.7 us

profile of v5, /device:TPU:4, one launch (start us, length us, event | category | flops | bytes accessed | tf_op | source)
XLA Modules:
  0.0 279.0 jit_solution(12027313739442100962)
XLA Ops:
  0.6 76.0 %dense_forward.1 = (bf16[128,1024]{1,0:T(8,128)(2,1)}, bf16[128,1024]{1,0:T(8,128)(2,1)}, f32[128,1024]{1,0:T(8,128)}, f32[8,1024]{1,0:T(8,128)}, bf16[512,1024]...) custom-call(bf16[128,1024]{1,0:T(8,128)(2,1)} %bitcast.17, ...), custom_call_target="tpu_custom_call" | custom-call | tf_op jit(solution)/shard_map/dense_forward/pallas_call | solution.py:619
  76.7 94.4 %experts.1 = (bf16[128,1024]{1,0:T(8,128)(2,1)}, f32[8,1024]{1,0:T(8,128)}, f32[128,1024]{1,0:T(8,128)}, f32[128,128]{1,0:T(8,128)}, bf16[512,1024]{1,0:T(8,128)...) custom-call(bf16[128,1024]{1,0:T(8,128)(2,1)} %get-tuple-element.63., ...), custom_call_target="tpu_custom_call" | custom-call | tf_op jit(solution)/shard_map/experts/pallas_call | solution.py:988
  171.1 99.9 %dense_backward.1 = (f32[128,1024]{1,0:T(8,128)}, bf16[8,32,1024]{2,1,0:T(8,128)(2,1)}, bf16[8,32,1024]{2,1,0:T(8,128)(2,1)}, bf16[8,32,256]{2,1,0:T(8,128)(2,1)...) custom-call(bf16[128,1024]{1,0:T(8,128)(2,1)} %get-tuple-element.67., ...), custom_call_target="tpu_custom_call" | custom-call | tf_op jit(solution)/shard_map/dense_backward/pallas_call | solution.py:1394
  271.1 7.7 %finish.1 = (f32[2,64]{1,0:T(2,128)}, f32[2,64]{1,0:T(2,128)}, f32[2,1024]{1,0:T(2,128)}, f32[2,1024]{1,0:T(2,128)}, f32[1,1024]{1,0:T(1,128)}, /*index=5*/bf16[...) custom-call(f32[8,128]{1,0:T(8,128)} %get-tuple-element.88.gvec, ...), custom_call_target="tpu_custom_call" | custom-call | tf_op jit(solution)/shard_map/finish/pallas_call | solution.py:1503

commit v6 on v5

--- a/solution.py
+++ b/solution.py
@@ -110,45 +110,53 @@
         for d in (1, 3, 2):
             self.copy(phase, d, own, own).start()
 
-    def near(self, phase, d, buf):
-        own = buf.at[block(self.pos)]
-        return self.copy(phase, d, own, own)
-
     def half(self, buf, d, upper):
         return buf.at[pl.ds(pl.multiple_of(128 * self.index(d) + 64 * upper, 64), 64)]
 
-    def onward(self, phase, buf, upper):
-        rows = self.half(buf, 3 if upper else 1, upper)
-        slot = 3 if upper else 1
-        to = self.device(self.index(1 if upper else 3))
+    def moving(self, phase, slot, rows, up):
+        to = self.device(self.index(1 if up else 3))
         return remote(rows, rows, self.send.at[phase, slot], self.recv.at[phase, slot], to)
 
+    def parts(self, phase, buf):
+        for slot, up, upper in ((2, 0, 0), (0, 1, 1), (3, 0, 1), (1, 1, 0)):
+            yield self.moving(phase, slot, self.half(buf, 0, upper), up)
+
+    def onward(self, phase, buf, up):
+        return self.moving(phase, 4 + up, self.half(buf, 3 if up else 1, up), up)
+
     def begin(self, phase, buf):
-        for d in (1, 3):
-            self.near(phase, d, buf).start()
+        for part in self.parts(phase, buf):
+            part.start()
 
     def relay(self, phase, buf):
-        for d in (1, 3):
-            self.arrived(phase, d, buf)
-        for upper in (0, 1):
-            self.onward(phase, buf, upper).start()
+        for up in (0, 1):
+            self.moving(phase, 0 if up else 2, self.half(buf, 3 if up else 1, up), up).wait_recv()
+            self.onward(phase, buf, up).start()
+
+    def above(self, phase, buf):
+        self.moving(phase, 3, self.half(buf, 1, 1), 0).wait_recv()
+
+    def below(self, phase, buf):
+        self.moving(phase, 1, self.half(buf, 3, 0), 1).wait_recv()
 
     def far(self, phase, buf):
-        for upper in (0, 1):
-            slot = 3 if upper else 1
-            rows = self.half(buf, 2, upper)
-            to = self.device(self.index(1 if upper else 3))
-            remote(rows, rows, self.send.at[phase, slot], self.recv.at[phase, slot], to).wait_recv()
+        for up in (0, 1):
+            self.moving(phase, 4 + up, self.half(buf, 2, up), up).wait_recv()
 
     def ready(self, phase, i, buf):
-        pl.when(i == 1)(lambda: self.relay(phase, buf))
+        @pl.when(i == 1)
+        def _():
+            self.relay(phase, buf)
+            self.above(phase, buf)
+
+        pl.when(i == 2)(lambda: self.below(phase, buf))
         pl.when(i == 3)(lambda: self.far(phase, buf))
 
     def sent_all(self, phase, buf):
-        for d in (1, 3):
-            self.near(phase, d, buf).wait_send()
-        for upper in (0, 1):
-            self.onward(phase, buf, upper).wait_send()
+        for part in self.parts(phase, buf):
+            part.wait_send()
+        for up in (0, 1):
+            self.onward(phase, buf, up).wait_send()
 
     def arrived(self, phase, d, buf):
         self.got(phase, d, buf.at[block(self.index(d))])
@@ -416,10 +424,10 @@
     qkv_b.start()
     plane.start(0, piece(sendc), piece(arrc))
     keep_piece(at, sendc, arrc)
+    qkv_a.turn()
+    qkv_b.turn()
     for weight in (out, up, down):
         weight.start()
-    qkv_a.turn()
-    qkv_b.turn()
     line.relay(0, xa)
 
     def wait_gain(i, carry):
@@ -443,6 +451,8 @@
 
     def project_qkv(i, carry):
         j = line.index(order(i))
+        pl.when(i == 1)(lambda: line.above(0, xa))
+        pl.when(i == 2)(lambda: line.below(0, xa))
         pl.when(i == 3)(lambda: line.far(0, xa))
         xhat = norm_parts(xa[block(j), :].astype(jnp.float32))[0]
         n1[block(j), :] = (xhat * gains[0:1, :] + gains[2:3, :]).astype(jnp.bfloat16)
@@ -627,7 +637,7 @@
             V((8, 1024), f32),
             *(line * 4), V((512, 256), bf), V((512, 512), bf), V((512, 512), bf), V((512, 256), bf),
             *line, V((512, 1024), f32), *(line * 2), V((256, 512), bf), V((256, 512), bf),
-            V((16, 128, 128), f32), V((512, 256), f32), dma((5, 4)), dma((5, 4)), dma((5, 3)), dma((5, 3)), dma((5, 3)), dma((5, 3)), dma((4,)), dma((4,)),
+            V((16, 128, 128), f32), V((512, 256), f32), dma((5, 6)), dma((5, 6)), dma((5, 3)), dma((5, 3)), dma((5, 3)), dma((5, 3)), dma((4,)), dma((4,)),
             dma((5,)), dma((5,)), dma((8,)), dma((8,)), dma((1, 15)), dma((1, 15)), dma((3,)), dma((3,)), dma((13,)),
         ],
         compiler_params=pltpu.CompilerParams(collective_id=2, has_side_effects=True, vmem_limit_bytes=60 << 20),
@@ -642,7 +652,7 @@
     e0, e1, g0, g1, ps0, ps1, pr0, pb0, pb1,
     act0, act1, dg0, dg1, gp0, gp1,
     arrived, base, xh0, xh1, sc, gates, dots, dots_in,
-    ga_in, ga_out, sb_in, sb_out, rb_in, rb_out, vec, vec_own, vec_other, vmine, vcore, vline, vsum, vswap,
+    ga_in, ga_out, sb_in, sb_out, rb_in, rb_out, vec, vec_own, vec_other, vmine, vcore, vline,
     wsem, zs, zr, cs, cr, ks, kr, osem, bs, br, ss, sr, vs, vr,
 ):
     at = Place()
@@ -947,9 +957,7 @@
     gh[...] = from_pieces(left, right, arrg[...])
     for d in (1, 3, 2):
         line.got(8, d, vline.at[line.index(d)])
-    vsum[...] = vline[0] + vline[1] + vline[2] + vline[3]
-    give_mate = remote(vsum, vswap, vs.at[1], vr.at[1], at.swap_mate)
-    pl.when(jnp.logical_not(same))(lambda: give_mate.start())
+    vecg[...] = vline[0] + vline[1] + vline[2] + vline[3]
     give_core.wait_send()
     for d in (1, 3, 2):
         give_line(d).wait_send()
@@ -967,15 +975,6 @@
     keep_ps.wait()
     finish(stores)
     on_either(lambda: finish(kept), lambda: finish(given))
-
-    @pl.when(same)
-    def _():
-        vecg[...] = vsum[...]
-
-    @pl.when(jnp.logical_not(same))
-    def _():
-        give_mate.wait()
-        vecg[...] = vswap[...]
 
 
 def expert_call(hid, route, exp_gain, exp_bias, centroid, cz, exp_in, exp_out, in0, out0):
@@ -1000,8 +999,8 @@
             *(rows * 4), *(small * 4),
             V((2, 1024, 512), f32), V((2, 512, 1024), f32),
             V((2, 1024, 512), bf), V((2, 512, 1024), bf), V((2, 1024, 512), bf), V((2, 512, 1024), bf),
-            *(vectors * 5), V((4, 8, 1024), f32), *(vectors * 2),
-            dma((3, 2)), dma((9, 4)), dma((9, 4)), dma((2, 15)), dma((2, 15)), dma((2, 2)), dma((2, 2)), dma((2, 2)),
+            *(vectors * 5), V((4, 8, 1024), f32),
+            dma((3, 2)), dma((9, 6)), dma((9, 6)), dma((2, 15)), dma((2, 15)), dma((2, 2)), dma((2, 2)), dma((2, 2)),
             dma((2, 2)), dma((2, 2)), dma((4,)), dma((4,)), dma((3,)), dma((3,)),
         ],
         compiler_params=pltpu.CompilerParams(collective_id=1, has_side_effects=True, vmem_limit_bytes=60 << 20),
@@ -1034,14 +1033,14 @@
 
 
 def dense_backward_kernel(
-    gh, after, docs, gains, mixed, route, mid, gate, x_h, n1_h, n2_h, act_h, dg_h, q_h, kv_h, kvo_h, wq_h, wo_h, wu_h,
+    gh, after, docs, gains, mixed, route, mid, gate, vec_sum, x_h, n1_h, n2_h, act_h, dg_h, q_h, kv_h, kvo_h, wq_h, wo_h, wu_h,
     wd_h, ps_h, gin0, gout0,
-    gx, bd, bu, bo, bq, gvec, res, fin0, fout0,
+    gx, bd, bu, bo, bq, gvec, res, vec_swap, fin0, fout0,
     ghs, xa, xh, n1, n2, act, dg, gp, qb, kvb, kvo, wq, wo, wu, wd,
     ps, pr, ps2, pr2, ps3, pr3, prob, gms, gm, dp, dkv, dkvo, kvs, kvr,
     md, mu, mo, mq, mkv, td, tu, to, tq, tkv, rd, ru, ro, rq, rkv, xd, xu, xo, sd, su, so, yd, yu, yo, rp, rpkv, sendr, arrr,
     vmine, vcore, vplane, vline, outz,
-    lsem, zs, zr, xs, xr, ys, yr, kvss, kvsr, ks, kr, cs, cr, qs, qr, ss, sr, vs, vr,
+    lsem, zs, zr, xs, xr, ys, yr, kvss, kvsr, ks, kr, cs, cr, qs, qr, ss, sr, vs, vr, fs, fr,
 ):
     at = Place()
     z, yh, c, col = at.z, at.yh, at.c, at.col
@@ -1072,8 +1071,11 @@
         remote(gin0, fin0, ss.at[0], sr.at[0], at.swap_mate),
         remote(gout0, fout0, ss.at[1], sr.at[1], at.swap_mate),
     ]
+    give_vec = remote(vec_sum, vec_swap, ss.at[2], sr.at[2], at.swap_mate)
+
     @pl.when(jnp.logical_not(at.same))
     def _():
+        give_vec.start()
         for swap in swaps:
             swap.start()
 
@@ -1166,11 +1168,59 @@
         for d in (1, 3, 2):
             y_copy(phase, d, part, dst).start()
 
+    def fin_copy(phase, d, buf):
+        own = buf.at[yh, z]
+        return line.copy(phase, d, own, own)
+
+    def fin_mate(phase, buf):
+        own = buf.at[yh]
+        return remote(own, own, fs.at[phase], fr.at[phase], at.mate)
+
+    def fin_z(phase, buf, values):
+        buf[yh, z] = values.astype(jnp.bfloat16)
+        for d in (1, 3, 2):
+            fin_copy(phase, d, buf).start()
+
+    def fin_y(phase, buf):
+        for d in (1, 3, 2):
+            line.got(phase, d, buf.at[yh, line.index(d)])
+        fin_mate(phase, buf).start()
+
+    def fin_wait(phase, buf):
+        dst = buf.at[1 - yh]
+        remote(dst, dst, fs.at[phase], fr.at[phase], at.mate).wait_recv()
+
     def y_total(phase, part, got):
         acc = part[at.yl, pl.ds(pl.multiple_of(32 * yh, 32), 32), :].astype(jnp.float32)
         for d in (1, 3, 2):
             j = ring_y.index(d)
             ring_y.got(phase, d, got.at[j])
+            acc += got[j].astype(jnp.float32)
+        return acc
+
+    def y_first(phase, d, mine, dst):
+        j = ring_y.index(d)
+        src = mine.at[lax.rem(j, 2), :, pl.ds(pl.multiple_of(32 * lax.div(j, 2), 32), 32)]
+        return ring_y.copy(phase, d, src, dst.at[ring_y.pos])
+
+    def x_second(phase, d, part, dst):
+        return ring_x.copy(phase, d, part.at[ring_x.index(d)], dst.at[at.x])
+
+    def turn_to_x(phase, mine, got, part, dst):
+        acc = mine[at.yl, :, pl.ds(pl.multiple_of(32 * yh, 32), 32), :].astype(jnp.float32)
+        for d in (1, 3, 2):
+            j = ring_y.index(d)
+            ring_y.got(phase, d, got.at[j])
+            acc += got[j].astype(jnp.float32)
+        part[...] = acc.astype(jnp.bfloat16)
+        for d in (1, 3, 2):
+            x_second(phase, d, part, dst).start()
+
+    def x_total(phase, part, got):
+        acc = part[at.x].astype(jnp.float32)
+        for d in (1, 3, 2):
+            j = ring_x.index(d)
+            ring_x.got(phase, d, got.at[j])
             acc += got[j].astype(jnp.float32)
         return acc
 
@@ -1181,7 +1231,8 @@
     join_cores(0, md, td, rd)
     to_x(0, md, xd)
     join_cores(1, mu, tu, ru)
-    to_x(1, mu, xu)
+    for d in (1, 3, 2):
+        y_first(1, d, mu, xu).start()
     grad_normed = line.total(1, ps, pr)
     xhat, scale = norm_parts(after[...])
     vmine[1:2, :] = jnp.sum(grad_normed * xhat, axis=0, keepdims=True)
@@ -1199,8 +1250,6 @@
     for d in (1, 3, 2):
         gm_copy(d).start()
     gm[block(z), :] = gms[:, pl.ds(pl.multiple_of(256 * z, 256), 256)]
-    for d in (1, 3, 2):
-        line.give(6, d, ps3, pr3)
     gp[block(0), :] = grad_attn
     weight_grad(mixed, gp.at[block(0)], mo, to)
     core_copy(2, to, ro).start()
@@ -1212,6 +1261,8 @@
     to_x(2, mo, xo)
     for d in (1, 3, 2):
         line.arrived(2, d, gm)
+    for d in (1, 3, 2):
+        line.give(6, d, ps3, pr3)
     dkv[...] = jnp.zeros_like(dkv)
     dkvo[...] = jnp.zeros_like(dkvo)
 
@@ -1242,11 +1293,14 @@
         kvs[rows, :] = dkvo[rows, :].astype(jnp.bfloat16)
         kv_copy(j).start()
 
-    for j in (3, 2, 1, 0):
-        attend_back(j)
+    attend_back(3)
+    attend_back(2)
+    attend_back(1)
+    attend_back(0)
     to_y(0, md, xd, sd, yd)
     weight_grad(n1, dp.at[:, 0:256], mq, tq)
     core_copy(3, tq, rq).start()
+    turn_to_x(1, mu, xu, su, yu)
     vmine[0:1, :] = jnp.zeros((1, 1024), jnp.float32)
     vmine[2:3, :] = jnp.zeros((1, 1024), jnp.float32)
     vmine[4:8, :] = jnp.zeros((4, 1024), jnp.float32)
@@ -1256,6 +1310,8 @@
         dp[rows, 256:768] = (dkv[rows, :] + kvr[rows, :].astype(jnp.float32)).astype(jnp.bfloat16)
     weight_grad(n1, dp.at[:, 256:768], mkv, tkv)
     core_copy(4, tkv, rkv).start()
+    fin_z(7, bd, y_total(0, sd, yd))
+    to_y(2, mo, xo, so, yo)
 
     def piece_of(mine):
         def at_piece(q):
@@ -1279,8 +1335,6 @@
 
     join_cores(3, mq, tq, rq)
     to_plane(0, mq, rp)
-    bd[at.s] = y_total(0, sd, yd).astype(jnp.bfloat16)
-    everyone.start(0, bd)
     join_cores(4, mkv, tkv, rkv)
     to_plane(3, mkv, rpkv)
 
@@ -1290,10 +1344,7 @@
         values = dp[block(j), :]
         for n in range(4):
             tile = slice(n * 256, (n + 1) * 256)
-            part = nt(values, tall_tile(wq, n))
-            ps2[block(j), tile] = part.astype(jnp.bfloat16)
-            vmine[0:1, tile] += jnp.sum(part * xh[block(j), tile], axis=0, keepdims=True)
-            vmine[2:3, tile] += jnp.sum(part, axis=0, keepdims=True)
+            ps2[block(j), tile] = nt(values, tall_tile(wq, n)).astype(jnp.bfloat16)
 
         @pl.when(i < 3)
         def _():
@@ -1302,9 +1353,24 @@
         return carry
 
     lax.fori_loop(0, 4, last, 0)
+
+    def out_copy(d):
+        return line.copy(4, d, outz.at[4 + line.index(d)], outz.at[z])
+
+    fin_z(8, bu, x_total(1, su, yu))
+    total_out = y_total(2, so, yo)
+    for n in range(4):
+        outz[4 + n] = total_out[:, 256 * n : 256 * n + 256].astype(jnp.bfloat16)
+
+    for d in (1, 3, 2):
+        out_copy(d).start()
+    for j in range(4):
+        part = ps2[block(j), :].astype(jnp.float32)
+        vmine[0:1, :] += jnp.sum(part * xh[block(j), :], axis=0, keepdims=True)
+        vmine[2:3, :] += jnp.sum(part, axis=0, keepdims=True)
     give_core = remote(vmine, vcore, vs.at[0], vr.at[0], at.other)
     give_core.start()
-    to_y(1, mu, xu, su, yu)
+    fin_y(7, bd)
 
     def tile_of(q):
         return vmine.at[:, pl.ds(pl.multiple_of(128 * lax.div(q, 2), 128), 128)]
@@ -1313,33 +1379,19 @@
     vmine[...] += vcore[...]
     plane.start(1, tile_of, slot_of(vplane))
     vplane[at.m] = vmine[:, pl.ds(pl.multiple_of(128 * col, 128), 128)]
-    to_y(2, mo, xo, so, yo)
-    bu[at.s] = y_total(1, su, yu).astype(jnp.bfloat16)
-    everyone.start(1, bu)
     sendr[...] = pieces_of(mid[...] + gate[:, 0:1] * line.total(6, ps3, pr3))
     plane.start(2, piece(sendr), piece(arrr))
     keep_piece(at, sendr, arrr)
-    total_out = y_total(2, so, yo)
-    for n in range(4):
-        outz[4 + n] = total_out[:, 256 * n : 256 * n + 256].astype(jnp.bfloat16)
-
-    def out_copy(d):
-        return line.copy(4, d, outz.at[4 + line.index(d)], outz.at[z])
-
-    for d in (1, 3, 2):
-        out_copy(d).start()
-    grad_normed = line.total(3, ps2, pr2)
-    scale = norm_parts(xa[block(z), :].astype(jnp.float32))[1]
-    gx[...] += norm_back(grad_normed, gains[0:1, :], xh[block(z), :], scale)
-    bq[at.s, :, 0:256] = plane_total(0, rp)
-    bq[at.s, :, 256:768] = plane_total(3, rpkv)
-    everyone.start(3, bq)
+    fin_y(8, bu)
     acc = outz[4 + z].astype(jnp.float32)
     for d in (1, 3, 2):
         line.got(4, d, outz.at[line.index(d)])
         acc += outz[line.index(d)].astype(jnp.float32)
-    bo[at.s] = acc.astype(jnp.bfloat16)
-    everyone.start(2, bo)
+    fin_z(9, bo, acc)
+    bq[at.s, :, 0:256] = plane_total(0, rp)
+    bq[at.s, :, 256:768] = plane_total(3, rpkv)
+    everyone.start(0, bq)
+    fin_y(9, bo)
     plane.wait(1, slot_of(vplane))
     vline[z] = jnp.sum(vplane[...], axis=0)
 
@@ -1348,16 +1400,21 @@
 
     for d in (1, 3, 2):
         vec_copy(d).start()
+    grad_normed = line.total(3, ps2, pr2)
+    scale = norm_parts(xa[block(z), :].astype(jnp.float32))[1]
+    gx[...] += norm_back(grad_normed, gains[0:1, :], xh[block(z), :], scale)
     plane.wait(2, piece(arrr))
     left, right = placings(route[0:1, :])
     res[...] = from_pieces(left, right, arrr[...])
-    everyone.wait(0, bd)
-    everyone.wait(1, bu)
-    everyone.wait(2, bo)
+    fin_wait(7, bd)
+    fin_wait(8, bu)
     for d in (1, 3, 2):
         line.got(5, d, vline.at[line.index(d)])
     gvec[...] = jnp.sum(vline[...], axis=0)
-    everyone.wait(3, bq)
+    fin_wait(9, bo)
+    everyone.wait(0, bq)
+    if_swapped = jnp.logical_not(at.same)
+    pl.when(if_swapped)(lambda: give_vec.wait())
     line.sent_all(0, ghs)
     line.sent(1, ps)
     line.sent(3, ps2)
@@ -1366,17 +1423,22 @@
         gm_copy(d).wait_send()
         out_copy(d).wait_send()
         vec_copy(d).wait_send()
-        for phase, (mine, x_got, part, y_got) in enumerate(((md, xd, sd, yd), (mu, xu, su, yu), (mo, xo, so, yo))):
+        for phase, mine, x_got, part, y_got in ((0, md, xd, sd, yd), (2, mo, xo, so, yo)):
             x_copy(phase, d, mine, x_got).wait_send()
             y_copy(phase, d, part, y_got).wait_send()
+        y_first(1, d, mu, xu).wait_send()
+        x_second(1, d, su, yu).wait_send()
     for j in range(4):
         kv_copy(j).wait_send()
     plane.sent(0, piece_of(mq), slot_of(rp))
     plane.sent(3, piece_of(mkv), slot_of(rpkv))
     plane.sent(1, tile_of, slot_of(vplane))
     plane.sent(2, piece(sendr), piece(arrr))
-    for phase, buf in enumerate((bd, bu, bo, bq)):
-        everyone.sent(phase, buf)
+    everyone.sent(0, bq)
+    for phase, buf in ((7, bd), (8, bu), (9, bo)):
+        fin_mate(phase, buf).wait_send()
+        for d in (1, 3, 2):
+            fin_copy(phase, d, buf).wait_send()
 
     @pl.when(jnp.logical_not(at.same))
     def _():
@@ -1384,7 +1446,7 @@
             swap.wait()
 
 
-def dense_backward_call(gh, after, docs, gains, mixed, route, mid, gate, saved, ps, gin0, gout0):
+def dense_backward_call(gh, after, docs, gains, mixed, route, mid, gate, vec_sum, saved, ps, gin0, gout0):
     bf, f32 = jnp.bfloat16, jnp.float32
     vmem, anywhere = pl.BlockSpec(memory_space=pltpu.VMEM), pl.BlockSpec(memory_space=pl.ANY)
     smem = pl.BlockSpec(memory_space=pltpu.SMEM)
@@ -1394,12 +1456,13 @@
     return pl.pallas_call(
         dense_backward_kernel,
         out_shape=[
-            shape((128, 1024), f32), shape((8, 32, 1024), bf), shape((8, 32, 1024), bf), shape((8, 32, 256), bf),
-            shape((8, 32, 768), bf), shape((8, 128), f32), shape((128, 1024), bf), shape((1024, 512), bf),
+            shape((128, 1024), f32), shape((2, 4, 32, 1024), bf), shape((2, 4, 32, 1024), bf),
+            shape((2, 4, 32, 256), bf), shape((8, 32, 768), bf), shape((8, 128), f32), shape((128, 1024), bf),
+            shape((8, 1024), f32), shape((1024, 512), bf),
             shape((512, 1024), bf),
         ],
-        in_specs=[vmem, vmem, smem] + [vmem] * 5 + [anywhere] * 15,
-        out_specs=[vmem] * 7 + [anywhere] * 2,
+        in_specs=[vmem, vmem, smem] + [vmem] * 6 + [anywhere] * 15,
+        out_specs=[vmem] * 8 + [anywhere] * 2,
         scratch_shapes=[
             *(line * 2), V((512, 1024), f32), *(line * 3), V((512, 1024), f32), *line,
             V((512, 256), bf), V((512, 512), bf), V((512, 512), bf),
@@ -1408,21 +1471,22 @@
             V((128, 1024), bf), V((512, 256), bf), V((512, 768), bf), V((512, 512), f32), V((512, 512), f32),
             V((512, 512), bf), V((512, 512), bf),
             *(wide * 3), *narrow, *(wide * 3), *narrow, *(wide * 3), *narrow,
-            *([V((4, 2, 64, 1024), bf)] * 3), *([V((2, 64, 1024), bf)] * 3), *([V((4, 32, 1024), bf)] * 3),
+            V((4, 2, 64, 1024), bf), V((4, 4, 32, 1024), bf), V((4, 2, 64, 1024), bf),
+            V((2, 64, 1024), bf), V((4, 32, 1024), bf), V((2, 64, 1024), bf), *([V((4, 32, 1024), bf)] * 3),
             V((16, 32, 256), bf), V((16, 32, 512), bf), *(pieces * 2),
             V((8, 1024), f32), V((8, 1024), f32), V((16, 8, 128), f32), V((4, 8, 128), f32),
             V((8, 32, 256), bf),
-            dma((13,)), dma((7, 4)), dma((7, 4)), dma((3, 3)), dma((3, 3)), dma((3, 3)), dma((3, 3)), dma((4,)),
-            dma((4,)), dma((5,)), dma((5,)), dma((4, 15)), dma((4, 15)), dma((4, 7)), dma((4, 7)), dma((2,)),
-            dma((2,)), dma((1,)), dma((1,)),
+            dma((13,)), dma((10, 6)), dma((10, 6)), dma((3, 3)), dma((3, 3)), dma((3, 3)), dma((3, 3)), dma((4,)),
+            dma((4,)), dma((5,)), dma((5,)), dma((4, 15)), dma((4, 15)), dma((1, 7)), dma((1, 7)), dma((3,)),
+            dma((3,)), dma((1,)), dma((1,)), dma((10,)), dma((10,)),
         ],
         compiler_params=pltpu.CompilerParams(collective_id=3, has_side_effects=True, vmem_limit_bytes=62 << 20),
         name="dense_backward",
-    )(gh, after, docs, gains, mixed, route, mid, gate, *saved, ps, gin0, gout0)
+    )(gh, after, docs, gains, mixed, route, mid, gate, vec_sum, *saved, ps, gin0, gout0)
 
 
 def finish_kernel(
-    gvec, vecg, res, gx, bd, bu, bo, bq, in0, in1, out0, out1, swapped_in, swapped_out,
+    gvec, vec_sum, vec_swap, res, gx, bd, bu, bo, bq, in0, in1, out0, out1, swapped_in, swapped_out,
     ng, nb, eg, eb, cen, o_res, o_gx, o_gq, o_go, o_gu, o_gd, o_in, o_out,
     b_in, b_out, f_in, f_out, vd, vu, vo, vq, gq, go, gu, gd, vres, vgx, isem, osem,
 ):
@@ -1453,9 +1517,10 @@
     mine = jnp.where(c == 0, gvec[0:4, 0:64], gvec[0:4, 64:128])
     ng[...] = mine[0:2]
     nb[...] = mine[2:4]
-    eg[...] = vecg[0:2, :]
-    eb[...] = vecg[2:4, :]
-    cen[...] = vecg[4:5, :]
+    vectors = jnp.where(at.same, vec_sum[...], vec_swap[...])
+    eg[...] = vectors[0:2]
+    eb[...] = vectors[2:4]
+    cen[...] = vectors[4:5]
     stores = []
 
     def store(src, dst):
@@ -1475,15 +1540,15 @@
     for half in range(2):
         rows = slice(32 * half, 32 * half + 32)
         for z in range(4):
-            gd[64 * z + 32 * half : 64 * z + 32 * half + 32, :] = vd[2 * z + half].astype(jnp.float32)
-            go[rows, 256 * z : 256 * z + 256] = vo[2 * z + half].astype(jnp.float32)
+            gd[64 * z + 32 * half : 64 * z + 32 * half + 32, :] = vd[half, z].astype(jnp.float32)
+            go[rows, 256 * z : 256 * z + 256] = vo[half, z].astype(jnp.float32)
             for part in range(3):
                 gq[rows, 1024 * part + 256 * z : 1024 * part + 256 * z + 256] = vq[
                     2 * z + half, :, 256 * part : 256 * part + 256
                 ].astype(jnp.float32)
         for n in range(8):
             tile = slice(128 * n, 128 * n + 128)
-            quarter = [vu[2 * z + half, :, tile].astype(jnp.float32) for z in range(4)]
+            quarter = [vu[half, z, :, tile].astype(jnp.float32) for z in range(4)]
             turned = [pltpu.roll(v, 64, 1) for v in quarter]
             first = 512 * n
             gu[rows, first : first + 128] = jnp.where(lane, quarter[0], turned[1])
@@ -1496,7 +1561,7 @@
         copy.wait()
 
 
-def finish_call(gvec, vecg, res, gx, bd, bu, bo, bq, in0, in1, out0, out1, swapped_in, swapped_out):
+def finish_call(gvec, vec_sum, vec_swap, res, gx, bd, bu, bo, bq, in0, in1, out0, out1, swapped_in, swapped_out):
     bf, f32 = jnp.bfloat16, jnp.float32
     vmem, anywhere = pl.BlockSpec(memory_space=pltpu.VMEM), pl.BlockSpec(memory_space=pl.ANY)
     shape, V, dma = jax.ShapeDtypeStruct, pltpu.VMEM, pltpu.SemaphoreType.DMA
@@ -1508,17 +1573,17 @@
             shape((64, 1024), f32), shape((64, 4096), f32), shape((256, 1024), f32), shape((2, 1024, 512), f32),
             shape((2, 512, 1024), f32),
         ],
-        in_specs=[vmem] * 2 + [anywhere] * 12,
+        in_specs=[vmem] * 3 + [anywhere] * 12,
         out_specs=[vmem] * 5 + [anywhere] * 8,
         scratch_shapes=[
             V((2, 1024, 512), bf), V((2, 512, 1024), bf), V((2, 1024, 512), f32), V((2, 512, 1024), f32),
-            V((8, 32, 1024), bf), V((8, 32, 1024), bf), V((8, 32, 256), bf), V((8, 32, 768), bf),
+            V((2, 4, 32, 1024), bf), V((2, 4, 32, 1024), bf), V((2, 4, 32, 256), bf), V((8, 32, 768), bf),
             V((64, 3072), f32), V((64, 1024), f32), V((64, 4096), f32), V((256, 1024), f32),
             V((128, 1024), bf), V((128, 1024), f32), dma((10,)), dma((10,)),
         ],
         compiler_params=pltpu.CompilerParams(vmem_limit_bytes=62 << 20),
         name="finish",
-    )(gvec, vecg, res, gx, bd, bu, bo, bq, in0, in1, out0, out1, swapped_in, swapped_out)
+    )(gvec, vec_sum, vec_swap, res, gx, bd, bu, bo, bq, in0, in1, out0, out1, swapped_in, swapped_out)
 
 
 def on_device(
@@ -1545,15 +1610,16 @@
     hidden, mixed, after, gains, *saved, cz, in0, out0 = dense_forward_call(
         x, norm_gain, norm_bias, doc_starts, slots, cot, w_qkv, w_out, w_up, w_down, exp_in[0], exp_out[0]
     )
-    grad_hidden, vec_grads, mid, gate, part, grad_in1, grad_out1, grad_in0, grad_out0 = expert_call(
+    grad_hidden, vec_sum, mid, gate, part, grad_in1, grad_out1, grad_in0, grad_out0 = expert_call(
         hidden, slots, exp_gain[0], exp_bias[0], centroid, cz, exp_in[0], exp_out[0], in0, out0
     )
-    grad_x, down, up, out, qkv, norm_grads, result, swapped_in, swapped_out = dense_backward_call(
-        grad_hidden, after, doc_starts, gains, mixed, slots, mid, gate, saved, part, grad_in0, grad_out0
+    grad_x, down, up, out, qkv, norm_grads, result, vec_swap, swapped_in, swapped_out = dense_backward_call(
+        grad_hidden, after, doc_starts, gains, mixed, slots, mid, gate, vec_sum, saved, part, grad_in0, grad_out0
     )
     gain, bias, e_gain, e_bias, center, result, grad_x, g_qkv, g_out, g_up, g_down, e_in, e_out = finish_call(
         norm_grads,
-        vec_grads,
+        vec_sum,
+        vec_swap,
         result,
         grad_x,
         down,

time: 282 us -> 288 us (1.021)
  Pallas kernels: 278 us -> 283 us
    pallas_call x1, Pallas kernels: 99.9 us -> 107 us  [dense_backward_call(): pl.pallas_call(dense_backward_kernel, out_shape=[shape((128, 1024), f32),...]
where the time goes in v6:
time: 288 us; the launch traced here: 284 us
  Pallas kernels  283 us (98%)
    pallas_call x1, Pallas kernels, dense_backward_call(): pl.pallas_call(dense_backward_kernel, out_shape=[shape((128, 1024), f32),...  107 us
    pallas_call x1, Pallas kernels, expert_call(): pl.pallas_call(expert_kernel, out_shape=(shape((128, 1024), bf), shape((8...  93.3 us
    pallas_call x1, Pallas kernels, dense_forward_call(): pl.pallas_call(dense_forward_kernel, out_shape=[shape((128, 1024), bf), s...  74.7 us
    pallas_call x1, Pallas kernels, finish_call(): pl.pallas_call(finish_kernel, out_shape=[shape((2, 64), f32), shape((2, 6...  7.72 us

profile of v6, /device:TPU:4, one launch (start us, length us, event | category | flops | bytes accessed | tf_op | source)
XLA Modules:
  0.0 283.8 jit_solution(6189921893099541870)
XLA Ops:
  0.6 74.7 %dense_forward.1 = (bf16[128,1024]{1,0:T(8,128)(2,1)}, bf16[128,1024]{1,0:T(8,128)(2,1)}, f32[128,1024]{1,0:T(8,128)}, f32[8,1024]{1,0:T(8,128)}, bf16[512,1024]...) custom-call(bf16[128,1024]{1,0:T(8,128)(2,1)} %bitcast.17, ...), custom_call_target="tpu_custom_call" | custom-call | tf_op jit(solution)/shard_map/dense_forward/pallas_call | solution.py:629
  75.4 93.3 %experts.1 = (bf16[128,1024]{1,0:T(8,128)(2,1)}, f32[8,1024]{1,0:T(8,128)}, f32[128,1024]{1,0:T(8,128)}, f32[128,128]{1,0:T(8,128)}, bf16[512,1024]{1,0:T(8,128)...) custom-call(bf16[128,1024]{1,0:T(8,128)(2,1)} %get-tuple-element.64., ...), custom_call_target="tpu_custom_call" | custom-call | tf_op jit(solution)/shard_map/experts/pallas_call | solution.py:987
  168.7 107.2 %dense_backward.1 = (f32[128,1024]{1,0:T(8,128)}, bf16[2,4,32,1024]{3,2,1,0:T(8,128)(2,1)}, bf16[2,4,32,1024]{3,2,1,0:T(8,128)(2,1)}, bf16[2,4,32,256]{3,2,1,0:T...) custom-call(bf16[128,1024]{1,0:T(8,128)(2,1)} %get-tuple-element.68., ...), custom_call_target="tpu_custom_call" | custom-call | tf_op jit(solution)/shard_map/dense_backward/pallas_call | solution.py:1456
  275.9 7.7 %finish.1 = (f32[2,64]{1,0:T(2,128)}, f32[2,64]{1,0:T(2,128)}, f32[2,1024]{1,0:T(2,128)}, f32[2,1024]{1,0:T(2,128)}, f32[1,1024]{1,0:T(1,128)}, /*index=5*/bf16[...) custom-call(f32[8,128]{1,0:T(8,128)} %get-tuple-element.90.gvec, ...), custom_call_target="tpu_custom_call" | custom-call | tf_op jit(solution)/shard_map/finish/pallas_call | solution.py:1568

commit v7 on v6

--- a/solution.py
+++ b/solution.py
@@ -1255,8 +1255,12 @@
     core_copy(2, to, ro).start()
     for load in loads[10:]:
         load.wait()
-    for j in range(4):
+
+    def normalise(j, carry):
         xh[block(j), :] = norm_parts(xa[block(j), :].astype(jnp.float32))[0]
+        return carry
+
+    lax.fori_loop(0, 4, normalise, 0)
     join_cores(2, mo, to, ro)
     to_x(2, mo, xo)
     for d in (1, 3, 2):
@@ -1328,9 +1332,8 @@
 
     def plane_total(phase, got):
         plane.wait(phase, slot_of(got))
-        acc = got[0].astype(jnp.float32)
-        for q in range(1, 16):
-            acc += got[q].astype(jnp.float32)
+        acc = jnp.zeros(got.shape[1:], jnp.float32)
+        acc = lax.fori_loop(0, 16, lambda q, total: total + got[q].astype(jnp.float32), acc)
         return acc.astype(jnp.bfloat16)
 
     join_cores(3, mq, tq, rq)
@@ -1364,10 +1367,14 @@
 
     for d in (1, 3, 2):
         out_copy(d).start()
-    for j in range(4):
+
+    def sum_rows(j, carry):
         part = ps2[block(j), :].astype(jnp.float32)
         vmine[0:1, :] += jnp.sum(part * xh[block(j), :], axis=0, keepdims=True)
         vmine[2:3, :] += jnp.sum(part, axis=0, keepdims=True)
+        return carry
+
+    lax.fori_loop(0, 4, sum_rows, 0)
     give_core = remote(vmine, vcore, vs.at[0], vr.at[0], at.other)
     give_core.start()
     fin_y(7, bd)

time: 288 us -> 275 us (0.955)
  Pallas kernels: 283 us -> 272 us
    pallas_call x1, Pallas kernels: 107 us -> 96.8 us  [dense_backward_call(): pl.pallas_call(dense_backward_kernel, out_shape=[shape((128, 1024), f32),...]
where the time goes in v7:
time: 275 us; the launch traced here: 273 us
  Pallas kernels  272 us (99%)
    pallas_call x1, Pallas kernels, dense_backward_call(): pl.pallas_call(dense_backward_kernel, out_shape=[shape((128, 1024), f32),...  96.8 us
    pallas_call x1, Pallas kernels, expert_call(): pl.pallas_call(expert_kernel, out_shape=(shape((128, 1024), bf), shape((8...  93.1 us
    pallas_call x1, Pallas kernels, dense_forward_call(): pl.pallas_call(dense_forward_kernel, out_shape=[shape((128, 1024), bf), s...  74.7 us
    pallas_call x1, Pallas kernels, finish_call(): pl.pallas_call(finish_kernel, out_shape=[shape((2, 64), f32), shape((2, 6...  7.72 us

profile of v7, /device:TPU:4, one launch (start us, length us, event | category | flops | bytes accessed | tf_op | source)
XLA Modules:
  0.0 273.2 jit_solution(7355505650738966771)
XLA Ops:
  0.6 74.7 %dense_forward.1 = (bf16[128,1024]{1,0:T(8,128)(2,1)}, bf16[128,1024]{1,0:T(8,128)(2,1)}, f32[128,1024]{1,0:T(8,128)}, f32[8,1024]{1,0:T(8,128)}, bf16[512,1024]...) custom-call(bf16[128,1024]{1,0:T(8,128)(2,1)} %bitcast.17, ...), custom_call_target="tpu_custom_call" | custom-call | tf_op jit(solution)/shard_map/dense_forward/pallas_call | solution.py:629
  75.4 93.1 %experts.1 = (bf16[128,1024]{1,0:T(8,128)(2,1)}, f32[8,1024]{1,0:T(8,128)}, f32[128,1024]{1,0:T(8,128)}, f32[128,128]{1,0:T(8,128)}, bf16[512,1024]{1,0:T(8,128)...) custom-call(bf16[128,1024]{1,0:T(8,128)(2,1)} %get-tuple-element.64., ...), custom_call_target="tpu_custom_call" | custom-call | tf_op jit(solution)/shard_map/experts/pallas_call | solution.py:987
  168.5 96.8 %dense_backward.1 = (f32[128,1024]{1,0:T(8,128)}, bf16[2,4,32,1024]{3,2,1,0:T(8,128)(2,1)}, bf16[2,4,32,1024]{3,2,1,0:T(8,128)(2,1)}, bf16[2,4,32,256]{3,2,1,0:T...) custom-call(bf16[128,1024]{1,0:T(8,128)(2,1)} %get-tuple-element.68., ...), custom_call_target="tpu_custom_call" | custom-call | tf_op jit(solution)/shard_map/dense_backward/pallas_call | solution.py:1463
  265.3 7.7 %finish.1 = (f32[2,64]{1,0:T(2,128)}, f32[2,64]{1,0:T(2,128)}, f32[2,1024]{1,0:T(2,128)}, f32[2,1024]{1,0:T(2,128)}, f32[1,1024]{1,0:T(1,128)}, /*index=5*/bf16[...) custom-call(f32[8,128]{1,0:T(8,128)} %get-tuple-element.90.gvec, ...), custom_call_target="tpu_custom_call" | custom-call | tf_op jit(solution)/shard_map/finish/pallas_call | solution.py:1575
